TPU v7x, 32 devices: a whole 2x2x4 slice. The times are simulated.
32 devices in a mesh: dp: 8 (over y, x, core), outer: 4 (over z).
Axes of the slice: x: 2, y: 2, z: 4, core: 2. Of those that a mesh axis runs over, the one named last changes fastest.
Arguments:
- questions: bfloat16 [256, 64, 256], P(('dp', 'outer')), may hold values from -6 to 6
- passages: bfloat16 [256, 256, 256], P(('dp', 'outer')), may hold values from -6 to 6
- q_lengths: int32 [256], P(('dp', 'outer')), may hold values from 16 to 64, as said below
- p_lengths: int32 [256], P(('dp', 'outer')), may hold values from 64 to 256, as said below
- positives: int32 [256, 4], P(('dp', 'outer')), may hold values from 0 to 255
- pos_counts: int32 [256], P(('dp', 'outer')), may hold values from 1 to 4
- attn: float32 [2, 4, 256, 256], replicated, may hold values from -0.375 to 0.375
- w_in: float32 [2, 256, 1024], replicated, may hold values from -0.375 to 0.375
- w_out: float32 [2, 1024, 256], replicated, may hold values from -0.1875 to 0.1875
- gains: float32 [2, 2, 256], replicated, may hold values from 0.5 to 1.5
- biases: float32 [2, 2560], replicated, may hold values from -0.3 to 0.3
- attn_mom: float32 [2, 4, 256, 256], replicated, may hold values from -0.00956832 to 0.00956832
- w_in_mom: float32 [2, 256, 1024], replicated, may hold values from -0.00956832 to 0.00956832
- w_out_mom: float32 [2, 1024, 256], replicated, may hold values from -0.00956832 to 0.00956832
- gain_mom: float32 [2, 2, 256], replicated, may hold values from -0.15309311 to 0.15309311
- bias_mom: float32 [2, 2560], replicated, may hold values from -0.03827328 to 0.03827328
- attn_err: float32 [32, 2, 4, 256, 256], P(('dp', 'outer')), may hold values from -0.12 to 0.12
- w_in_err: float32 [32, 2, 256, 1024], P(('dp', 'outer')), may hold values from -0.12 to 0.12
- w_out_err: float32 [32, 2, 1024, 256], P(('dp', 'outer')), may hold values from -0.12 to 0.12
- attn_start: float32 [2, 4, 256, 8], replicated, may hold values from -6 to 6
- w_in_start: float32 [2, 1024, 8], replicated, may hold values from -6 to 6
- w_out_start: float32 [2, 256, 8], replicated, may hold values from -6 to 6
Outputs:
- question_loss: float32 [256], P(('dp', 'outer'))
- question_grad: float32 [256, 64, 256], P(('dp', 'outer'))
- passage_grad: float32 [256, 256, 256], P(('dp', 'outer'))
- attn_new: float32 [2, 4, 256, 256], replicated
- w_in_new: float32 [2, 256, 1024], replicated
- w_out_new: float32 [2, 1024, 256], replicated
- gains_new: float32 [2, 2, 256], replicated
- biases_new: float32 [2, 2560], replicated
- attn_mom_new: float32 [2, 4, 256, 256], replicated
- w_in_mom_new: float32 [2, 256, 1024], replicated
- w_out_mom_new: float32 [2, 1024, 256], replicated
- gain_mom_new: float32 [2, 2, 256], replicated
- bias_mom_new: float32 [2, 2560], replicated
- attn_err_new: float32 [32, 2, 4, 256, 256], P(('dp', 'outer'))
- w_in_err_new: float32 [32, 2, 256, 1024], P(('dp', 'outer'))
- w_out_err_new: float32 [32, 2, 1024, 256], P(('dp', 'outer'))
- attn_factor: float32 [2, 4, 256, 8], replicated
- w_in_factor: float32 [2, 1024, 8], replicated
- w_out_factor: float32 [2, 256, 8], replicated
- grad_norm: float32 [], replicated
Inputs may be any that keep to these rules, and one draw needn't show every extreme that they name: `q_lengths`: at least one question has 64 tokens. `p_lengths`: at least one passage has 256 tokens. `positives`: entries past a row's pos_counts are ignored; a list may name a passage twice.
All inputs are finite; a program needn't handle non-finite values.
Results may differ from a plain program's by a relative error of at most 0.015.
The roundings to bfloat16 on the way count: a program that leaves them out, or rounds other values in their place, can miss the bound.
Values may be sent and summed in bfloat16 or wider, within the bound.
No kernel may reach another device: no remote copies, remote signals or barrier semaphores. Data moves between devices by JAX's collectives and lax.ppermute only.
A program may use at most 192 MiB of HBM per device.

v0:
```python
import math

import jax
import jax.numpy as jnp
from jax import lax
from jax.sharding import PartitionSpec as P

HEAD = 64


NORM_EPSILON = 1e-06
UNIT_EPSILON = 1e-06
SCORE_SCALE = 20.0
MOMENTUM_DECAY = 0.9
LEARNING_RATE = 10.0
CLIP_NORM = 2.0
MASKED_SCORE = -1e30
HIGHEST = lax.Precision.HIGHEST


def project(values, weight):
    return jnp.einsum("bld,de->ble", values, weight, preferred_element_type=jnp.float32)


def project_back(gradient, weight):
    return jnp.einsum("ble,de->bld", gradient, weight, preferred_element_type=jnp.float32)


def weight_grad(values, gradient):
    return jnp.einsum("bld,ble->de", values, gradient, preferred_element_type=jnp.float32)


def row_total(gradient):
    return jnp.sum(gradient, axis=(0, 1), dtype=jnp.float32)


def split_shifts(shifts, features):
    return [shifts[features * offset : features * (offset + 1)] for offset in range(6)] + [
        shifts[6 * features :]
    ]


def norm_forward(hidden, gain, shift):
    center = hidden - jnp.mean(hidden, axis=-1, keepdims=True)
    inverse = lax.rsqrt(jnp.mean(center * center, axis=-1, keepdims=True) + NORM_EPSILON)
    normed = center * inverse
    return (normed * gain + shift, normed, inverse)


def norm_backward(grad_out, normed, inverse, gain):
    scaled = grad_out * gain
    inner_term = (
        scaled
        - jnp.mean(scaled, axis=-1, keepdims=True)
        - normed * jnp.mean(scaled * normed, axis=-1, keepdims=True)
    )
    return (
        inner_term * inverse,
        jnp.sum(grad_out * normed, axis=(0, 1)),
        jnp.sum(grad_out, axis=(0, 1)),
    )


def gelu_slope(upper_in):
    return (
        0.5 * (1.0 + lax.erf(upper_in * 0.5**0.5))
        + upper_in * jnp.exp(-0.5 * upper_in * upper_in) * (0.5 / math.pi) ** 0.5
    )


def attention_scores(query_heads, key_heads, valid_keys):
    scores = jnp.einsum(
        "bqhe,bkhe->bhqk", query_heads, key_heads, preferred_element_type=jnp.float32
    ) * HEAD ** (-0.5)
    return jnp.where(valid_keys[:, None, None, :], scores, MASKED_SCORE)


def encoder_forward(inputs, lengths, attn_low, inner_low, outer_low, gain_pair, shifts):
    seq_count, length, features = inputs.shape
    head_shape = (seq_count, length, features // HEAD, HEAD)
    query_shift, value_shift, output_shift, first_shift, down_shift, second_shift, up_shift = (
        split_shifts(shifts, features)
    )
    query_heads = (
        (project(inputs, attn_low[0]) + query_shift).astype(jnp.bfloat16).reshape(head_shape)
    )
    key_heads = project(inputs, attn_low[1]).astype(jnp.bfloat16).reshape(head_shape)
    value_heads = (
        (project(inputs, attn_low[2]) + value_shift).astype(jnp.bfloat16).reshape(head_shape)
    )
    valid_keys = lax.broadcasted_iota(jnp.int32, (seq_count, length), 1) < lengths[:, None]
    scores = attention_scores(query_heads, key_heads, valid_keys)
    highest = jnp.max(scores, axis=-1, keepdims=True)
    exponent = jnp.exp(scores - highest)
    totals = jnp.sum(exponent, axis=-1, keepdims=True)
    attention = exponent / totals
    log_total = highest + jnp.log(totals)
    context_low = (
        jnp.einsum(
            "bhqk,bkhe->bqhe",
            attention.astype(jnp.bfloat16),
            value_heads,
            preferred_element_type=jnp.float32,
        )
        .astype(jnp.bfloat16)
        .reshape(seq_count, length, features)
    )
    branch = project(context_low, attn_low[3]) + output_shift
    first, normed_one, inverse_one = norm_forward(
        inputs.astype(jnp.float32) + branch, gain_pair[0], first_shift
    )
    first_low = first.astype(jnp.bfloat16)
    upper_in = project(first_low, inner_low) + up_shift
    active_low = jax.nn.gelu(upper_in, approximate=False).astype(jnp.bfloat16)
    second, normed_two, inverse_two = norm_forward(
        first + project(active_low, outer_low) + down_shift, gain_pair[1], second_shift
    )
    position_share = valid_keys.astype(jnp.float32) / lengths[:, None].astype(jnp.float32)
    pooled = jnp.sum(second * position_share[:, :, None], axis=1)
    inverse_unit = lax.rsqrt(jnp.sum(pooled * pooled, axis=-1, keepdims=True) + UNIT_EPSILON)
    unit_low = (pooled * inverse_unit).astype(jnp.bfloat16)
    saved = (
        query_heads,
        key_heads,
        value_heads,
        valid_keys,
        log_total,
        context_low,
        normed_one,
        inverse_one,
        first_low,
        upper_in,
        active_low,
        normed_two,
        inverse_two,
        position_share,
        pooled,
        inverse_unit,
    )
    return (unit_low, saved)


def encoder_backward(grad_unit, saved, inputs, attn_low, inner_low, outer_low, gain_pair):
    (
        query_heads,
        key_heads,
        value_heads,
        valid_keys,
        log_total,
        context_low,
        normed_one,
        inverse_one,
        first_low,
        upper_in,
        active_low,
        normed_two,
        inverse_two,
        position_share,
        pooled,
        inverse_unit,
    ) = saved
    seq_count, length, features = inputs.shape
    head_shape = (seq_count, length, features // HEAD, HEAD)
    pooled_dot = jnp.sum(pooled * grad_unit, axis=-1, keepdims=True)
    grad_pooled = inverse_unit * grad_unit - inverse_unit**3 * pooled * pooled_dot
    grad_second = position_share[:, :, None] * grad_pooled[:, None, :]
    grad_two, gain_two, shift_two = norm_backward(
        grad_second, normed_two, inverse_two, gain_pair[1]
    )
    down_low = grad_two.astype(jnp.bfloat16)
    outer_grad = jnp.einsum("blf,bld->fd", active_low, down_low, preferred_element_type=jnp.float32)
    grad_active = jnp.einsum("bld,fd->blf", down_low, outer_low, preferred_element_type=jnp.float32)
    up_low = (grad_active * gelu_slope(upper_in)).astype(jnp.bfloat16)
    inner_grad = jnp.einsum("bld,blf->df", first_low, up_low, preferred_element_type=jnp.float32)
    grad_first = grad_two + jnp.einsum(
        "blf,df->bld", up_low, inner_low, preferred_element_type=jnp.float32
    )
    grad_one, gain_one, shift_one = norm_backward(grad_first, normed_one, inverse_one, gain_pair[0])
    branch_low = grad_one.astype(jnp.bfloat16)
    output_grad = weight_grad(context_low, branch_low)
    grad_context = project_back(branch_low, attn_low[3]).astype(jnp.bfloat16).reshape(head_shape)
    grad_attention = jnp.einsum(
        "bqhe,bkhe->bhqk", grad_context, value_heads, preferred_element_type=jnp.float32
    )
    attention = jnp.exp(attention_scores(query_heads, key_heads, valid_keys) - log_total)
    value_grad = (
        jnp.einsum(
            "bhqk,bqhe->bkhe",
            attention.astype(jnp.bfloat16),
            grad_context,
            preferred_element_type=jnp.float32,
        )
        .astype(jnp.bfloat16)
        .reshape(seq_count, length, features)
    )
    grad_scores = attention * (
        grad_attention - jnp.sum(grad_attention * attention, axis=-1, keepdims=True)
    )
    grad_raw = (grad_scores * HEAD ** (-0.5)).astype(jnp.bfloat16)
    query_grad = (
        jnp.einsum("bhqk,bkhe->bqhe", grad_raw, key_heads, preferred_element_type=jnp.float32)
        .astype(jnp.bfloat16)
        .reshape(seq_count, length, features)
    )
    key_grad = (
        jnp.einsum("bhqk,bqhe->bkhe", grad_raw, query_heads, preferred_element_type=jnp.float32)
        .astype(jnp.bfloat16)
        .reshape(seq_count, length, features)
    )
    input_grad = (
        grad_one
        + project_back(query_grad, attn_low[0])
        + project_back(key_grad, attn_low[1])
        + project_back(value_grad, attn_low[2])
    )
    attn_grad = jnp.stack(
        [
            weight_grad(inputs, query_grad),
            weight_grad(inputs, key_grad),
            weight_grad(inputs, value_grad),
            output_grad,
        ]
    )
    shift_grad = jnp.concatenate(
        [
            row_total(query_grad),
            row_total(value_grad),
            row_total(branch_low),
            shift_one,
            row_total(down_low),
            shift_two,
            row_total(up_low),
        ]
    )
    gain_grad = jnp.stack([gain_one, gain_two])
    return (input_grad, attn_grad, inner_grad, outer_grad, gain_grad, shift_grad)


def contrast(scores, positive_lists, counts, passage_count):
    slot_live = lax.broadcasted_iota(jnp.int32, positive_lists.shape, 1) < counts[:, None]
    columns = lax.broadcasted_iota(jnp.int32, (1, 1, passage_count), 2)
    is_positive = jnp.any((positive_lists[:, :, None] == columns) & slot_live[:, :, None], axis=1)
    highest = jnp.max(scores, axis=1, keepdims=True)
    whole_lse = highest + jnp.log(jnp.sum(jnp.exp(scores - highest), axis=1, keepdims=True))
    chosen = jnp.where(is_positive, scores, MASKED_SCORE)
    chosen_top = jnp.max(chosen, axis=1, keepdims=True)
    within = chosen_top + jnp.log(jnp.sum(jnp.exp(chosen - chosen_top), axis=1, keepdims=True))
    gradient = jnp.exp(scores - whole_lse) - jnp.exp(chosen - within)
    return ((whole_lse - within)[:, 0], gradient)


def orthonormal_rows(factor):
    rows_done = []
    for row_index in range(factor.shape[-2]):
        column = factor[..., row_index, :]
        for earlier in rows_done:
            column = column - jnp.sum(earlier * column, axis=-1, keepdims=True) * earlier
        column = column * lax.rsqrt(jnp.sum(column * column, axis=-1, keepdims=True) + 1e-06)
        rows_done.append(column)
    return jnp.stack(rows_done, axis=-2)


def momentum_step(weight, moment, gradient, clip_factor):
    moment_new = MOMENTUM_DECAY * moment + clip_factor * gradient
    return (weight - LEARNING_RATE * moment_new, moment_new)


def per_device(
    questions,
    passages,
    q_lengths,
    p_lengths,
    positives,
    pos_counts,
    attn,
    w_in,
    w_out,
    gains,
    biases,
    attn_mom,
    w_in_mom,
    w_out_mom,
    gain_mom,
    bias_mom,
    attn_err,
    w_in_err,
    w_out_err,
    attn_start,
    w_in_start,
    w_out_start,
):
    attn_low = attn.astype(jnp.bfloat16)
    inner_low = w_in.astype(jnp.bfloat16)
    outer_low = w_out.astype(jnp.bfloat16)
    question_unit, question_saved = encoder_forward(
        questions, q_lengths, attn_low[0], inner_low[0], outer_low[0], gains[0], biases[0]
    )
    passage_unit, passage_saved = encoder_forward(
        passages, p_lengths, attn_low[1], inner_low[1], outer_low[1], gains[1], biases[1]
    )
    passage_all = lax.all_gather(passage_unit, ("dp", "outer"), axis=0, tiled=True)
    passage_count = passage_all.shape[0]
    contract_rows = (((0,), (0,)), ((), ()))
    contract_cols = (((1,), (1,)), ((), ()))
    scores = SCORE_SCALE * lax.dot_general(
        question_unit, passage_all, contract_cols, preferred_element_type=jnp.float32
    )
    question_loss, grad_scores = contrast(scores, positives, pos_counts, passage_count)
    grad_low = (SCORE_SCALE * grad_scores).astype(jnp.bfloat16)
    grad_question_unit = jnp.dot(grad_low, passage_all, preferred_element_type=jnp.float32)
    partial_terms = lax.dot_general(
        grad_low, question_unit, contract_rows, preferred_element_type=jnp.float32
    )
    grad_passage_unit = lax.psum_scatter(
        partial_terms, ("dp", "outer"), scatter_dimension=0, tiled=True
    )
    question_back = encoder_backward(
        grad_question_unit,
        question_saved,
        questions,
        attn_low[0],
        inner_low[0],
        outer_low[0],
        gains[0],
    )
    passage_back = encoder_backward(
        grad_passage_unit,
        passage_saved,
        passages,
        attn_low[1],
        inner_low[1],
        outer_low[1],
        gains[1],
    )
    question_grad = question_back[0]
    passage_grad = passage_back[0]
    attn_grad = jnp.stack([question_back[1], passage_back[1]])
    inner_grad = jnp.stack([question_back[2], passage_back[2]])
    outer_grad = jnp.stack([question_back[3], passage_back[3]])
    gain_grad = jnp.stack([question_back[4], passage_back[4]])
    shift_grad = jnp.stack([question_back[5], passage_back[5]])
    replicas = lax.axis_size("dp") * lax.axis_size("outer")
    merged_attn = attn_grad + attn_err[0]
    merged_inner = inner_grad + w_in_err[0]
    merged_outer = outer_grad + w_out_err[0]
    left_attn = jnp.einsum("tkmn,tknj->tkjm", merged_attn, attn_start, precision=HIGHEST)
    left_inner = jnp.einsum("tmn,tnj->tjm", merged_inner, w_in_start, precision=HIGHEST)
    left_outer = jnp.einsum("tmn,tnj->tjm", merged_outer, w_out_start, precision=HIGHEST)
    left_attn, left_inner, left_outer, gain_sum, shift_sum = lax.psum(
        (left_attn, left_inner, left_outer, gain_grad, shift_grad), ("dp", "outer")
    )
    basis_attn = orthonormal_rows(left_attn)
    basis_inner = orthonormal_rows(left_inner)
    basis_outer = orthonormal_rows(left_outer)
    right_attn = jnp.einsum("tkmn,tkjm->tkjn", merged_attn, basis_attn, precision=HIGHEST)
    right_inner = jnp.einsum("tmn,tjm->tjn", merged_inner, basis_inner, precision=HIGHEST)
    right_outer = jnp.einsum("tmn,tjm->tjn", merged_outer, basis_outer, precision=HIGHEST)
    right_attn, right_inner, right_outer = lax.psum(
        (right_attn, right_inner, right_outer), ("dp", "outer")
    )
    approx_attn = jnp.einsum("tkjm,tkjn->tkmn", basis_attn, right_attn, precision=HIGHEST)
    approx_inner = jnp.einsum("tjm,tjn->tmn", basis_inner, right_inner, precision=HIGHEST)
    approx_outer = jnp.einsum("tjm,tjn->tmn", basis_outer, right_outer, precision=HIGHEST)
    attn_err_new = (merged_attn - approx_attn / replicas)[None]
    w_in_err_new = (merged_inner - approx_inner / replicas)[None]
    w_out_err_new = (merged_outer - approx_outer / replicas)[None]
    norm_square = (
        jnp.sum(approx_attn * approx_attn)
        + jnp.sum(approx_inner * approx_inner)
        + jnp.sum(approx_outer * approx_outer)
        + jnp.sum(gain_sum * gain_sum)
        + jnp.sum(shift_sum * shift_sum)
    )
    grad_norm = jnp.sqrt(norm_square)
    clip_factor = jnp.minimum(1.0, CLIP_NORM / grad_norm)
    attn_new, attn_mom_new = momentum_step(attn, attn_mom, approx_attn, clip_factor)
    w_in_new, w_in_mom_new = momentum_step(w_in, w_in_mom, approx_inner, clip_factor)
    w_out_new, w_out_mom_new = momentum_step(w_out, w_out_mom, approx_outer, clip_factor)
    gains_new, gain_mom_new = momentum_step(gains, gain_mom, gain_sum, clip_factor)
    biases_new, bias_mom_new = momentum_step(biases, bias_mom, shift_sum, clip_factor)
    attn_factor = jnp.swapaxes(right_attn, -1, -2)
    w_in_factor = jnp.swapaxes(right_inner, -1, -2)
    w_out_factor = jnp.swapaxes(right_outer, -1, -2)
    return (
        question_loss,
        question_grad,
        passage_grad,
        attn_new,
        w_in_new,
        w_out_new,
        gains_new,
        biases_new,
        attn_mom_new,
        w_in_mom_new,
        w_out_mom_new,
        gain_mom_new,
        bias_mom_new,
        attn_err_new,
        w_in_err_new,
        w_out_err_new,
        attn_factor,
        w_in_factor,
        w_out_factor,
        grad_norm,
    )


def solution(mesh):
    return jax.shard_map(
        per_device,
        mesh=mesh,
        in_specs=(
            P(("dp", "outer"), None, None),
            P(("dp", "outer"), None, None),
            P(("dp", "outer")),
            P(("dp", "outer")),
            P(("dp", "outer"), None),
            P(("dp", "outer")),
            P(),
            P(),
            P(),
            P(),
            P(),
            P(),
            P(),
            P(),
            P(),
            P(),
            P(("dp", "outer"), None, None, None, None),
            P(("dp", "outer"), None, None, None),
            P(("dp", "outer"), None, None, None),
            P(),
            P(),
            P(),
        ),
        out_specs=(
            P(("dp", "outer")),
            P(("dp", "outer"), None, None),
            P(("dp", "outer"), None, None),
            P(),
            P(),
            P(),
            P(),
            P(),
            P(),
            P(),
            P(),
            P(),
            P(),
            P(("dp", "outer"), None, None, None, None),
            P(("dp", "outer"), None, None, None),
            P(("dp", "outer"), None, None, None),
            P(),
            P(),
            P(),
            P(),
        ),
        check_vma=False,
    )
```

profile of v0, /device:TPU:0, one launch (start us, length us, event | category | flops | bytes accessed | tf_op | source)
XLA Modules:
  0.0 741.7 jit_solution(7868493692935574734)
XLA Ops:
  34.5 4.8 fusion.57
  41.4 2.2 fusion.19
  43.6 2.1 fusion.18
  46.8 2.8 fusion.77
  52.0 3.7 fusion.75
  55.7 19.0 %fusion.4 = bf16[8,256,1024]{2,1,0:T(8,128)(2,1)S(1)} fusion(f32[8,256,1024]{2,1,0:T(8,128)S(1)} %get-tuple-element.370, f32[1024]{0:T(1024)S(1)} %bitcast.791, u8[256,1024]{1,0:T(8,128)(4,1)S(1)} %get-tuple-element.101, u8[256,1024]{1,0:T(8,128)(4,1)S(1)} %get-tuple-element.100), kind=kLoop, calls=%fused_computation.6 | loop fusion | flops 148897792 | bytes 13111296 | tf_op jit(solution)/shard_map/convert_element_type | solution.py:114
  78.7 70.7 %all_gather.3 = bf16[256,256]{1,0:T(8,128)(2,1)S(1)} all-gather(bf16[8,256]{1,0:T(8,128)(2,1)S(1)} %multiply_convert_fusion.2), channel_id=1, replica_groups=mesh['dp'=8,'outer'=4] {'dp','outer'}, dimensions={0}, use_global_device_ids=true | all-gather | bytes 135168 | tf_op jit(solution)/shard_map/all_gather | solution.py:301
  154.8 3.5 convert_reduce_fusion.5
  166.0 2.4 fusion.129
  169.1 3.9 convolution_convert_fusion.3
  172.9 4.4 convert_reduce_fusion.7
  177.3 3.0 convert_reduce_fusion.6
  186.3 2.2 reshape.1828
  190.4 2.4 fusion.95
  193.9 2.1 convolution_add_fusion.3
  200.5 2.2 maximum_bitcast_fusion
  203.3 1.9 copy.428
  206.1 3.0 convolution_bitcast_fusion.3
  209.1 72.5 %reduce-scatter.2.cloned.1.call-done = f32[8,256]{1,0:T(8,128)} async-done(((f32[256,256]{1,0:T(8,128)}), f32[8,256]{1,0:T(8,128)}) %reduce-scatter.2.cloned.1.call-update) | async-done | bytes 8208 | tf_op jit(solution)/shard_map/reduce_scatter | solution.py:314
  283.4 2.6 fusion.67
  287.2 7.6 %convert_reduce_fusion = (f32[1024]{0:T(1024)}, bf16[8,256,1024]{2,1,0:T(8,128)(2,1)S(1)}) fusion(f32[8,256,1024]{2,1,0:T(8,128)} %copy-done.28, f32[1024]{0:T(1024)S(1)} %bitcast.792, bf16[8,256,256]{1,2,0:T(8,128)(2,1)S(1)} %get-tuple-element.268, bf16[2,1024,256]{2,1,0:T(8,128)(2,1)S(1)} %copy-done.69), kind=kOutput, calls=%fused_computation.18 | convolution fusion | flops 1101003776 | bytes 14163968 | tf_op jit(solution)/shard_map/bld,fd->blf/dot_general | solution.py:172
  294.9 2.3 convolution_bitcast_fusion
  297.2 3.1 multiply_reduce_fusion.2
  300.3 2.4 convolution_bitcast_fusion.2
  307.0 4.5 fusion.252
  311.5 3.3 convert_reduce_fusion.3
  314.8 16.6 %fusion.84 = bf16[8,4,64,256]{3,2,1,0:T(8,128)(2,1)} fusion(bf16[8,256,4,64]{1,3,2,0:T(8,128)(2,1)} %bitcast.749, f32[8,4,256,256]{2,3,1,0:T(8,128)} %fusion.252, f32[8,4,256,256]{2,3,1,0:T(8,128)} %copy-done.2, f32[8,4,256]{2,1,0:T(4,128)S(1)} %bitcast.779, pred[8,256]{1,0:T(8,128)(4,1)S(1)} %copy-done.101), kind=kOutput, calls=%fused_computation.139 | convolution fusion | flops 292036864 | bytes 18909184 | tf_op jit(solution)/shard_map/bhqk,bqhe->bkhe/dot_general | solution.py:206
  331.3 17.1 %convert_reduce_fusion.4 = (f32[4,64]{1,0:T(4,128)S(1)}, bf16[8,4,64,256]{3,2,1,0:T(8,128)(2,1)}) fusion(bf16[8,256,4,64]{1,3,2,0:T(8,128)(2,1)} %bitcast.746, f32[8,4,256,256]{2,3,1,0:T(8,128)} %fusion.252, f32[8,4,256,256]{2,3,1,0:T(8,128)} %copy-done.2, f32[8,4,256]{2,1,0:T(4,128)S(1)} %bitcast.780, pred[8,256]{1,0:T(8,128)(4,1)S(1)} %copy-done.101), kind=kOutput, calls=%fused_computation.99 | convolution fusion | flops 293085184 | bytes 18910208 | tf_op jit(solution)/shard_map/bhqk,bkhe->bqhe/dot_general | solution.py:201
  350.2 2.8 fusion.138
  354.1 2.8 fusion.137
  357.0 1.9 fusion.234
  361.8 2.4 convolution_bitcast_fusion.9
  368.4 3.6 add_add_fusion
  372.0 2.9 copy.467
  375.1 119.2 %all-reduce.8.cloned.1.call-done = (f32[2,4,8,256]{3,1,0,2:T(4,128)}, f32[2,8,1024]{2,0,1:T(2,128)}) async-done(((f32[2,4,8,256]{3,1,0,2:T(4,128)}, f32[2,8,1024]{2,0,1:T(2,128)}), (f32[2,4,8,256]{3,1,0,2:T(4,128)}, f32[2,8,1024]{2,0,1:T(2,128)})) %all-reduce.8.cloned.1.call-update) | async-done | bytes 131088 | tf_op jit(solution)/shard_map/psum | solution.py:349
  509.5 3.4 fusion.139
  512.9 40.3 %all-reduce = (f32[2,8,256]{2,0,1:T(2,128)S(1)}, f32[2,8,256]{2,1,0:T(8,128)S(1)}, f32[2,2,256]{2,1,0:T(2,128)S(1)}, f32[2,2560]{1,0:T(2,128)S(1)}) all-reduce(f32[2,8,256]{2,0,1:T(2,128)S(1)} %bitcast.777, f32[2,8,256]{2,1,0:T(8,128)S(1)} %fusion.139, ...), channel_id=1, replica_groups=mesh['dp'=8,'outer'=4] {'dp','outer'}, use_global_device_ids=true, to_apply=%region_73.74 | all-reduce | flops 14336 | bytes 114688 | tf_op jit(solution)/shard_map/psum | solution.py:349
  556.8 3.8 fusion.143
  566.4 3.9 multiply_reduce_fusion.3
  570.9 122.2 %all-reduce.6.cloned.1.call-done = (f32[2,4,8,256]{3,2,1,0:T(8,128)}, f32[2,8,1024]{2,1,0:T(8,128)}) async-done(((f32[2,4,8,256]{3,2,1,0:T(8,128)}, f32[2,8,1024]{2,1,0:T(8,128)}), (f32[2,4,8,256]{3,2,1,0:T(8,128)}, f32[2,8,1024]{2,1,0:T(8,128)})) %all-reduce.6.cloned.1.call-update) | async-done | bytes 131088 | tf_op jit(solution)/shard_map/psum | solution.py:358
  693.2 4.7 multiply_reduce_fusion.5
  697.9 3.8 multiply_reduce_fusion.4
  706.2 2.9 copy.466
  709.1 3.6 subtract_bitcast_fusion.2
  712.7 3.1 copy.468
  715.8 5.6 multiply_subtract_fusion.2
  723.2 3.9 multiply_subtract_fusion.1
  729.5 3.1 multiply_subtract_fusion
  (531 shorter events, 113.3 us)
Async XLA Ops:
  7.2 358.5 %copy-start = (f32[2,4,256,8]{2,3,1,0:T(8,128)S(1)}, f32[2,4,256,8]{2,3,1,0:T(8,128)}, u32[]{:S(2)}) copy-start(f32[2,4,256,8]{2,3,1,0:T(8,128)} %param.41) | copy-start | bytes 196612
  7.2 11.6 %copy-start.1 = (bf16[8,256,256]{2,1,0:T(8,128)(2,1)S(1)}, bf16[8,256,256]{2,1,0:T(8,128)(2,1)}, u32[]{:S(2)}) copy-start(bf16[8,256,256]{2,1,0:T(8,128)(2,1)} %param.23) | copy-start | bytes 3145732
  7.2 274.4 %reduce-scatter.2.cloned.1.call-start = ((), (), s32[]{:S(2)}) async-start(), calls=%async_computation.1 | async-start | bytes 270336 | tf_op jit(solution)/shard_map/reduce_scatter | solution.py:314
  13.1 21.4 %copy-start.111 = (f32[1,1024]{1,0:T(1,128)}, f32[1,1024]{1,0:T(1,128)S(1)}, u32[]{:S(2)}) copy-start(f32[1,1024]{1,0:T(1,128)S(1)} %get-tuple-element.356) | copy-start | bytes 12292
  18.8 13.7 %copy-start.16 = (bf16[2,4,256,256]{3,2,1,0:T(8,128)(2,1)}, bf16[2,4,256,256]{3,2,1,0:T(8,128)(2,1)S(1)}, u32[]{:S(2)}) copy-start(bf16[2,4,256,256]{3,2,1,0:T(8,128)(2,1)S(1)} %convert_element_type.201) | copy-start | bytes 3145732
  25.9 15.5 %copy-start.42 = (bf16[8,256,256]{1,2,0:T(8,128)(2,1)}, bf16[8,256,256]{1,2,0:T(8,128)(2,1)S(1)}, u32[]{:S(2)}) copy-start(bf16[8,256,256]{1,2,0:T(8,128)(2,1)S(1)} %add_convert_fusion) | copy-start | bytes 3145732
  27.3 18.5 %copy-start.43 = (bf16[8,256,256]{1,2,0:T(8,128)(2,1)}, bf16[8,256,256]{1,2,0:T(8,128)(2,1)S(1)}, u32[]{:S(2)}) copy-start(bf16[8,256,256]{1,2,0:T(8,128)(2,1)S(1)} %add_convert_fusion.1) | copy-start | bytes 3145732
  29.3 22.3 %copy-start.64 = (bf16[2,256,1024]{2,1,0:T(8,128)(2,1)}, bf16[2,256,1024]{2,1,0:T(8,128)(2,1)S(1)}, u32[]{:S(2)}) copy-start(bf16[2,256,1024]{2,1,0:T(8,128)(2,1)S(1)} %convert_element_type.209) | copy-start | bytes 3145732
  29.4 45.4 %copy-start.67 = (bf16[2,1024,256]{2,1,0:T(8,128)(2,1)}, bf16[2,1024,256]{2,1,0:T(8,128)(2,1)S(1)}, u32[]{:S(2)}) copy-start(bf16[2,1024,256]{2,1,0:T(8,128)(2,1)S(1)} %convert_element_type.211) | copy-start | bytes 3145732
  33.0 6.4 copy-start.35
  41.3 109.3 %copy-start.129 = (f32[8]{0:T(128)}, f32[8]{0:T(128)S(1)}, u32[]{:S(2)}) copy-start(f32[8]{0:T(128)S(1)} %get-tuple-element.365) | copy-start | bytes 100
  51.3 23.5 %copy-start.12 = (f32[8,256,256]{1,2,0:T(8,128)}, f32[8,256,256]{1,2,0:T(8,128)S(1)}, u32[]{:S(2)}) copy-start(f32[8,256,256]{1,2,0:T(8,128)S(1)} %get-tuple-element.369) | copy-start | bytes 6291460
  51.3 23.4 %copy-start.80 = (f32[8,256]{1,0:T(8,128)}, f32[8,256]{1,0:T(8,128)S(1)}, u32[]{:S(2)}) copy-start(f32[8,256]{1,0:T(8,128)S(1)} %broadcast_multiply_fusion.14) | copy-start | bytes 24580
  51.6 23.2 %copy-start.97 = (f32[8,256]{1,0:T(8,128)}, f32[8,256]{1,0:T(8,128)S(1)}, u32[]{:S(2)}) copy-start(f32[8,256]{1,0:T(8,128)S(1)} %add_rsqrt_fusion.1) | copy-start | bytes 24580
  55.7 19.0 %copy-start.28 = (f32[8,256,1024]{2,1,0:T(8,128)}, f32[8,256,1024]{2,1,0:T(8,128)S(1)}, u32[]{:S(2)}) copy-start(f32[8,256,1024]{2,1,0:T(8,128)S(1)} %get-tuple-element.370) | copy-start | bytes 25165828
  55.7 19.1 %copy-start.138 = (f32[1,256]{1,0:T(1,128)S(1)}, f32[1,256]{1,0:T(1,128)}, u32[]{:S(2)}) copy-start(f32[1,256]{1,0:T(1,128)} %get-tuple-element.345) | copy-start | bytes 3076
  76.7 72.8 %copy-start.133 = (s32[8,4]{0,1:T(4,128)S(1)}, s32[8,4]{0,1:T(4,128)}, u32[]{:S(2)}) copy-start(s32[8,4]{0,1:T(4,128)} %param.26) | copy-start | bytes 388
  76.7 72.8 %copy-start.145 = (pred[8,4]{0,1:T(4,128)(4,1)S(1)}, pred[8,4]{0,1:T(4,128)(4,1)}, u32[]{:S(2)}) copy-start(pred[8,4]{0,1:T(4,128)(4,1)} %iota_compare_fusion.3) | copy-start | bytes 100
  77.4 74.7 %copy-start.146 = (f32[8]{0:T(128)S(1)}, f32[8]{0:T(128)}, u32[]{:S(2)}) copy-start(f32[8]{0:T(128)} %get-tuple-element.364) | copy-start | bytes 100
  77.4 75.4 %copy-start.38 = (f32[8,64,256]{2,1,0:T(8,128)S(1)}, f32[8,64,256]{2,1,0:T(8,128)}, u32[]{:S(2)}) copy-start(f32[8,64,256]{2,1,0:T(8,128)} %copy-done.37) | copy-start | bytes 1572868
  77.4 75.4 %copy-start.84 = (f32[8,64]{1,0:T(8,128)S(1)}, f32[8,64]{1,0:T(8,128)}, u32[]{:S(2)}) copy-start(f32[8,64]{1,0:T(8,128)} %copy-done.83) | copy-start | bytes 6148
  77.4 75.4 %copy-start.87 = (f32[8,64]{1,0:T(8,128)S(1)}, f32[8,64]{1,0:T(8,128)}, u32[]{:S(2)}) copy-start(f32[8,64]{1,0:T(8,128)} %copy-done.86) | copy-start | bytes 6148
  77.4 75.4 %copy-start.107 = (f32[1,1,256]{2,1,0:T(1,128)S(1)}, f32[1,1,256]{2,1,0:T(1,128)}, u32[]{:S(2)}) copy-start(f32[1,1,256]{2,1,0:T(1,128)} %get-tuple-element.358) | copy-start | bytes 3076
  77.5 77.3 %copy-start.68 = (bf16[2,1024,256]{2,1,0:T(8,128)(2,1)S(1)}, bf16[2,1024,256]{2,1,0:T(8,128)(2,1)}, u32[]{:S(2)}) copy-start(bf16[2,1024,256]{2,1,0:T(8,128)(2,1)} %copy-done.67) | copy-start | bytes 3145732
  77.5 77.3 %copy-start.112 = (f32[1,1024]{1,0:T(1,128)S(1)}, f32[1,1024]{1,0:T(1,128)}, u32[]{:S(2)}) copy-start(f32[1,1024]{1,0:T(1,128)} %copy-done.111) | copy-start | bytes 12292
  78.7 70.9 %copy-start.131 = (f32[8]{0:T(128)}, f32[8]{0:T(128)S(1)}, u32[]{:S(2)}) copy-start(f32[8]{0:T(128)S(1)} %get-tuple-element.363) | copy-start | bytes 100
  151.7 342.6 %all-reduce.8.cloned.1.call-start = ((), (), s32[]{:S(2)}) async-start(), calls=%async_computation.3 | async-start | bytes 262144 | tf_op jit(solution)/shard_map/psum | solution.py:349
  181.3 9.1 %copy-start.95 = (f32[8,64]{1,0:T(8,128)S(1)}, f32[8,64]{1,0:T(8,128)}, u32[]{:S(2)}) copy-start(f32[8,64]{1,0:T(8,128)} %copy-done.93) | copy-start | bytes 6148
  186.3 6.6 copy-start.57
  193.6 9.1 %copy-start.124 = (f32[256]{0:T(256)S(1)}, f32[256]{0:T(256)}, u32[]{:S(2)}) copy-start(f32[256]{0:T(256)} %get-tuple-element.112) | copy-start | bytes 3076
  193.6 9.1 %copy-start.142 = (f32[256]{0:T(256)S(1)}, f32[256]{0:T(256)}, u32[]{:S(2)}) copy-start(f32[256]{0:T(256)} %get-tuple-element.110) | copy-start | bytes 3076
  205.3 77.3 %copy-start.132 = (f32[8]{0:T(128)S(1)}, f32[8]{0:T(128)}, u32[]{:S(2)}) copy-start(f32[8]{0:T(128)} %copy-done.131) | copy-start | bytes 100
  205.3 77.3 %copy-start.143 = (f32[8]{0:T(128)S(1)}, f32[8]{0:T(128)}, u32[]{:S(2)}) copy-start(f32[8]{0:T(128)} %get-tuple-element.362) | copy-start | bytes 100
  205.3 78.0 %copy-start.103 = (f32[1,1,256]{2,1,0:T(1,128)S(1)}, f32[1,1,256]{2,1,0:T(1,128)}, u32[]{:S(2)}) copy-start(f32[1,1,256]{2,1,0:T(1,128)} %get-tuple-element.361) | copy-start | bytes 3076
  287.2 7.6 %copy-start.53 = (bf16[8,256,1024]{2,1,0:T(8,128)(2,1)S(1)}, bf16[8,256,1024]{2,1,0:T(8,128)(2,1)}, u32[]{:S(2)}) copy-start(bf16[8,256,1024]{2,1,0:T(8,128)(2,1)} %copy-done.52) | copy-start | bytes 12582916
  303.9 7.6 %slice-start = ((s8[8388608]{0:T(1024)(128)(4,1)}), s8[4194304]{0:T(1024)(128)(4,1)S(1)}, s32[]{:S(2)}) async-start(s8[8388608]{0:T(1024)(128)(4,1)} %bitcast.742), calls=%async_computation.4 | async-start | bytes 8388608
  375.0 318.2 %all-reduce.6.cloned.1.call-start = ((), (), s32[]{:S(2)}) async-start(), calls=%async_computation.2 | async-start | bytes 262144 | tf_op jit(solution)/shard_map/psum | solution.py:358
  509.4 44.3 %copy-start.63 = (f32[2,4,8,256]{3,1,0,2:T(4,128)S(1)}, f32[2,4,8,256]{3,1,0,2:T(4,128)}, u32[]{:S(2)}) copy-start(f32[2,4,8,256]{3,1,0,2:T(4,128)} %get-tuple-element.211) | copy-start | bytes 196612
  553.2 13.2 %copy-start.105 = (f32[2,8,256]{2,1,0:T(8,128)}, f32[2,8,256]{2,1,0:T(8,128)S(1)}, u32[]{:S(2)}) copy-start(f32[2,8,256]{2,1,0:T(8,128)S(1)} %get-tuple-element.206) | copy-start | bytes 49156
  556.8 7.9 %copy-start.8 = (f32[1,2,256,1024]{3,2,1,0:T(8,128)S(1)}, f32[1,2,256,1024]{3,2,1,0:T(8,128)}, u32[]{:S(2)}) copy-start(f32[1,2,256,1024]{3,2,1,0:T(8,128)} %param.39) | copy-start | bytes 6291460
  556.8 7.8 %copy-start.21 = (f32[1,256,1024]{2,1,0:T(8,128)S(1)}, f32[1,256,1024]{2,1,0:T(8,128)}, u32[]{:S(2)}) copy-start(f32[1,256,1024]{2,1,0:T(8,128)} %convolution_bitcast_fusion.3) | copy-start | bytes 3145732
  556.8 7.8 %copy-start.26 = (f32[1,256,1024]{2,1,0:T(8,128)S(1)}, f32[1,256,1024]{2,1,0:T(8,128)}, u32[]{:S(2)}) copy-start(f32[1,256,1024]{2,1,0:T(8,128)} %convolution_bitcast_fusion.2) | copy-start | bytes 3145732
  693.2 11.8 %copy-start.113 = (f32[2,2,256]{2,1,0:T(2,128)S(1)}, f32[2,2,256]{2,1,0:T(2,128)}, u32[]{:S(2)}) copy-start(f32[2,2,256]{2,1,0:T(2,128)} %param.31) | copy-start | bytes 12292
  693.2 11.8 %copy-start.128 = (f32[2,2,256]{2,1,0:T(2,128)S(1)}, f32[2,2,256]{2,1,0:T(2,128)}, u32[]{:S(2)}) copy-start(f32[2,2,256]{2,1,0:T(2,128)} %param.36) | copy-start | bytes 12292
  693.2 12.4 %copy-start.79 = (f32[2,2560]{1,0:T(2,128)S(1)}, f32[2,2560]{1,0:T(2,128)}, u32[]{:S(2)}) copy-start(f32[2,2560]{1,0:T(2,128)} %param.32) | copy-start | bytes 61444
  693.2 12.4 %copy-start.99 = (f32[2,2560]{1,0:T(2,128)S(1)}, f32[2,2560]{1,0:T(2,128)}, u32[]{:S(2)}) copy-start(f32[2,2560]{1,0:T(2,128)} %param.37) | copy-start | bytes 61444
  715.8 6.8 copy-start.34
  715.8 7.4 %copy-start.54 = (f32[2,256,1024]{2,1,0:T(8,128)S(1)}, f32[2,256,1024]{2,1,0:T(8,128)}, u32[]{:S(2)}) copy-start(f32[2,256,1024]{2,1,0:T(8,128)} %param.34) | copy-start | bytes 6291460
  (107 other events, 281.7 us)
Sparse Core Ops, SparseCore 0:
  151.8 129.7 reduce-scatter.1
  375.1 119.0 all-reduce.7
  570.5 122.6 all-reduce.5
where the time goes:
time: 753 us; the launch traced here: 742 us
  waiting for transfers between devices  314 us (42%)
  matrix products  154 us (20%)
  blocking collectives  111 us (15%)
  other arithmetic  93.1 us (12%)
  local copies, waits for them, and re-layouts  49.4 us (7%)
  between operations  20.3 us (3%)
    psum x1, waiting for transfers between devices, per_device(): lax.psum((right_attn, right_inner, right_outer), ('dp', 'outer'))  122 us
    psum x1, waiting for transfers between devices, per_device(): lax.psum((left_attn, left_inner, left_outer, gain_grad, shift_grad), ('dp...  119 us
    reduce_scatter x1, waiting for transfers between devices, per_device(): lax.psum_scatter(partial_terms, ('dp', 'outer'), scatter_dimension=0, til...  72.5 us
    all_gather x1, blocking collectives, per_device(): lax.all_gather(passage_unit, ('dp', 'outer'), axis=0, tiled=True)  70.7 us
    psum x1, blocking collectives, per_device(): lax.psum((left_attn, left_inner, left_outer, gain_grad, shift_grad), ('dp...  40.3 us
    unnamed x322, local copies, waits for them, and re-layouts  28.3 us
    convert_element_type x2, other arithmetic, encoder_forward(): active_low = jax.nn.gelu(upper_in, approximate=False).astype(jnp.bfloat16)  23.8 us
    dot_general x2, matrix products, encoder_backward(): jnp.einsum('bhqk,bkhe->bqhe', grad_raw, key_heads, preferred_element_type...  21.5 us
  transfers between devices with their start and end apart: 3, of which 3 were waited for; matrix products, arithmetic and copies ran while one was open for 8% of the time, Pallas kernels for 0%

commit v1 on v0

v1 whole, which is shorter than its diff:
```python
import functools
import math

import jax
import jax.numpy as jnp
from jax import lax
from jax.experimental import pallas as pl
from jax.experimental.pallas import tpu as pltpu
from jax.sharding import PartitionSpec as P

HEAD = 64
TOK = 256
ONES = 16

NORM_EPSILON = 1e-06
UNIT_EPSILON = 1e-06
SCORE_SCALE = 20.0
MOMENTUM_DECAY = 0.9
LEARNING_RATE = 10.0
CLIP_NORM = 2.0
MASKED_SCORE = -1e30
HIGHEST = lax.Precision.HIGHEST
AXES = ("dp", "outer")
F32 = jnp.float32
BF16 = jnp.bfloat16
VMEM_LIMIT = 56 << 20


def mm(a, b, precision=None):
    return lax.dot_general(a, b, (((1,), (0,)), ((), ())), precision=precision, preferred_element_type=F32)


def mm_nt(a, b, precision=None):
    return lax.dot_general(a, b, (((1,), (1,)), ((), ())), precision=precision, preferred_element_type=F32)


def mm_tn(a, b, precision=None):
    return lax.dot_general(a, b, (((0,), (0,)), ((), ())), precision=precision, preferred_element_type=F32)


def wide(column):
    return jnp.concatenate([column, column], axis=1)


def split_two(v):
    high = v.astype(BF16)
    return high, (v - high.astype(F32)).astype(BF16)


def split_three(v):
    high = v.astype(BF16)
    rest = v - high.astype(F32)
    middle = rest.astype(BF16)
    return high, middle, (rest - middle.astype(F32)).astype(BF16)


def norm_columns(hidden, gain, shift):
    share = 1.0 / hidden.shape[0]
    center = hidden - jnp.sum(hidden, axis=0, keepdims=True) * share
    inverse = lax.rsqrt(jnp.sum(center * center, axis=0, keepdims=True) * share + NORM_EPSILON)
    normed = center * inverse
    return normed * gain + shift, normed, inverse


def norm_columns_back(grad, normed, inverse, gain):
    share = 1.0 / grad.shape[0]
    scaled = grad * gain
    mean = jnp.sum(scaled, axis=0, keepdims=True) * share
    along = jnp.sum(scaled * normed, axis=0, keepdims=True) * share
    return inverse * (scaled - mean - normed * along)


def gelu_and_slope(u):
    d = 1.0 + (0.3275911 * 0.5**0.5) * jnp.abs(u)
    t = pl.reciprocal(d, approx=True)
    t = t * (2.0 - d * t)
    poly = t * (0.127414796 + t * (-0.142248368 + t * (0.7107068705 + t * (-0.7265760135 + t * 0.5307027145))))
    bell = jnp.exp2(u * u * (-0.5 * math.log2(math.e)))
    tail = poly * bell
    phi = jnp.where(u >= 0.0, 1.0 - tail, tail)
    return u * phi, phi + u * bell * (0.5 / math.pi) ** 0.5


def forward_kernel(
    nqu, qlen, plen, xq, xp, attn, w_in, w_out, gains, biases,
    x_out, qk_out, v_out, p_out, ctx_out, n1_out, first_out, slope_out, act_out, n2_out, inv_out, share_out, pooled_out, units_out,
    wproj, wo_t, win_t, wout_t, bias_bc, gain_bc, qblk, xs, away,
):
    i = pl.program_id(0)
    last = pl.num_programs(0) - 1
    is_q = i < nqu
    t = jnp.where(is_q, 0, 1)
    d = xs.shape[1]
    ff = win_t.shape[0]
    heads = d // HEAD
    segs = TOK // HEAD

    @pl.when(i == 0)
    def _():
        qblk[...] = jnp.zeros_like(qblk)

    @pl.when((i == 0) | (i == nqu))
    def _():
        eye = (lax.broadcasted_iota(jnp.int32, (d, d), 0) == lax.broadcasted_iota(jnp.int32, (d, d), 1)).astype(F32).astype(BF16)
        for j in range(3):
            wproj[j * d : (j + 1) * d, :] = mm_nt(eye, attn[0, j].astype(BF16)).astype(BF16)
        wproj[3 * d : 4 * d, :] = eye
        wproj[4 * d : 5 * d, :] = attn[0, 1].astype(BF16)
        wproj[5 * d : 6 * d, :] = attn[0, 2].astype(BF16)
        wo_t[...] = mm_nt(eye, attn[0, 3].astype(BF16)).astype(BF16)
        for c in range(ff // d):
            at = slice(c * d, (c + 1) * d)
            win_t[at, :] = mm_nt(eye, w_in[0, :, at].astype(BF16)).astype(BF16)
            wout_t[:, at] = mm_nt(eye, w_out[0, at, :].astype(BF16)).astype(BF16)
        for c in range(bias_bc.shape[0] // d):
            row = biases[pl.ds(t, 1), c * d : (c + 1) * d]
            bias_bc[c * d : (c + 1) * d, :] = jnp.broadcast_to(row, (128, d)).T
        for c in range(2):
            row = gains[pl.ds(t * 2 + c, 1), :]
            gain_bc[c * d : (c + 1) * d, :] = jnp.broadcast_to(row, (128, d)).T

    @pl.when(is_q)
    def _():
        xs[...] = xq[0]

    @pl.when(jnp.logical_not(is_q))
    def _():
        xs[...] = xp[0]

    lens = [qlen[jnp.minimum(i, nqu - 1) * segs + s] for s in range(segs)]
    whole = plen[jnp.maximum(i - nqu, 0)]

    def length_of(segment):
        out = jnp.full(segment.shape, lens[segs - 1], jnp.int32)
        for s in range(segs - 1):
            out = jnp.where(segment == s, lens[s], out)
        return jnp.where(is_q, out, whole)

    key = lax.broadcasted_iota(jnp.int32, (TOK, TOK), 0)
    ask = lax.broadcasted_iota(jnp.int32, (TOK, TOK), 1)
    bad_far = is_q & ((key // HEAD) != (ask // HEAD))
    place = jnp.where(is_q, key % HEAD, key)
    away[...] = jnp.where(bad_far | (place >= length_of(key // HEAD)), MASKED_SCORE, 0.0)

    row = lax.broadcasted_iota(jnp.int32, (8, TOK), 0)
    token = lax.broadcasted_iota(jnp.int32, (8, TOK), 1)
    live_len = length_of(token // HEAD)
    owner = jnp.where(is_q, token // HEAD, 0)
    place = jnp.where(is_q, token % HEAD, token)
    share = jnp.where((place < live_len) & (row == owner), 1.0 / live_len.astype(F32), 0.0)
    share_out[0] = share

    def bias(at, size):
        return wide(bias_bc[at : at + size, :])

    x = xs[...]
    q_t = (mm_nt(wproj[0:d, :], x) + bias(0, d)).astype(BF16)
    qk_out[0, 0:d, :] = q_t
    qk_out[0, d : 2 * d, :] = mm_nt(wproj[d : 2 * d, :], x).astype(BF16)
    v_t = (mm_nt(wproj[2 * d : 3 * d, :], x) + bias(d, d)).astype(BF16)
    x_t = mm_nt(wproj[3 * d : 4 * d, :], x)
    x_out[0, 0:d, :] = x_t.astype(BF16)
    k_row = mm(x, wproj[4 * d : 5 * d, :]).astype(BF16)
    v_out[0] = (mm(x, wproj[5 * d : 6 * d, :]) + biases[pl.ds(t, 1), d : 2 * d]).astype(BF16)
    for h in range(heads):
        qblk[h * HEAD : (h + 1) * HEAD, h * TOK : (h + 1) * TOK] = q_t[h * HEAD : (h + 1) * HEAD, :] * BF16(HEAD**-0.5)
    for h in range(heads):
        scores = mm(k_row, qblk[:, h * TOK : (h + 1) * TOK]) + away[...]
        exponent = jnp.exp(scores - jnp.max(scores, axis=0, keepdims=True))
        probs = exponent * (1.0 / jnp.sum(exponent, axis=0, keepdims=True))
        p_low = probs.astype(BF16)
        p_out[0, h] = p_low
        ctx_out[0, h * HEAD : (h + 1) * HEAD, :] = mm(v_t[h * HEAD : (h + 1) * HEAD, :], p_low).astype(BF16)
    hidden = x_t + (mm(wo_t[...], ctx_out[0, 0:d, :]) + bias(2 * d, d))
    first, n1, inv1 = norm_columns(hidden, wide(gain_bc[0:d, :]), bias(3 * d, d))
    n1_out[0] = n1
    first_low = first.astype(BF16)
    first_out[0, 0:d, :] = first_low
    hidden = first + bias(4 * d, d)
    for c in range(ff // d):
        at = slice(c * d, (c + 1) * d)
        upper = mm(win_t[at, :], first_low) + bias(6 * d + c * d, d)
        active, slope = gelu_and_slope(upper)
        slope_out[0, at, :] = slope
        active_low = active.astype(BF16)
        act_out[0, at, :] = active_low
        hidden = hidden + mm(wout_t[:, at], active_low)
    second, n2, inv2 = norm_columns(hidden, wide(gain_bc[d : 2 * d, :]), bias(5 * d, d))
    n2_out[0] = n2
    inv_out[0] = jnp.where(row == 0, inv1, inv2)
    pooled = mm_nt(share, second, HIGHEST)
    ones = jnp.ones((ONES, TOK), BF16)
    x_out[0, d:, :] = ones
    ctx_out[0, d:, :] = ones
    first_out[0, d:, :] = ones
    act_out[0, ff:, :] = ones

    @pl.when(is_q)
    def _():
        for s in range(segs):
            pooled_out[pl.ds(i * segs + s, 1), :] = pooled[s : s + 1, :]

    @pl.when(jnp.logical_not(is_q))
    def _():
        pooled_out[pl.ds(nqu * segs + i - nqu, 1), :] = pooled[0:1, :]

    @pl.when(i == last)
    def _():
        rows = pooled_out[...]
        unit = (rows * lax.rsqrt(jnp.sum(rows * rows, axis=1, keepdims=True) + UNIT_EPSILON)).astype(BF16)
        units_out[...] = jnp.broadcast_to(unit[None], units_out.shape)


def tower_of(nqu):
    return lambda i, *_: jnp.where(i < nqu, 0, 1)


def unit_spec(*shape):
    return pl.BlockSpec((1,) + shape, lambda i, *_: (i,) + (0,) * len(shape))


def tower_spec(nqu, *shape):
    return pl.BlockSpec((1,) + shape, lambda i, *_: (jnp.where(i < nqu, 0, 1),) + (0,) * len(shape))


def whole_spec(*shape):
    return pl.BlockSpec(shape, lambda i, *_: (0,) * len(shape))


def forward(devices, q_lengths, p_lengths, xq, xp, attn, w_in, w_out, gains, biases):
    nqu, npu = xq.shape[0], xp.shape[0]
    units = nqu + npu
    d, ff = w_in.shape[1:]
    heads = d // HEAD
    seqs = q_lengths.shape[0] + npu
    outs = [
        ((d + ONES, TOK), BF16),
        ((2 * d, TOK), BF16),
        ((TOK, d), BF16),
        ((heads, TOK, TOK), BF16),
        ((d + ONES, TOK), BF16),
        ((d, TOK), F32),
        ((d + ONES, TOK), BF16),
        ((ff, TOK), F32),
        ((ff + ONES, TOK), BF16),
        ((d, TOK), F32),
        ((8, TOK), F32),
        ((8, TOK), F32),
    ]
    return pl.pallas_call(
        functools.partial(forward_kernel, nqu),
        grid_spec=pltpu.PrefetchScalarGridSpec(
            num_scalar_prefetch=2,
            grid=(units,),
            in_specs=[
                pl.BlockSpec((1, TOK, d), lambda i, *_: (jnp.minimum(i, nqu - 1), 0, 0)),
                pl.BlockSpec((1, TOK, d), lambda i, *_: (jnp.maximum(i - nqu, 0), 0, 0)),
                tower_spec(nqu, 4, d, d),
                tower_spec(nqu, d, ff),
                tower_spec(nqu, ff, d),
                whole_spec(4, d),
                whole_spec(2, biases.shape[1]),
            ],
            out_specs=[unit_spec(*shape) for shape, _ in outs] + [whole_spec(seqs, d), whole_spec(devices, seqs, d)],
            scratch_shapes=[
                pltpu.VMEM((6 * d, d), BF16),
                pltpu.VMEM((d, d), BF16),
                pltpu.VMEM((ff, d), BF16),
                pltpu.VMEM((d, ff), BF16),
                pltpu.VMEM((biases.shape[1], 128), F32),
                pltpu.VMEM((2 * d, 128), F32),
                pltpu.VMEM((d, heads * TOK), BF16),
                pltpu.VMEM((TOK, d), BF16),
                pltpu.VMEM((TOK, TOK), F32),
            ],
        ),
        out_shape=[jax.ShapeDtypeStruct((units,) + shape, kind) for shape, kind in outs]
        + [jax.ShapeDtypeStruct((seqs, d), F32), jax.ShapeDtypeStruct((devices, seqs, d), BF16)],
        compiler_params=pltpu.CompilerParams(vmem_limit_bytes=VMEM_LIMIT),
        name="forward",
    )(q_lengths, p_lengths, xq, xp, attn, w_in, w_out, gains.reshape(4, d), biases)


def contrast_kernel(nqu, index, units, lists, pooled, loss_out, gp_out, low_rows, gup_rows):
    devices, seqs, d = units.shape
    own = lists.shape[0] // devices
    mine = pl.multiple_of(index[0] * own, own)
    pown = seqs - own
    pmine = pl.multiple_of(index[0] * pown, pown)
    both = units[...].astype(F32)
    uq = both[:, :own, :].reshape(devices * own, d).astype(BF16)
    up = both[:, own:, :].reshape(devices * pown, d).astype(BF16)
    scores = SCORE_SCALE * mm_nt(uq, up)
    columns = lax.broadcasted_iota(jnp.int32, scores.shape, 1)
    slots = lists.shape[1] - 1
    positive = None
    for k in range(slots):
        hit = (lists[:, k : k + 1] == columns) & (lists[:, slots : slots + 1] > k)
        positive = hit if positive is None else positive | hit
    highest = jnp.max(scores, axis=1, keepdims=True)
    whole = highest + jnp.log(jnp.sum(jnp.exp(scores - highest), axis=1, keepdims=True))
    chosen = jnp.where(positive, scores, MASKED_SCORE)
    top = jnp.max(chosen, axis=1, keepdims=True)
    within = top + jnp.log(jnp.sum(jnp.exp(chosen - top), axis=1, keepdims=True))
    low = (SCORE_SCALE * (jnp.exp(scores - whole) - jnp.exp(chosen - within))).astype(BF16)
    low_rows[:, : scores.shape[1]] = low.astype(F32)
    low_rows[:, scores.shape[1] :] = jnp.broadcast_to(whole - within, (scores.shape[0], 128))
    loss_out[...] = low_rows[pl.ds(mine, own), scores.shape[1] :]
    grad_q = mm(low_rows[pl.ds(mine, own), : scores.shape[1]].astype(BF16), up)
    gup_rows[...] = mm_tn(low, uq)
    grad_p = gup_rows[pl.ds(pmine, pown), :]
    grad = jnp.concatenate([grad_q, grad_p], axis=0)
    rows = pooled[...]
    inverse = lax.rsqrt(jnp.sum(rows * rows, axis=1, keepdims=True) + UNIT_EPSILON)
    grad = inverse * grad - inverse * inverse * inverse * rows * jnp.sum(rows * grad, axis=1, keepdims=True)
    segs = own // nqu
    gp_out[...] = jnp.zeros_like(gp_out)
    for s in range(own):
        gp_out[s // segs, s % segs : s % segs + 1, :] = grad[s : s + 1, :]
    for s in range(pown):
        gp_out[nqu + s, 0:1, :] = grad[own + s : own + s + 1, :]


def contrast(nqu, npu, index, units, lists, pooled):
    devices, seqs, d = units.shape
    own = lists.shape[0] // devices
    passages = devices * (seqs - own)
    vmem = pl.BlockSpec(memory_space=pltpu.VMEM)
    return pl.pallas_call(
        functools.partial(contrast_kernel, nqu),
        in_specs=[pl.BlockSpec(memory_space=pltpu.SMEM), vmem, vmem, vmem],
        out_specs=[vmem, vmem],
        out_shape=[jax.ShapeDtypeStruct((own, 128), F32), jax.ShapeDtypeStruct((nqu + npu, 8, d), F32)],
        scratch_shapes=[pltpu.VMEM((devices * own, passages + 128), F32), pltpu.VMEM((passages, d), F32)],
        compiler_params=pltpu.CompilerParams(vmem_limit_bytes=VMEM_LIMIT),
        name="contrast",
    )(index, units, lists, pooled)


def left_rows(start_t, matrix):
    s_high, s_low = split_two(start_t)
    m_high, m_low = split_two(matrix)
    both = mm_nt(jnp.concatenate([s_high, s_low], axis=0), m_high)
    return both[:8] + both[8:] + mm_nt(jnp.concatenate([s_high, s_high], axis=0), m_low)[:8]


def right_rows(basis, matrix):
    b_high, b_low = split_two(basis)
    m_high, m_low = split_two(matrix)
    both = mm(jnp.concatenate([b_high, b_low], axis=0), m_high)
    return both[:8] + both[8:] + mm(jnp.concatenate([b_high, b_high], axis=0), m_low)[:8]


def backward_kernel(
    nqu, gp, x_in, qk_in, v_in, p_in, ctx_in, n1_in, first_in, slope_in, act_in, n2_in, inv_in, share_in,
    attn, w_in, w_out, gains, attn_err, in_err, out_err, attn_start, in_start, out_start,
    qgrad, pgrad, attn_m, in_m, out_m, left,
    wqkv, wo, win, wout, gain_bc, gz, graw_s, gqkv, acc_qkv, acc_o, acc_in, acc_out, acc_gain,
):
    i = pl.program_id(0)
    last = pl.num_programs(0) - 1
    is_q = i < nqu
    t = jnp.where(is_q, 0, 1)
    d = wo.shape[0]
    ff = wout.shape[0]
    heads = d // HEAD

    @pl.when(i == 0)
    def _():
        gz[...] = jnp.zeros_like(gz)

    @pl.when((i == 0) | (i == nqu))
    def _():
        for j in range(3):
            wqkv[:, j * d : (j + 1) * d] = attn[0, j].astype(BF16)
        wo[...] = attn[0, 3].astype(BF16)
        win[...] = w_in[0].astype(BF16)
        wout[...] = w_out[0].astype(BF16)
        for c in range(2):
            row = gains[pl.ds(t * 2 + c, 1), :]
            gain_bc[c * d : (c + 1) * d, :] = jnp.broadcast_to(row, (128, d)).T
        acc_qkv[...] = jnp.zeros_like(acc_qkv)
        acc_o[...] = jnp.zeros_like(acc_o)
        acc_in[...] = jnp.zeros_like(acc_in)
        acc_out[...] = jnp.zeros_like(acc_out)
        acc_gain[...] = jnp.zeros_like(acc_gain)

    def add_gain(at, value):
        acc_gain[at * d : (at + 1) * d, :] += value[:, :128] + value[:, 128:]

    grad_second = mm_tn(gp[0], share_in[0], HIGHEST)
    n2 = n2_in[0]
    grad_two = norm_columns_back(grad_second, n2, inv_in[0, 1:2, :], wide(gain_bc[d : 2 * d, :]))
    add_gain(1, grad_second * n2)
    add_gain(3, grad_second)
    down_low = grad_two.astype(BF16)
    acc_out[...] += mm_nt(act_in[0], down_low)
    grad_first = grad_two
    for c in range(ff // d):
        at = slice(c * d, (c + 1) * d)
        up_low = (mm(wout[at, :], down_low) * slope_in[0, at, :]).astype(BF16)
        acc_in[:, at] += mm_nt(first_in[0], up_low)
        grad_first = grad_first + mm(win[:, at], up_low)
    n1 = n1_in[0]
    grad_one = norm_columns_back(grad_first, n1, inv_in[0, 0:1, :], wide(gain_bc[0:d, :]))
    add_gain(0, grad_first * n1)
    add_gain(2, grad_first)
    branch_low = grad_one.astype(BF16)
    acc_o[...] += mm_nt(ctx_in[0], branch_low)
    grad_context = mm(wo[...], branch_low).astype(BF16)
    for h in range(heads):
        at = slice(h * HEAD, (h + 1) * HEAD)
        gz[at, h * TOK : (h + 1) * TOK] = grad_context[at, :]
    for h in range(heads):
        at = slice(h * HEAD, (h + 1) * HEAD)
        p_low = p_in[0, h]
        probs = p_low.astype(F32)
        grad_probs = mm(v_in[0], gz[:, h * TOK : (h + 1) * TOK])
        inner = jnp.sum(grad_probs * probs, axis=0, keepdims=True)
        graw = (probs * (grad_probs - inner) * HEAD**-0.5).astype(BF16)
        gqkv[at, :] = mm(qk_in[0, d + h * HEAD : d + (h + 1) * HEAD, :], graw).astype(BF16)
        gqkv[d + h * HEAD : d + (h + 1) * HEAD, :] = mm_nt(qk_in[0, at, :], graw).astype(BF16)
        gqkv[2 * d + h * HEAD : 2 * d + (h + 1) * HEAD, :] = mm_nt(grad_context[at, :], p_low).astype(BF16)
    acc_qkv[...] += mm_nt(x_in[0], gqkv[...])
    result = (grad_one + mm(wqkv[...], gqkv[...])).T

    @pl.when(is_q)
    def _():
        qgrad[0] = result

    @pl.when(jnp.logical_not(is_q))
    def _():
        pgrad[0] = result

    @pl.when((i == nqu - 1) | (i == last))
    def _():
        base_in = 8 * d
        base_out = base_in + 2 * d
        base_vec = base_out + 2 * ff
        for j in range(4):
            grad = acc_o[0:d, :] if j == 3 else acc_qkv[0:d, j * d : (j + 1) * d]
            merged = grad + attn_err[0, 0, j]
            attn_m[0, j] = merged
            left[:, pl.ds(pl.multiple_of((t * 4 + j) * d, 128), d)] = left_rows(attn_start[0, j], merged)
        merged = acc_in[0:d, :] + in_err[0, 0]
        in_m[0] = merged
        left[:, pl.ds(pl.multiple_of(base_in + t * d, 128), d)] = left_rows(in_start[0], merged)
        merged = acc_out[0:ff, :] + out_err[0, 0]
        out_m[0] = merged
        left[:, pl.ds(pl.multiple_of(base_out + t * ff, 128), ff)] = left_rows(out_start[0], merged)
        sums = mm_nt(jnp.ones((8, 128), F32), acc_gain[...], HIGHEST)

        def vectors():
            yield sums[0:1, 0:d]
            yield sums[0:1, d : 2 * d]
            yield acc_qkv[d : d + 1, 0:d]
            yield acc_qkv[d : d + 1, 2 * d : 3 * d]
            yield acc_o[d : d + 1, :]
            yield sums[0:1, 2 * d : 3 * d]
            yield acc_out[ff : ff + 1, :]
            yield sums[0:1, 3 * d : 4 * d]
            for c in range(ff // d):
                yield acc_in[d : d + 1, c * d : (c + 1) * d]

        for tower in range(2):

            @pl.when(t == tower)
            def _(tower=tower):
                for v, vector in enumerate(vectors()):
                    at = tower * 12 + v
                    left[at // 3 : at // 3 + 1, base_vec + (at % 3) * d : base_vec + (at % 3 + 1) * d] = vector


def backward(nqu, npu, gp, saved, attn, w_in, w_out, gains, attn_err, in_err, out_err, starts):
    units = nqu + npu
    d, ff = w_in.shape[1:]
    heads = d // HEAD
    width = 8 * d + 2 * d + 2 * ff + 3 * d
    tower = functools.partial(tower_spec, nqu)

    def error_spec(*shape):
        return pl.BlockSpec((1, 1) + shape, lambda i: (0, jnp.where(i < nqu, 0, 1)) + (0,) * len(shape))

    return pl.pallas_call(
        functools.partial(backward_kernel, nqu),
        grid=(units,),
        in_specs=[unit_spec(8, d)]
        + [unit_spec(*array.shape[1:]) for array in saved]
        + [tower(4, d, d), tower(d, ff), tower(ff, d), whole_spec(4, d)]
        + [error_spec(4, d, d), error_spec(d, ff), error_spec(ff, d)]
        + [tower(4, 8, d), tower(8, ff), tower(8, d)],
        out_specs=[
            pl.BlockSpec((1, TOK, d), lambda i: (jnp.minimum(i, nqu - 1), 0, 0)),
            pl.BlockSpec((1, TOK, d), lambda i: (jnp.maximum(i - nqu, 0), 0, 0)),
            tower(4, d, d),
            tower(d, ff),
            tower(ff, d),
            whole_spec(8, width),
        ],
        out_shape=[
            jax.ShapeDtypeStruct((nqu, TOK, d), F32),
            jax.ShapeDtypeStruct((npu, TOK, d), F32),
            jax.ShapeDtypeStruct((2, 4, d, d), F32),
            jax.ShapeDtypeStruct((2, d, ff), F32),
            jax.ShapeDtypeStruct((2, ff, d), F32),
            jax.ShapeDtypeStruct((8, width), F32),
        ],
        scratch_shapes=[
            pltpu.VMEM((d, 3 * d), BF16),
            pltpu.VMEM((d, d), BF16),
            pltpu.VMEM((d, ff), BF16),
            pltpu.VMEM((ff, d), BF16),
            pltpu.VMEM((2 * d, 128), F32),
            pltpu.VMEM((d, heads * TOK), BF16),
            pltpu.VMEM((TOK, TOK), BF16),
            pltpu.VMEM((3 * d, TOK), BF16),
            pltpu.VMEM((d + ONES, 3 * d), F32),
            pltpu.VMEM((d + ONES, d), F32),
            pltpu.VMEM((d + ONES, ff), F32),
            pltpu.VMEM((ff + ONES, d), F32),
            pltpu.VMEM((4 * d, 128), F32),
        ],
        compiler_params=pltpu.CompilerParams(vmem_limit_bytes=VMEM_LIMIT),
        name="backward",
    )(gp, *saved, attn, w_in, w_out, gains.reshape(4, d), attn_err, in_err, out_err, *starts)


def right_kernel(left, attn_m, in_m, out_m, basis, right):
    d, ff = in_m.shape[1:]
    places = [(j * d, d) for j in range(8)] + [(8 * d + t * d, d) for t in range(2)] + [(10 * d + t * ff, ff) for t in range(2)]
    blocks = [left[:, at : at + size] for at, size in places]
    for j in range(8):
        for b, block in enumerate(blocks):
            order = lax.broadcasted_iota(jnp.int32, (8, 1), 0)
            column = block[j : j + 1, :]
            dots = jnp.sum(block * column, axis=1, keepdims=True)
            scale = lax.rsqrt(dots[j : j + 1, :] + 1e-06)
            unit = column * scale
            step = jnp.where(order > j, dots * scale, 0.0)
            blocks[b] = jnp.where(order == j, unit, block - step * unit)
    for (at, size), block in zip(places, blocks):
        basis[:, at : at + size] = block
    for j in range(8):
        right[:, j * d : (j + 1) * d] = right_rows(blocks[j], attn_m[j // 4, j % 4])
    for t in range(2):
        right[:, 8 * d + t * ff : 8 * d + (t + 1) * ff] = right_rows(blocks[8 + t], in_m[t])
        right[:, 8 * d + 2 * ff + t * d : 8 * d + 2 * ff + (t + 1) * d] = right_rows(blocks[10 + t], out_m[t])


def right_factors(left, attn_m, in_m, out_m):
    d, ff = in_m.shape[1:]
    vmem = pl.BlockSpec(memory_space=pltpu.VMEM)
    return pl.pallas_call(
        right_kernel,
        in_specs=[vmem] * 4,
        out_specs=[vmem] * 2,
        out_shape=[jax.ShapeDtypeStruct((8, 10 * d + 2 * ff), F32), jax.ShapeDtypeStruct((8, 10 * d + 2 * ff), F32)],
        compiler_params=pltpu.CompilerParams(vmem_limit_bytes=VMEM_LIMIT),
        name="right",
    )(left, attn_m, in_m, out_m)


def update_kernel(
    replicas, basis, right, left, attn_m, in_m, out_m, attn, w_in, w_out, attn_mom, in_mom, out_mom,
    attn_new, in_new, out_new, attn_mom_new, in_mom_new, out_mom_new, attn_err, in_err, out_err, norm_out, clip_s,
):
    i = pl.program_id(0)
    d = attn.shape[2]
    ff = (right.shape[1] - 10 * d) // 2
    t, c = i // 4, i % 4

    @pl.when(i == 0)
    def _():
        places = [((j * d, d), (j * d, d)) for j in range(8)]
        places += [((8 * d + s * d, d), (8 * d + s * ff, ff)) for s in range(2)]
        places += [((10 * d + s * ff, ff), (8 * d + 2 * ff + s * d, d)) for s in range(2)]
        total = jnp.zeros((8, 8), F32)
        for (b_at, b_size), (r_at, r_size) in places:
            b = basis[:, b_at : b_at + b_size]
            r = right[:, r_at : r_at + r_size]
            total = total + mm_nt(b, b, HIGHEST) * mm_nt(r, r, HIGHEST)
        vector = left[:, 10 * d + 2 * ff :]
        square = jnp.sum(jnp.sum(total, axis=1, keepdims=True), axis=0, keepdims=True)
        square = square + jnp.sum(jnp.sum(vector * vector, axis=1, keepdims=True), axis=0, keepdims=True)
        norm = jnp.sqrt(jnp.broadcast_to(square, (8, 128)))
        norm_out[...] = norm
        clip_s[...] = jnp.minimum(1.0, CLIP_NORM / norm)

    clip = clip_s[0:1, 0:1]

    def step(b_at, r_at, merged, weight, moment, weight_new, moment_new, error):
        b1, b2, b3 = split_three(basis[:, pl.ds(pl.multiple_of(b_at, 128), d)])
        r1, r2, r3 = split_three(right[:, pl.ds(pl.multiple_of(r_at, 128), d)])
        approx = mm_tn(jnp.concatenate([b1, b1, b2, b1, b2, b3], axis=0), jnp.concatenate([r1, r2, r1, r3, r2, r1], axis=0))
        moved = MOMENTUM_DECAY * moment + clip * approx
        moment_new[...] = moved.reshape(moment_new.shape)
        weight_new[...] = (weight - LEARNING_RATE * moved).reshape(weight_new.shape)
        error[...] = (merged - approx * (1.0 / replicas)).reshape(error.shape)

    step(i * d, i * d, attn_m[0, 0], attn[0, 0], attn_mom[0, 0], attn_new, attn_mom_new, attn_err)
    step((8 + t) * d, 8 * d + t * ff + c * d, in_m[0], w_in[0], in_mom[0], in_new, in_mom_new, in_err)
    step(10 * d + t * ff + c * d, 8 * d + 2 * ff + t * d, out_m[0], w_out[0], out_mom[0], out_new, out_mom_new, out_err)


def update(replicas, basis, right, left, attn_m, in_m, out_m, attn, w_in, w_out, attn_mom, in_mom, out_mom):
    d, ff = w_in.shape[1:]
    a_spec = pl.BlockSpec((1, 1, d, d), lambda i: (i // 4, i % 4, 0, 0))
    i_spec = pl.BlockSpec((1, d, d), lambda i: (i // 4, 0, i % 4))
    o_spec = pl.BlockSpec((1, d, d), lambda i: (i // 4, i % 4, 0))
    ae_spec = pl.BlockSpec((1, 1, 1, d, d), lambda i: (0, i // 4, i % 4, 0, 0))
    ie_spec = pl.BlockSpec((1, 1, d, d), lambda i: (0, i // 4, 0, i % 4))
    oe_spec = pl.BlockSpec((1, 1, d, d), lambda i: (0, i // 4, i % 4, 0))
    shape = jax.ShapeDtypeStruct
    return pl.pallas_call(
        functools.partial(update_kernel, replicas),
        grid=(8,),
        in_specs=[whole_spec(*basis.shape), whole_spec(*right.shape), whole_spec(*left.shape)] + [a_spec, i_spec, o_spec] * 3,
        out_specs=[a_spec, i_spec, o_spec] * 2 + [ae_spec, ie_spec, oe_spec, whole_spec(8, 128)],
        out_shape=[shape(a.shape, F32) for a in (attn, w_in, w_out, attn, w_in, w_out)]
        + [shape((1,) + a.shape, F32) for a in (attn, w_in, w_out)]
        + [shape((8, 128), F32)],
        scratch_shapes=[pltpu.VMEM((8, 128), F32)],
        compiler_params=pltpu.CompilerParams(vmem_limit_bytes=VMEM_LIMIT),
        name="update",
    )(basis, right, left, attn_m, in_m, out_m, attn, w_in, w_out, attn_mom, in_mom, out_mom)


def swap_with(x, axis, mask):
    return lax.ppermute(x, axis, [(i, i ^ mask) for i in range(lax.axis_size(axis))])


def sum_over(x):
    half = x.shape[1] // 2
    core = lax.axis_index("dp") % 2
    mine = lax.dynamic_slice_in_dim(x, core * half, half, 1)
    other = lax.dynamic_slice_in_dim(x, (1 - core) * half, half, 1)
    mine = mine + swap_with(other, "dp", 1)
    size = lax.axis_size("dp")
    if size == 8:
        steps = [("dp", (2, 4, 6))]
    else:
        steps = [("dp", (1 << b,)) for b in range(1, size.bit_length() - 1)]
    steps.append(("outer", tuple(range(1, lax.axis_size("outer")))))
    for axis, masks in steps:
        for got in [swap_with(mine, axis, mask) for mask in masks]:
            mine = mine + got
    other = swap_with(mine, "dp", 1)
    low = jnp.where(core == 0, mine, other)
    high = jnp.where(core == 0, other, mine)
    return jnp.concatenate([low, high], axis=1)


def momentum_step(weight, moment, gradient, clip_factor):
    moment_new = MOMENTUM_DECAY * moment + clip_factor * gradient
    return (weight - LEARNING_RATE * moment_new, moment_new)


def per_device(
    questions, passages, q_lengths, p_lengths, positives, pos_counts, attn, w_in, w_out, gains, biases, attn_mom, w_in_mom,
    w_out_mom, gain_mom, bias_mom, attn_err, w_in_err, w_out_err, attn_start, w_in_start, w_out_start,
):
    devices = lax.axis_size("dp") * lax.axis_size("outer")
    d, ff = w_in.shape[1:]
    xq = questions.reshape(-1, TOK, d)
    xp = passages.reshape(-1, TOK, d)
    nqu, npu = xq.shape[0], xp.shape[0]
    own = positives.shape[0]
    index = (lax.axis_index("dp") * lax.axis_size("outer") + lax.axis_index("outer")).astype(jnp.int32).reshape(1)
    lists = jnp.concatenate([positives, pos_counts[:, None]], axis=1)
    lists = lax.all_to_all(jnp.broadcast_to(lists[None], (devices,) + lists.shape), AXES, 0, 0).reshape(devices * own, -1)
    *saved, pooled, units = forward(devices, q_lengths, p_lengths, xq, xp, attn, w_in, w_out, gains, biases)
    units = lax.all_to_all(units, AXES, 0, 0)
    loss, gp = contrast(nqu, npu, index, units, lists, pooled)
    starts = [jnp.swapaxes(start, -1, -2) for start in (attn_start, w_in_start, w_out_start)]
    qgrad, pgrad, attn_m, in_m, out_m, left = backward(
        nqu, npu, gp, saved, attn, w_in, w_out, gains, attn_err, w_in_err, w_out_err, starts
    )
    left = sum_over(left)
    basis, right = right_factors(left, attn_m, in_m, out_m)
    right = sum_over(right)
    *new, norm = update(devices, basis, right, left, attn_m, in_m, out_m, attn, w_in, w_out, attn_mom, w_in_mom, w_out_mom)
    attn_new, w_in_new, w_out_new, attn_mom_new, w_in_mom_new, w_out_mom_new, attn_err_new, w_in_err_new, w_out_err_new = new
    grad_norm = norm[0, 0]
    clip = jnp.minimum(1.0, CLIP_NORM / grad_norm)
    vector = left[:, 10 * d + 2 * ff :].reshape(2, 12, d)
    gains_new, gain_mom_new = momentum_step(gains, gain_mom, vector[:, :2], clip)
    biases_new, bias_mom_new = momentum_step(biases, bias_mom, vector[:, 2:].reshape(biases.shape), clip)
    attn_factor = jnp.transpose(right[:, : 8 * d].reshape(8, 2, 4, d), (1, 2, 3, 0))
    w_in_factor = jnp.transpose(right[:, 8 * d : 8 * d + 2 * ff].reshape(8, 2, ff), (1, 2, 0))
    w_out_factor = jnp.transpose(right[:, 8 * d + 2 * ff :].reshape(8, 2, d), (1, 2, 0))
    return (
        loss[:, 0], qgrad.reshape(questions.shape), pgrad.reshape(passages.shape),
        attn_new, w_in_new, w_out_new, gains_new, biases_new,
        attn_mom_new, w_in_mom_new, w_out_mom_new, gain_mom_new, bias_mom_new,
        attn_err_new, w_in_err_new, w_out_err_new, attn_factor, w_in_factor, w_out_factor, grad_norm,
    )


def solution(mesh):
    split = ("dp", "outer")
    share = P(split)
    return jax.shard_map(
        per_device,
        mesh=mesh,
        in_specs=(share,) * 6 + (P(),) * 10 + (share,) * 3 + (P(),) * 3,
        out_specs=(share,) * 3 + (P(),) * 10 + (share,) * 3 + (P(),) * 4,
        check_vma=False,
    )
```

time: 753 us -> 203 us (0.27); the launches traced: 742 us -> 202 us
  waiting for transfers between devices: 314 us -> 31.6 us
  matrix products: 154 us -> 0 us
  Pallas kernels: 0 us -> 126 us
  blocking collectives: 111 us -> 0 us
  other arithmetic: 93.1 us -> 5.89 us
  local copies, waits for them, and re-layouts: 49.4 us -> 7.02 us
  starting transfers between devices: 0.12 us -> 30 us
  between operations: 20.3 us -> 1.54 us
    psum x2 -> x0, waiting for transfers between devices: 241 us -> none  [the longest x1 122 us: per_device(): lax.psum((right_attn, right_inner, right_outer), ('dp', 'outer'))]
    dot_general x60 -> x0, matrix products: 154 us -> none  [the longest x2 21.5 us: encoder_backward(): jnp.einsum('bhqk,bkhe->bqhe', grad_raw, key_heads, preferred_element_type...]
    pallas_call x0 -> x5, Pallas kernels: none -> 126 us  [the longest x1 52.4 us: backward(): pl.pallas_call(functools.partial(backward_kernel, nqu), grid=(units,), in...]
    reduce_scatter x1 -> x0, waiting for transfers between devices: 72.5 us -> none  [per_device(): lax.psum_scatter(partial_terms, ('dp', 'outer'), scatter_dimension=0, til...]
    all_gather x1 -> x0, blocking collectives: 70.7 us -> none  [per_device(): lax.all_gather(passage_unit, ('dp', 'outer'), axis=0, tiled=True)]
    psum x1 -> x0, blocking collectives: 40.3 us -> none  [per_device(): lax.psum((left_attn, left_inner, left_outer, gain_grad, shift_grad), ('dp...]
    convert_element_type x8 -> x0, other arithmetic: 28.3 us -> none  [the longest x2 23.8 us: encoder_forward(): active_low = jax.nn.gelu(upper_in, approximate=False).astype(jnp.bfloat16)]
    unnamed x322 -> x15, local copies, waits for them, and re-layouts: 28.3 us -> 0.74 us
  transfers between devices with their start and end apart: 3 -> 18, of which waited for: 3 -> 13; matrix products, arithmetic and copies ran while one was open for 8% -> 1% of each run, Pallas kernels for 0% -> 24%
where the time goes in v1:
time: 203 us; the launch traced here: 202 us
  Pallas kernels  126 us (62%)
  waiting for transfers between devices  31.6 us (16%)
  starting transfers between devices  30 us (15%)
  local copies, waits for them, and re-layouts  7.02 us (3%)
  other arithmetic  5.89 us (3%)
    pallas_call x1, Pallas kernels, backward(): pl.pallas_call(functools.partial(backward_kernel, nqu), grid=(units,), in...  52.4 us
    pallas_call x1, Pallas kernels, forward(): pl.pallas_call(functools.partial(forward_kernel, nqu), grid_spec=pltpu.Pr...  49 us
    ppermute x16, waiting for transfers between devices, swap_with(): lax.ppermute(x, axis, [(i, i ^ mask) for i in range(lax.axis_size(axis))])  21.6 us
    ppermute x16, starting transfers between devices, swap_with(): lax.ppermute(x, axis, [(i, i ^ mask) for i in range(lax.axis_size(axis))])  16.7 us
    pallas_call x1, Pallas kernels, update(): pl.pallas_call(functools.partial(update_kernel, replicas), grid=(8,), in_...  16.2 us
    all_to_all x1, waiting for transfers between devices, per_device(): units = lax.all_to_all(units, AXES, 0, 0)  10 us
    all_to_all x1, starting transfers between devices, per_device(): lax.all_to_all(jnp.broadcast_to(lists[None], (devices,) + lists.shape), A...  7.3 us
    all_to_all x1, starting transfers between devices, per_device(): units = lax.all_to_all(units, AXES, 0, 0)  6.02 us
  transfers between devices with their start and end apart: 18, of which 13 were waited for; matrix products, arithmetic and copies ran while one was open for 1% of the time, Pallas kernels for 24%

profile of v1, /device:TPU:0, one launch (start us, length us, event | category | flops | bytes accessed | tf_op | source)
XLA Modules:
  0.0 202.2 jit_solution(9518790654153364873)
XLA Ops:
  0.7 0.7 pad_add_fusion
  1.4 0.7 broadcast_in_dim.10
  2.1 7.3 %all-to-all-start.1 = ((s32[32,8,5]{2,1,0:T(8,128)}), s32[32,8,5]{2,1,0:T(8,128)S(1)}, u32[]{:S(2)}, u32[]{:S(2)}) async-start(s32[32,8,5]{2,1,0:T(8,128)} %broadcast_in_dim.10), calls=%async_computation.1 | async-start | bytes 262144 | tf_op jit(solution)/shard_map/all_to_all | solution.py:670
  9.4 1.3 reshape.74.gains
  10.7 49.0 %forward.1 = (bf16[10,272,256]{2,1,0:T(8,128)(2,1)}, bf16[10,512,256]{2,1,0:T(8,128)(2,1)}, bf16[10,256,256]{2,1,0:T(8,128)(2,1)}, bf16[10,4,256,256]{3,2,1,0:T(...) custom-call(s32[8]{0:T(128)} %qlen.1, s32[8]{0:T(128)} %plen.1, ...), custom_call_target="tpu_custom_call" | custom-call | tf_op jit(solution)/shard_map/forward/pallas_call | solution.py:250
  59.7 6.0 %all-to-all-start = ((bf16[32,16,256]{2,1,0:T(8,128)(2,1)}), bf16[32,16,256]{2,1,0:T(8,128)(2,1)S(1)}, u32[]{:S(2)}, u32[]{:S(2)}) async-start(bf16[32,16,256]{2,1,0:T(8,128)(2,1)} %get-tuple-element.54), calls=%async_computation | async-start | bytes 524288 | tf_op jit(solution)/shard_map/all_to_all | solution.py:672
  65.8 10.0 %all-to-all-done.units = bf16[32,16,256]{2,1,0:T(8,128)(2,1)S(1)} async-done(((bf16[32,16,256]{2,1,0:T(8,128)(2,1)}), bf16[32,16,256]{2,1,0:T(8,128)(2,1)S(1)}, u32[]{:S(2)}, u32[]{:S(2)}) %all-to-all-start) | async-done | bytes 262176 | tf_op jit(solution)/shard_map/all_to_all | solution.py:672
  75.8 0.7 copy-done
  76.5 2.8 %contrast.1 = (f32[8,128]{1,0:T(8,128)}, f32[10,8,256]{2,1,0:T(8,128)}) custom-call(s32[1]{0:T(128)} %bitcast.index, bf16[32,16,256]{2,1,0:T(8,128)(2,1)} %copy-done, s32[256,5]{1,0:T(8,128)} %bitcast.21, f32[16,256]{1,0:T(8,128)} %get-tuple-element.55.pooled), custom_call_target="tpu_custom_call" | custom-call | tf_op jit(solution)/shard_map/contrast/pallas_call | solution.py:329
  79.2 52.4 %backward.1 = (f32[2,256,256]{2,1,0:T(8,128)}, f32[8,256,256]{2,1,0:T(8,128)}, f32[2,4,256,256]{3,2,1,0:T(8,128)}, f32[2,256,1024]{2,1,0:T(8,128)}, f32[2,1024,256]{2,1,0:T(8,128)}, /*index=5*/f32[8,5376]{1,0:T(8,128)}) custom-call(f32[10,8,256]{2,1,0:T(8,128)} %get-tuple-element.57.gp, bf16[10,272,256]{2,1,0:T(8,128)(2,1)} %get-tuple-element.58.x_in, ...), custom_call_target="tpu_custom_call" | custom-call | tf_op jit(solution)/shard_map/backward/pallas_call | solution.py:484
  131.7 0.9 constant_dynamic-slice_fusion.1
  132.6 0.4 collective-permute-start
  133.0 0.9 collective-permute-done
  133.9 0.9 dynamic-slice_add_fusion
  134.8 1.0 collective-permute-start.3
  135.8 1.5 collective-permute-start.2
  137.3 1.0 collective-permute-start.1
  138.4 2.8 %collective-permute-done.3 = f32[8,2688]{1,0:T(8,128)S(1)} collective-permute-done((f32[8,2688]{1,0:T(8,128)S(1)}, f32[8,2688]{1,0:T(8,128)S(1)}, u32[]{:S(2)}, u32[]{:S(2)}) %collective-permute-start.3) | collective-permute-done | bytes 86048 | tf_op jit(solution)/shard_map/ppermute | solution.py:629
  141.2 0.9 collective-permute-done.2
  142.1 1.7 collective-permute-start.6
  143.9 0.6 collective-permute-start.5
  144.5 2.1 %collective-permute-start.4 = (f32[8,2688]{1,0:T(8,128)S(1)}, f32[8,2688]{1,0:T(8,128)S(1)}, u32[]{:S(2)}, u32[]{:S(2)}) collective-permute-start(f32[8,2688]{1,0:T(8,128)S(1)} %add_add_fusion.1), channel_id=1, source_target_pairs={{0,1},{1,0},{2,3},{3,2},{4,5},{5,4},{6,7},{7,6},{8,9},{9,8},{10,11... | collective-permute-start | bytes 258056 | tf_op jit(solution)/shard_map/ppermute | solution.py:629
  146.6 2.8 %collective-permute-done.6 = f32[8,2688]{1,0:T(8,128)S(1)} collective-permute-done((f32[8,2688]{1,0:T(8,128)S(1)}, f32[8,2688]{1,0:T(8,128)S(1)}, u32[]{:S(2)}, u32[]{:S(2)}) %collective-permute-start.6) | collective-permute-done | bytes 86048 | tf_op jit(solution)/shard_map/ppermute | solution.py:629
  149.4 3.1 %collective-permute-done.5 = f32[8,2688]{1,0:T(8,128)S(1)} collective-permute-done((f32[8,2688]{1,0:T(8,128)S(1)}, f32[8,2688]{1,0:T(8,128)S(1)}, u32[]{:S(2)}, u32[]{:S(2)}) %collective-permute-start.5) | collective-permute-done | bytes 86048 | tf_op jit(solution)/shard_map/ppermute | solution.py:629
  152.6 1.3 collective-permute-done.7
  153.9 0.7 pad_maximum_fusion.1.left
  154.6 5.6 %right.1 = (f32[8,4608]{1,0:T(8,128)}, f32[8,4608]{1,0:T(8,128)}) custom-call(f32[8,5376]{1,0:T(8,128)} %pad_maximum_fusion.1.left, f32[2,4,256,256]{3,2,1,0:T(8,128)} %get-tuple-element.73.attn_m, f32[2,256,1024]{2,1,0:T(8,128)} %get-tuple-element.74.in_m, f32[2,1024,256]{2,1,0:T(8,128)} %get-tuple-element.75.out_m), custom_call_target="tpu_custom_call" | custom-call | tf_op jit(solution)/shard_map/right/pallas_call | solution.py:553
  160.2 0.9 constant_dynamic-slice_fusion
  161.3 1.1 collective-permute-done.8
  162.4 0.9 dynamic-slice_add_fusion.1
  163.3 1.2 collective-permute-start.11
  164.5 1.3 collective-permute-start.10
  165.8 1.1 collective-permute-start.9
  166.8 2.3 %collective-permute-done.11 = f32[8,2304]{1,0:T(8,128)S(1)} collective-permute-done((f32[8,2304]{1,0:T(8,128)S(1)}, f32[8,2304]{1,0:T(8,128)S(1)}, u32[]{:S(2)}, u32[]{:S(2)}) %collective-permute-start.11) | collective-permute-done | bytes 73760 | tf_op jit(solution)/shard_map/ppermute | solution.py:629
  169.1 1.0 collective-permute-done.10
  170.2 1.7 collective-permute-start.14
  171.9 2.8 %collective-permute-start.12 = (f32[8,2304]{1,0:T(8,128)S(1)}, f32[8,2304]{1,0:T(8,128)S(1)}, u32[]{:S(2)}, u32[]{:S(2)}) collective-permute-start(f32[8,2304]{1,0:T(8,128)S(1)} %add_add_fusion.3), channel_id=1, source_target_pairs={{0,1},{1,0},{2,3},{3,2},{4,5},{5,4},{6,7},{7,6},{8,9},{9,8},{10,11... | collective-permute-start | bytes 221192 | tf_op jit(solution)/shard_map/ppermute | solution.py:629
  174.6 2.6 %collective-permute-done.14 = f32[8,2304]{1,0:T(8,128)S(1)} collective-permute-done((f32[8,2304]{1,0:T(8,128)S(1)}, f32[8,2304]{1,0:T(8,128)S(1)}, u32[]{:S(2)}, u32[]{:S(2)}) %collective-permute-start.14) | collective-permute-done | bytes 73760 | tf_op jit(solution)/shard_map/ppermute | solution.py:629
  177.2 2.2 %collective-permute-done.13 = f32[8,2304]{1,0:T(8,128)S(1)} collective-permute-done((f32[8,2304]{1,0:T(8,128)S(1)}, f32[8,2304]{1,0:T(8,128)S(1)}, u32[]{:S(2)}, u32[]{:S(2)}) %collective-permute-start.13) | collective-permute-done | bytes 73760 | tf_op jit(solution)/shard_map/ppermute | solution.py:629
  179.5 0.6 slice_reduce_fusion
  180.1 0.6 collective-permute-done.15
  180.8 0.7 pad_maximum_fusion.right
  181.4 0.7 fusion
  182.1 0.6 slice.38
  182.7 16.2 %update.1 = (f32[2,4,256,256]{3,2,1,0:T(8,128)}, f32[2,256,1024]{2,1,0:T(8,128)}, f32[2,1024,256]{2,1,0:T(8,128)}, f32[2,4,256,256]{3,2,1,0:T(8,128)}, f32[2,256...) custom-call(f32[8,4608]{1,0:T(8,128)} %get-tuple-element.76.basis, ...), custom_call_target="tpu_custom_call" | custom-call | tf_op jit(solution)/shard_map/update/pallas_call | solution.py:614
  198.9 1.2 slice.25
  200.9 0.6 multiply_subtract_fusion.1
  201.5 0.6 multiply_subtract_fusion
  (33 shorter events, 0.6 us)
Async XLA Ops:
  2.1 57.6 %all-to-all-start.1 = ((s32[32,8,5]{2,1,0:T(8,128)}), s32[32,8,5]{2,1,0:T(8,128)S(1)}, u32[]{:S(2)}, u32[]{:S(2)}) async-start(s32[32,8,5]{2,1,0:T(8,128)} %broadcast_in_dim.10), calls=%async_computation.1 | async-start | bytes 262144 | tf_op jit(solution)/shard_map/all_to_all | solution.py:670
  59.7 16.1 %copy-start.1 = (s32[32,8,5]{2,1,0:T(8,128)}, s32[32,8,5]{2,1,0:T(8,128)S(1)}, u32[]{:S(2)}) copy-start(s32[32,8,5]{2,1,0:T(8,128)S(1)} %all-to-all-done.1) | copy-start | bytes 15364
  59.7 16.0 %all-to-all-start = ((bf16[32,16,256]{2,1,0:T(8,128)(2,1)}), bf16[32,16,256]{2,1,0:T(8,128)(2,1)S(1)}, u32[]{:S(2)}, u32[]{:S(2)}) async-start(bf16[32,16,256]{2,1,0:T(8,128)(2,1)} %get-tuple-element.54), calls=%async_computation | async-start | bytes 524288 | tf_op jit(solution)/shard_map/all_to_all | solution.py:672
  75.8 0.7 copy-start
  132.6 1.3 collective-permute-start
  134.8 6.4 %collective-permute-start.3 = (f32[8,2688]{1,0:T(8,128)S(1)}, f32[8,2688]{1,0:T(8,128)S(1)}, u32[]{:S(2)}, u32[]{:S(2)}) collective-permute-start(f32[8,2688]{1,0:T(8,128)S(1)} %dynamic-slice_add_fusion), channel_id=1, source_target_pairs={{0,24},{4,28},{8,16},{12,20},{16,8},{20,12},{24,0},{28,4},{1,25},{... | collective-permute-start | bytes 258056 | tf_op jit(solution)/shard_map/ppermute | solution.py:629
  135.8 6.3 %collective-permute-start.2 = (f32[8,2688]{1,0:T(8,128)S(1)}, f32[8,2688]{1,0:T(8,128)S(1)}, u32[]{:S(2)}, u32[]{:S(2)}) collective-permute-start(f32[8,2688]{1,0:T(8,128)S(1)} %dynamic-slice_add_fusion), channel_id=1, source_target_pairs={{0,16},{4,20},{8,24},{12,28},{16,0},{20,4},{24,8},{28,12},{1,17},{... | collective-permute-start | bytes 258056 | tf_op jit(solution)/shard_map/ppermute | solution.py:629
  137.3 4.8 %collective-permute-start.1 = (f32[8,2688]{1,0:T(8,128)S(1)}, f32[8,2688]{1,0:T(8,128)S(1)}, u32[]{:S(2)}, u32[]{:S(2)}) collective-permute-start(f32[8,2688]{1,0:T(8,128)S(1)} %dynamic-slice_add_fusion), channel_id=1, source_target_pairs={{0,8},{4,12},{8,0},{12,4},{16,24},{20,28},{24,16},{28,20},{1,9},{5... | collective-permute-start | bytes 258056 | tf_op jit(solution)/shard_map/ppermute | solution.py:629
  142.1 7.3 %collective-permute-start.6 = (f32[8,2688]{1,0:T(8,128)S(1)}, f32[8,2688]{1,0:T(8,128)S(1)}, u32[]{:S(2)}, u32[]{:S(2)}) collective-permute-start(f32[8,2688]{1,0:T(8,128)S(1)} %add_add_fusion.1), channel_id=1, source_target_pairs={{0,3},{1,2},{2,1},{3,0},{4,7},{5,6},{6,5},{7,4},{8,11},{9,10},{10,... | collective-permute-start | bytes 258056 | tf_op jit(solution)/shard_map/ppermute | solution.py:629
  143.9 8.6 %collective-permute-start.5 = (f32[8,2688]{1,0:T(8,128)S(1)}, f32[8,2688]{1,0:T(8,128)S(1)}, u32[]{:S(2)}, u32[]{:S(2)}) collective-permute-start(f32[8,2688]{1,0:T(8,128)S(1)} %add_add_fusion.1), channel_id=1, source_target_pairs={{0,2},{1,3},{2,0},{3,1},{4,6},{5,7},{6,4},{7,5},{8,10},{9,11},{10,... | collective-permute-start | bytes 258056 | tf_op jit(solution)/shard_map/ppermute | solution.py:629
  144.5 8.0 %collective-permute-start.4 = (f32[8,2688]{1,0:T(8,128)S(1)}, f32[8,2688]{1,0:T(8,128)S(1)}, u32[]{:S(2)}, u32[]{:S(2)}) collective-permute-start(f32[8,2688]{1,0:T(8,128)S(1)} %add_add_fusion.1), channel_id=1, source_target_pairs={{0,1},{1,0},{2,3},{3,2},{4,5},{5,4},{6,7},{7,6},{8,9},{9,8},{10,11... | collective-permute-start | bytes 258056 | tf_op jit(solution)/shard_map/ppermute | solution.py:629
  152.5 1.3 collective-permute-start.7
  154.6 24.9 %copy-start.5 = (f32[8,128]{1,0:T(8,128)S(1)}, f32[8,128]{1,0:T(8,128)}, u32[]{:S(2)}) copy-start(f32[8,128]{1,0:T(8,128)} %get-tuple-element.56) | copy-start | bytes 12292
  161.1 1.3 collective-permute-start.8
  163.3 5.8 %collective-permute-start.11 = (f32[8,2304]{1,0:T(8,128)S(1)}, f32[8,2304]{1,0:T(8,128)S(1)}, u32[]{:S(2)}, u32[]{:S(2)}) collective-permute-start(f32[8,2304]{1,0:T(8,128)S(1)} %dynamic-slice_add_fusion.1), channel_id=1, source_target_pairs={{0,24},{4,28},{8,16},{12,20},{16,8},{20,12},{24,0},{28,4},{1,25},{... | collective-permute-start | bytes 221192 | tf_op jit(solution)/shard_map/ppermute | solution.py:629
  164.5 5.6 %collective-permute-start.10 = (f32[8,2304]{1,0:T(8,128)S(1)}, f32[8,2304]{1,0:T(8,128)S(1)}, u32[]{:S(2)}, u32[]{:S(2)}) collective-permute-start(f32[8,2304]{1,0:T(8,128)S(1)} %dynamic-slice_add_fusion.1), channel_id=1, source_target_pairs={{0,16},{4,20},{8,24},{12,28},{16,0},{20,4},{24,8},{28,12},{1,17},{... | collective-permute-start | bytes 221192 | tf_op jit(solution)/shard_map/ppermute | solution.py:629
  165.8 4.4 %collective-permute-start.9 = (f32[8,2304]{1,0:T(8,128)S(1)}, f32[8,2304]{1,0:T(8,128)S(1)}, u32[]{:S(2)}, u32[]{:S(2)}) collective-permute-start(f32[8,2304]{1,0:T(8,128)S(1)} %dynamic-slice_add_fusion.1), channel_id=1, source_target_pairs={{0,8},{4,12},{8,0},{12,4},{16,24},{20,28},{24,16},{28,20},{1,9},{5... | collective-permute-start | bytes 221192 | tf_op jit(solution)/shard_map/ppermute | solution.py:629
  170.2 7.1 %collective-permute-start.14 = (f32[8,2304]{1,0:T(8,128)S(1)}, f32[8,2304]{1,0:T(8,128)S(1)}, u32[]{:S(2)}, u32[]{:S(2)}) collective-permute-start(f32[8,2304]{1,0:T(8,128)S(1)} %add_add_fusion.3), channel_id=1, source_target_pairs={{0,3},{1,2},{2,1},{3,0},{4,7},{5,6},{6,5},{7,4},{8,11},{9,10},{10,... | collective-permute-start | bytes 221192 | tf_op jit(solution)/shard_map/ppermute | solution.py:629
  171.9 7.5 %collective-permute-start.13 = (f32[8,2304]{1,0:T(8,128)S(1)}, f32[8,2304]{1,0:T(8,128)S(1)}, u32[]{:S(2)}, u32[]{:S(2)}) collective-permute-start(f32[8,2304]{1,0:T(8,128)S(1)} %add_add_fusion.3), channel_id=1, source_target_pairs={{0,2},{1,3},{2,0},{3,1},{4,6},{5,7},{6,4},{7,5},{8,10},{9,11},{10,... | collective-permute-start | bytes 221192 | tf_op jit(solution)/shard_map/ppermute | solution.py:629
  171.9 7.5 %collective-permute-start.12 = (f32[8,2304]{1,0:T(8,128)S(1)}, f32[8,2304]{1,0:T(8,128)S(1)}, u32[]{:S(2)}, u32[]{:S(2)}) collective-permute-start(f32[8,2304]{1,0:T(8,128)S(1)} %add_add_fusion.3), channel_id=1, source_target_pairs={{0,1},{1,0},{2,3},{3,2},{4,5},{5,4},{6,7},{7,6},{8,9},{9,8},{10,11... | collective-permute-start | bytes 221192 | tf_op jit(solution)/shard_map/ppermute | solution.py:629
  179.4 1.3 collective-permute-start.15
  182.7 18.1 %copy-start.4 = (f32[2,2,256]{2,1,0:T(2,128)S(1)}, f32[2,2,256]{2,1,0:T(2,128)}, u32[]{:S(2)}) copy-start(f32[2,2,256]{2,1,0:T(2,128)} %param.31) | copy-start | bytes 12292
  182.7 18.2 %copy-start.6 = (f32[2,2,256]{2,1,0:T(2,128)S(1)}, f32[2,2,256]{2,1,0:T(2,128)}, u32[]{:S(2)}) copy-start(f32[2,2,256]{2,1,0:T(2,128)} %param.36) | copy-start | bytes 12292
  182.7 18.8 %copy-start.2 = (f32[2,2560]{1,0:T(2,128)S(1)}, f32[2,2560]{1,0:T(2,128)}, u32[]{:S(2)}) copy-start(f32[2,2560]{1,0:T(2,128)} %biases.1) | copy-start | bytes 61444
  182.7 18.8 %copy-start.3 = (f32[2,2560]{1,0:T(2,128)S(1)}, f32[2,2560]{1,0:T(2,128)}, u32[]{:S(2)}) copy-start(f32[2,2560]{1,0:T(2,128)} %param.37) | copy-start | bytes 61444

commit v2 on v1

v2 whole, which is shorter than its diff:
```python
import functools
import math

import jax
import jax.numpy as jnp
from jax import lax
from jax.experimental import pallas as pl
from jax.experimental.pallas import tpu as pltpu
from jax.sharding import PartitionSpec as P

HEAD = 64
TOK = 256
GROUP = 2
PART = 64
ONES = 16

NORM_EPSILON = 1e-06
UNIT_EPSILON = 1e-06
SCORE_SCALE = 20.0
MOMENTUM_DECAY = 0.9
LEARNING_RATE = 10.0
CLIP_NORM = 2.0
MASKED_SCORE = -1e30
HIGHEST = lax.Precision.HIGHEST
AXES = ("dp", "outer")
F32 = jnp.float32
BF16 = jnp.bfloat16
VMEM_LIMIT = 56 << 20
SEND = F32


def mm(a, b, precision=None):
    return lax.dot_general(a, b, (((1,), (0,)), ((), ())), precision=precision, preferred_element_type=F32)


def mm_nt(a, b, precision=None):
    return lax.dot_general(a, b, (((1,), (1,)), ((), ())), precision=precision, preferred_element_type=F32)


def mm_tn(a, b, precision=None):
    return lax.dot_general(a, b, (((0,), (0,)), ((), ())), precision=precision, preferred_element_type=F32)


def wide(column):
    return jnp.concatenate([column] * (GROUP * TOK // 128), axis=1)


def split_two(v):
    high = v.astype(BF16)
    return high, (v - high.astype(F32)).astype(BF16)


def split_three(v):
    high = v.astype(BF16)
    rest = v - high.astype(F32)
    middle = rest.astype(BF16)
    return high, middle, (rest - middle.astype(F32)).astype(BF16)


def norm_columns(hidden, gain, shift):
    share = 1.0 / hidden.shape[0]
    center = hidden - jnp.sum(hidden, axis=0, keepdims=True) * share
    inverse = lax.rsqrt(jnp.sum(center * center, axis=0, keepdims=True) * share + NORM_EPSILON)
    normed = center * inverse
    return normed * gain + shift, normed, inverse


def norm_columns_back(grad, normed, inverse, gain):
    share = 1.0 / grad.shape[0]
    scaled = grad * gain
    mean = jnp.sum(scaled, axis=0, keepdims=True) * share
    along = jnp.sum(scaled * normed, axis=0, keepdims=True) * share
    return inverse * (scaled - mean - normed * along)


def gelu_and_slope(u):
    d = 1.0 + (0.3275911 * 0.5**0.5) * jnp.abs(u)
    t = pl.reciprocal(d, approx=True)
    t = t * (2.0 - d * t)
    poly = t * (0.127414796 + t * (-0.142248368 + t * (0.7107068705 + t * (-0.7265760135 + t * 0.5307027145))))
    bell = jnp.exp2(u * u * (-0.5 * math.log2(math.e)))
    tail = poly * bell
    phi = jnp.where(u >= 0.0, 1.0 - tail, tail)
    return u * phi, phi + u * bell * (0.5 / math.pi) ** 0.5


def forward_kernel(
    nqs, qlen, plen, xq, xp, attn, w_in, w_out, gains, biases, lists, counts,
    x_out, qk_out, v_out, p_out, ctx_out, n1_out, first_out, slope_out, act_out, n2_out, inv_out, live_out, pooled_out, units_out,
    wproj, wo_t, win_t, wout_t, bias_bc, gain_bc, qblk, xs, away, score_s, turn,
):
    i = pl.program_id(0)
    last = pl.num_programs(0) - 1
    is_q = i < nqs
    t = jnp.where(is_q, 0, 1)
    d = xs.shape[1]
    ff = win_t.shape[0]
    heads = d // HEAD
    segs = TOK // HEAD
    span = GROUP * TOK

    @pl.when(i == 0)
    def _():
        qblk[...] = jnp.zeros_like(qblk)

    @pl.when((i == 0) | (i == nqs))
    def _():
        eye = (lax.broadcasted_iota(jnp.int32, (d, d), 0) == lax.broadcasted_iota(jnp.int32, (d, d), 1)).astype(F32).astype(BF16)
        for j in range(3):
            wproj[j * d : (j + 1) * d, :] = mm_nt(eye, attn[0, j].astype(BF16)).astype(BF16)
        wproj[3 * d : 4 * d, :] = eye
        wproj[4 * d : 5 * d, :] = attn[0, 1].astype(BF16)
        wproj[5 * d : 6 * d, :] = attn[0, 2].astype(BF16)
        wo_t[...] = mm_nt(eye, attn[0, 3].astype(BF16)).astype(BF16)
        for c in range(ff // d):
            at = slice(c * d, (c + 1) * d)
            win_t[at, :] = mm_nt(eye, w_in[0, :, at].astype(BF16)).astype(BF16)
            wout_t[:, at] = mm_nt(eye, w_out[0, at, :].astype(BF16)).astype(BF16)
        for c in range(bias_bc.shape[0] // d):
            row = biases[pl.ds(t, 1), c * d : (c + 1) * d]
            bias_bc[c * d : (c + 1) * d, :] = jnp.broadcast_to(row, (128, d)).T
        for c in range(2):
            row = gains[t, c : c + 1, :]
            gain_bc[c * d : (c + 1) * d, :] = jnp.broadcast_to(row, (128, d)).T

    @pl.when(is_q)
    def _():
        xs[...] = xq[...].reshape(span, d)

    @pl.when(jnp.logical_not(is_q))
    def _():
        xs[...] = xp[...].reshape(span, d)

    def length_of(u, segment):
        base = (jnp.minimum(i, nqs - 1) * GROUP + u) * segs
        out = jnp.full(segment.shape, qlen[base + segs - 1], jnp.int32)
        for s in range(segs - 1):
            out = jnp.where(segment == s, qlen[base + s], out)
        return jnp.where(is_q, out, plen[jnp.maximum(i - nqs, 0) * GROUP + u])

    key = lax.broadcasted_iota(jnp.int32, (TOK, TOK), 0)
    ask = lax.broadcasted_iota(jnp.int32, (TOK, TOK), 1)
    row = lax.broadcasted_iota(jnp.int32, (16, TOK), 0)
    token = lax.broadcasted_iota(jnp.int32, (16, TOK), 1)
    key_col = lax.broadcasted_iota(jnp.int32, (TOK, 1), 0)
    far = is_q & ((key // HEAD) != (ask // HEAD))
    owner = jnp.where(is_q, token // HEAD, 0)
    place = jnp.where(is_q, token % HEAD, token)
    seg_row = lax.broadcasted_iota(jnp.int32, (16, 1), 0)
    for u in range(GROUP):
        dead = jnp.where(is_q, key_col % HEAD, key_col) >= length_of(u, key_col // HEAD)
        away[u] = jnp.where(far | dead, MASKED_SCORE, 0.0)
        live = ((place < length_of(u, token // HEAD)) & (row == owner)).astype(F32)
        live_out[0, :, u * TOK : (u + 1) * TOK] = live.astype(BF16)

    def bias(at, size):
        return wide(bias_bc[at : at + size, :])

    x = xs[...]
    q_t = (mm_nt(wproj[0:d, :], x) + bias(0, d)).astype(BF16)
    qk_out[0, 0:d, :] = q_t
    for u in range(GROUP):
        for h in range(heads):
            piece = q_t[h * HEAD : (h + 1) * HEAD, u * TOK : (u + 1) * TOK]
            qblk[u, h * HEAD : (h + 1) * HEAD, h * TOK : (h + 1) * TOK] = piece * BF16(HEAD**-0.5)
    k_row = mm(x, wproj[4 * d : 5 * d, :]).astype(BF16)
    for u in range(GROUP):
        for h in range(heads):
            score_s[u, h] = mm(k_row[u * TOK : (u + 1) * TOK, :], qblk[u, :, h * TOK : (h + 1) * TOK])
    v_t = (mm_nt(wproj[2 * d : 3 * d, :], x) + bias(d, d)).astype(BF16)
    qk_out[0, d : 2 * d, :] = mm_nt(wproj[d : 2 * d, :], x).astype(BF16)
    v_out[0] = (mm(x, wproj[5 * d : 6 * d, :]) + biases[pl.ds(t, 1), d : 2 * d]).astype(BF16)
    x_t = mm_nt(wproj[3 * d : 4 * d, :], x)
    x_out[0, 0:d, :] = x_t.astype(BF16)
    for u in range(GROUP):
        for h in range(heads):
            scores = score_s[u, h] + away[u]
            exponent = jnp.exp(scores - jnp.max(scores, axis=0, keepdims=True))
            probs = exponent * (1.0 / jnp.sum(exponent, axis=0, keepdims=True))
            p_out[0, u, h] = probs.astype(BF16)
    for u in range(GROUP):
        for h in range(heads):
            at = slice(h * HEAD, (h + 1) * HEAD)
            over = slice(u * TOK, (u + 1) * TOK)
            ctx_out[0, at, over] = mm(v_t[at, over], p_out[0, u, h]).astype(BF16)
    hidden = x_t + (mm(wo_t[...], ctx_out[0, 0:d, :]) + bias(2 * d, d))
    first, n1, inv1 = norm_columns(hidden, wide(gain_bc[0:d, :]), bias(3 * d, d))
    n1_out[0] = n1
    first_low = first.astype(BF16)
    first_out[0, 0:d, :] = first_low
    hidden = first + bias(4 * d, d)
    for c in range(ff // d):
        at = slice(c * d, (c + 1) * d)
        upper = mm(win_t[at, :], first_low) + bias(6 * d + c * d, d)
        active, slope = gelu_and_slope(upper)
        slope_out[0, at, :] = slope
        active_low = active.astype(BF16)
        act_out[0, at, :] = active_low
        hidden = hidden + mm(wout_t[:, at], active_low)
    second, n2, inv2 = norm_columns(hidden, wide(gain_bc[d : 2 * d, :]), bias(5 * d, d))
    n2_out[0] = n2
    which = lax.broadcasted_iota(jnp.int32, (8, span), 0)
    inv_out[0] = jnp.where(which == 0, inv1, inv2)
    second_high, second_low = split_two(second)
    ones = jnp.ones((ONES, span), BF16)
    x_out[0, d:, :] = ones
    ctx_out[0, d:, :] = ones
    first_out[0, d:, :] = ones
    act_out[0, ff:, :] = ones
    for u in range(GROUP):
        over = slice(u * TOK, (u + 1) * TOK)
        live = live_out[0, :, over]
        pooled = mm_nt(live, second_high[:, over]) + mm_nt(live, second_low[:, over])
        pooled = pooled / length_of(u, seg_row).astype(F32)

        @pl.when(is_q)
        def _(pooled=pooled, u=u):
            for s in range(segs):
                pooled_out[pl.ds((i * GROUP + u) * segs + s, 1), :] = pooled[s : s + 1, :]

        @pl.when(jnp.logical_not(is_q))
        def _(pooled=pooled, u=u):
            pooled_out[pl.ds(nqs * GROUP * segs + (i - nqs) * GROUP + u, 1), :] = pooled[0:1, :]

    @pl.when(i == last)
    def _():
        rows = pooled_out[...]
        unit = rows * lax.rsqrt(jnp.sum(rows * rows, axis=1, keepdims=True) + UNIT_EPSILON)
        slots, own = lists.shape
        turn[...] = jnp.zeros_like(turn)
        turn[0:slots, 0:own] = (lists[...] // PART).astype(F32)
        turn[slots : 2 * slots, 0:own] = (lists[...] % PART).astype(F32)
        turn[2 * slots : 2 * slots + 1, 0:own] = counts[...].astype(F32)
        extra = turn[...].T[0:own, :]
        sent = jnp.concatenate([unit[:, c * 128 : (c + 1) * 128] for c in range(d // 128)] + [extra], axis=0)
        units_out[...] = jnp.broadcast_to(sent.astype(BF16)[None], units_out.shape)


def step_spec(*shape):
    return pl.BlockSpec((1,) + shape, lambda i, *_: (i,) + (0,) * len(shape))


def tower_spec(nqs, *shape):
    return pl.BlockSpec((1,) + shape, lambda i, *_: (jnp.where(i < nqs, 0, 1),) + (0,) * len(shape))


def whole_spec(*shape):
    return pl.BlockSpec(shape, lambda i, *_: (0,) * len(shape))


def forward(devices, q_lengths, p_lengths, xq, xp, attn, w_in, w_out, gains, biases, positives, counts):
    nqs, nps = xq.shape[0] // GROUP, xp.shape[0] // GROUP
    steps = nqs + nps
    span = GROUP * TOK
    d, ff = w_in.shape[1:]
    heads = d // HEAD
    seqs = q_lengths.shape[0] + xp.shape[0]
    sent = seqs * d // 128 + positives.shape[1]
    outs = [
        ((d + ONES, span), BF16),
        ((2 * d, span), BF16),
        ((span, d), BF16),
        ((GROUP, heads, TOK, TOK), BF16),
        ((d + ONES, span), BF16),
        ((d, span), F32),
        ((d + ONES, span), BF16),
        ((ff, span), F32),
        ((ff + ONES, span), BF16),
        ((d, span), F32),
        ((8, span), F32),
        ((16, span), BF16),
    ]
    return pl.pallas_call(
        functools.partial(forward_kernel, nqs),
        grid_spec=pltpu.PrefetchScalarGridSpec(
            num_scalar_prefetch=2,
            grid=(steps,),
            in_specs=[
                pl.BlockSpec((GROUP, TOK, d), lambda i, *_: (jnp.minimum(i, nqs - 1), 0, 0)),
                pl.BlockSpec((GROUP, TOK, d), lambda i, *_: (jnp.maximum(i - nqs, 0), 0, 0)),
                tower_spec(nqs, 4, d, d),
                tower_spec(nqs, d, ff),
                tower_spec(nqs, ff, d),
                whole_spec(2, 2, d),
                whole_spec(2, biases.shape[1]),
                whole_spec(*positives.shape),
                whole_spec(1, positives.shape[1]),
            ],
            out_specs=[step_spec(*shape) for shape, _ in outs] + [whole_spec(seqs, d), whole_spec(devices, sent, 128)],
            scratch_shapes=[
                pltpu.VMEM((6 * d, d), BF16),
                pltpu.VMEM((d, d), BF16),
                pltpu.VMEM((ff, d), BF16),
                pltpu.VMEM((d, ff), BF16),
                pltpu.VMEM((biases.shape[1], 128), F32),
                pltpu.VMEM((2 * d, 128), F32),
                pltpu.VMEM((GROUP, d, heads * TOK), BF16),
                pltpu.VMEM((span, d), BF16),
                pltpu.VMEM((GROUP, TOK, TOK), F32),
                pltpu.VMEM((GROUP, heads, TOK, TOK), F32),
                pltpu.VMEM((128, 128), F32),
            ],
        ),
        out_shape=[jax.ShapeDtypeStruct((steps,) + shape, kind) for shape, kind in outs]
        + [jax.ShapeDtypeStruct((seqs, d), F32), jax.ShapeDtypeStruct((devices, sent, 128), BF16)],
        compiler_params=pltpu.CompilerParams(vmem_limit_bytes=VMEM_LIMIT),
        name="forward",
    )(q_lengths, p_lengths, xq, xp, attn, w_in, w_out, gains, biases, positives, counts)


def contrast_kernel(nqu, slots, index, qlen, plen, units, pooled, loss_out, gp_out, low_rows, gup_rows, gp_rows, turn):
    devices = units.shape[0]
    seqs, d = pooled.shape
    own = qlen.shape[0]
    mine = pl.multiple_of(index[0] * own, own)
    pown = seqs - own
    pmine = pl.multiple_of(index[0] * pown, pown)
    both = units[...].astype(F32)
    parts = range(0, seqs * d // 128, seqs)
    uq = jnp.concatenate([both[:, at : at + own, :] for at in parts], axis=2).reshape(devices * own, d).astype(BF16)
    up = jnp.concatenate([both[:, at + own : at + seqs, :] for at in parts], axis=2).reshape(devices * pown, d).astype(BF16)
    lists = both[:, seqs * d // 128 :, :].reshape(devices * own, 128)
    scores = SCORE_SCALE * mm_nt(uq, up)
    columns = lax.broadcasted_iota(jnp.int32, scores.shape, 1).astype(F32)
    positive = None
    for k in range(slots):
        listed = lists[:, k : k + 1] * PART + lists[:, slots + k : slots + k + 1]
        hit = (listed == columns) & (lists[:, 2 * slots : 2 * slots + 1] > k)
        positive = hit if positive is None else positive | hit
    highest = jnp.max(scores, axis=1, keepdims=True)
    whole = highest + jnp.log(jnp.sum(jnp.exp(scores - highest), axis=1, keepdims=True))
    chosen = jnp.where(positive, scores, MASKED_SCORE)
    top = jnp.max(chosen, axis=1, keepdims=True)
    within = top + jnp.log(jnp.sum(jnp.exp(chosen - top), axis=1, keepdims=True))
    low = (SCORE_SCALE * (jnp.exp(scores - whole) - jnp.exp(chosen - within))).astype(BF16)
    low_rows[:, : scores.shape[1]] = low.astype(F32)
    low_rows[:, scores.shape[1] :] = jnp.broadcast_to(whole - within, (scores.shape[0], 128))
    turn[...] = jnp.zeros_like(turn)
    turn[0:own, :] = low_rows[pl.ds(mine, own), scores.shape[1] :]
    loss_out[...] = turn[...].T[0:1, 0:own]
    grad_q = mm(low_rows[pl.ds(mine, own), : scores.shape[1]].astype(BF16), up)
    gup_rows[...] = mm_tn(low, uq)
    grad_p = gup_rows[pl.ds(pmine, pown), :]
    grad = jnp.concatenate([grad_q, grad_p], axis=0)
    rows = pooled[...]
    inverse = lax.rsqrt(jnp.sum(rows * rows, axis=1, keepdims=True) + UNIT_EPSILON)
    grad = inverse * grad - inverse * inverse * inverse * rows * jnp.sum(rows * grad, axis=1, keepdims=True)
    segs = own // nqu
    gp_rows[...] = jnp.zeros_like(gp_rows)
    for s in range(own):
        gp_rows[s // segs, s % segs : s % segs + 1, :] = grad[s : s + 1, :] / jnp.full((1, d), qlen[s], jnp.int32).astype(F32)
    for s in range(pown):
        gp_rows[nqu + s, 0:1, :] = grad[own + s : own + s + 1, :] / jnp.full((1, d), plen[s], jnp.int32).astype(F32)
    for term, value in enumerate(split_three(gp_rows[...])):
        gp_out[:, term * 16 : (term + 1) * 16, :] = value


def contrast(nqu, npu, slots, index, q_lengths, p_lengths, units, pooled):
    devices = units.shape[0]
    seqs, d = pooled.shape
    own = q_lengths.shape[0]
    passages = devices * (seqs - own)
    vmem = pl.BlockSpec(memory_space=pltpu.VMEM)
    return pl.pallas_call(
        functools.partial(contrast_kernel, nqu, slots),
        in_specs=[pl.BlockSpec(memory_space=pltpu.SMEM)] * 3 + [vmem, vmem],
        out_specs=[vmem, vmem],
        out_shape=[jax.ShapeDtypeStruct((1, own), F32), jax.ShapeDtypeStruct((nqu + npu, 48, d), BF16)],
        scratch_shapes=[
            pltpu.VMEM((devices * own, passages + 128), F32),
            pltpu.VMEM((passages, d), F32),
            pltpu.VMEM((nqu + npu, 16, d), F32),
            pltpu.VMEM((128, 128), F32),
        ],
        compiler_params=pltpu.CompilerParams(vmem_limit_bytes=VMEM_LIMIT),
        name="contrast",
    )(index, q_lengths, p_lengths, units, pooled)


def left_rows(start_t, matrix):
    s_high, s_low = split_two(start_t)
    m_high, m_low = split_two(matrix)
    both = mm_nt(jnp.concatenate([s_high, s_low], axis=0), m_high)
    return both[:8] + both[8:] + mm_nt(jnp.concatenate([s_high, s_high], axis=0), m_low)[:8]


def right_rows(basis, matrix):
    b_high, b_low = split_two(basis)
    m_high, m_low = split_two(matrix)
    both = mm(jnp.concatenate([b_high, b_low], axis=0), m_high)
    return both[:8] + both[8:] + mm(jnp.concatenate([b_high, b_high], axis=0), m_low)[:8]


def core_of(index, outer):
    return (index[0] // outer) % 2


def part_halves(core, whole, mine, other):
    half = whole.shape[1] // 2
    for c in range(2):

        @pl.when(core == c)
        def _(c=c):
            mine[...] = whole[:, c * half : (c + 1) * half]
            other[...] = whole[:, (1 - c) * half : (2 - c) * half]


def join_halves(core, whole, mine, other):
    half = whole.shape[1] // 2
    for c in range(2):

        @pl.when(core == c)
        def _(c=c):
            whole[:, c * half : (c + 1) * half] = mine[...]
            whole[:, (1 - c) * half : (2 - c) * half] = other[...]


def backward_kernel(
    nqs, outer, index, gp, x_in, qk_in, v_in, p_in, ctx_in, n1_in, first_in, slope_in, act_in, n2_in, inv_in, live_in,
    attn, w_in, w_out, gains, attn_err, in_err, out_err, attn_start, in_start, out_start,
    qgrad, pgrad, attn_m, in_m, out_m, left_mine, left_other,
    left, wqkv, wo, win, wout, gain_bc, gz, gp_s, graw_s, gqkv, acc_qkv, acc_o, acc_in, acc_out, acc_gain,
):
    i = pl.program_id(0)
    last = pl.num_programs(0) - 1
    is_q = i < nqs
    t = jnp.where(is_q, 0, 1)
    d = wo.shape[0]
    ff = wout.shape[0]
    heads = d // HEAD
    span = GROUP * TOK

    @pl.when(i == 0)
    def _():
        gz[...] = jnp.zeros_like(gz)

    @pl.when((i == 0) | (i == nqs))
    def _():
        for j in range(3):
            wqkv[:, j * d : (j + 1) * d] = attn[0, j].astype(BF16)
        wo[...] = attn[0, 3].astype(BF16)
        win[...] = w_in[0].astype(BF16)
        wout[...] = w_out[0].astype(BF16)
        for c in range(2):
            row = gains[t, c : c + 1, :]
            gain_bc[c * d : (c + 1) * d, :] = jnp.broadcast_to(row, (128, d)).T
        acc_qkv[...] = jnp.zeros_like(acc_qkv)
        acc_o[...] = jnp.zeros_like(acc_o)
        acc_in[...] = jnp.zeros_like(acc_in)
        acc_out[...] = jnp.zeros_like(acc_out)
        acc_gain[...] = jnp.zeros_like(acc_gain)

    def add_gain(at, value):
        total = value[:, :128]
        for c in range(1, span // 128):
            total = total + value[:, c * 128 : (c + 1) * 128]
        acc_gain[at * d : (at + 1) * d, :] += total

    pieces = []
    for u in range(GROUP):
        live = live_in[0, :, u * TOK : (u + 1) * TOK]
        pieces.append(mm_tn(gp[u], jnp.concatenate([live, live, live], axis=0)))
    grad_second = jnp.concatenate(pieces, axis=1)
    n2 = n2_in[0]
    grad_two = norm_columns_back(grad_second, n2, inv_in[0, 1:2, :], wide(gain_bc[d : 2 * d, :]))
    down_low = grad_two.astype(BF16)
    grad_first = grad_two
    for c in range(ff // d):
        at = slice(c * d, (c + 1) * d)
        up_low = (mm(wout[at, :], down_low) * slope_in[0, at, :]).astype(BF16)
        acc_in[:, at] += mm_nt(first_in[0], up_low)
        grad_first = grad_first + mm(win[:, at], up_low)
    add_gain(1, grad_second * n2)
    add_gain(3, grad_second)
    n1 = n1_in[0]
    grad_one = norm_columns_back(grad_first, n1, inv_in[0, 0:1, :], wide(gain_bc[0:d, :]))
    branch_low = grad_one.astype(BF16)
    grad_context = mm(wo[...], branch_low).astype(BF16)
    for u in range(GROUP):
        for h in range(heads):
            at = slice(h * HEAD, (h + 1) * HEAD)
            gz[u, at, h * TOK : (h + 1) * TOK] = grad_context[at, u * TOK : (u + 1) * TOK]
    for u in range(GROUP):
        for h in range(heads):
            gp_s[u, h] = mm(v_in[0, u * TOK : (u + 1) * TOK, :], gz[u, :, h * TOK : (h + 1) * TOK])
    acc_out[...] += mm_nt(act_in[0], down_low)
    add_gain(0, grad_first * n1)
    add_gain(2, grad_first)
    acc_o[...] += mm_nt(ctx_in[0], branch_low)
    for u in range(GROUP):
        for h in range(heads):
            probs = p_in[0, u, h].astype(F32)
            grad_probs = gp_s[u, h]
            inner = jnp.sum(grad_probs * probs, axis=0, keepdims=True)
            graw_s[u, h] = (probs * (grad_probs - inner) * HEAD**-0.5).astype(BF16)
    for u in range(GROUP):
        over = slice(u * TOK, (u + 1) * TOK)
        for h in range(heads):
            at = slice(h * HEAD, (h + 1) * HEAD)
            later = slice(d + h * HEAD, d + (h + 1) * HEAD)
            last_at = slice(2 * d + h * HEAD, 2 * d + (h + 1) * HEAD)
            gqkv[last_at, over] = mm_nt(grad_context[at, over], p_in[0, u, h]).astype(BF16)
            gqkv[at, over] = mm(qk_in[0, later, over], graw_s[u, h]).astype(BF16)
            gqkv[later, over] = mm_nt(qk_in[0, at, over], graw_s[u, h]).astype(BF16)
    acc_qkv[...] += mm_nt(x_in[0], gqkv[...])
    result = (grad_one + mm(wqkv[...], gqkv[...])).T.reshape(GROUP, TOK, d)

    @pl.when(is_q)
    def _():
        qgrad[...] = result

    @pl.when(jnp.logical_not(is_q))
    def _():
        pgrad[...] = result

    @pl.when((i == nqs - 1) | (i == last))
    def _():
        base_in = 8 * d
        base_out = base_in + 2 * d
        base_vec = base_out + 2 * ff
        for j in range(4):
            grad = acc_o[0:d, :] if j == 3 else acc_qkv[0:d, j * d : (j + 1) * d]
            merged = grad + attn_err[0, 0, j]
            attn_m[0, j] = merged
            left[:, pl.ds(pl.multiple_of((t * 4 + j) * d, 128), d)] = left_rows(attn_start[0, j], merged)
        merged = acc_in[0:d, :] + in_err[0, 0]
        in_m[0] = merged
        left[:, pl.ds(pl.multiple_of(base_in + t * d, 128), d)] = left_rows(in_start[0], merged)
        merged = acc_out[0:ff, :] + out_err[0, 0]
        out_m[0] = merged
        left[:, pl.ds(pl.multiple_of(base_out + t * ff, 128), ff)] = left_rows(out_start[0], merged)
        sums = mm_nt(jnp.ones((8, 128), F32), acc_gain[...], HIGHEST)

        def vectors():
            yield sums[0:1, 0:d]
            yield sums[0:1, d : 2 * d]
            yield acc_qkv[d : d + 1, 0:d]
            yield acc_qkv[d : d + 1, 2 * d : 3 * d]
            yield acc_o[d : d + 1, :]
            yield sums[0:1, 2 * d : 3 * d]
            yield acc_out[ff : ff + 1, :]
            yield sums[0:1, 3 * d : 4 * d]
            for c in range(ff // d):
                yield acc_in[d : d + 1, c * d : (c + 1) * d]

        for tower in range(2):

            @pl.when(t == tower)
            def _(tower=tower):
                for v, vector in enumerate(vectors()):
                    at = tower * 12 + v
                    left[at // 3 : at // 3 + 1, base_vec + (at % 3) * d : base_vec + (at % 3 + 1) * d] = vector

    @pl.when(i == last)
    def _():
        part_halves(core_of(index, outer), left, left_mine, left_other)


def backward(nqs, nps, outer, index, gp, saved, attn, w_in, w_out, gains, attn_err, in_err, out_err, starts):
    steps = nqs + nps
    nqu, npu = nqs * GROUP, nps * GROUP
    span = GROUP * TOK
    d, ff = w_in.shape[1:]
    heads = d // HEAD
    width = 8 * d + 2 * d + 2 * ff + 3 * d
    tower = functools.partial(tower_spec, nqs)

    def error_spec(*shape):
        return pl.BlockSpec((1, 1) + shape, lambda i: (0, jnp.where(i < nqs, 0, 1)) + (0,) * len(shape))

    return pl.pallas_call(
        functools.partial(backward_kernel, nqs, outer),
        grid=(steps,),
        in_specs=[pl.BlockSpec(memory_space=pltpu.SMEM), pl.BlockSpec((GROUP, 48, d), lambda i: (i, 0, 0))]
        + [step_spec(*array.shape[1:]) for array in saved]
        + [tower(4, d, d), tower(d, ff), tower(ff, d), whole_spec(2, 2, d)]
        + [error_spec(4, d, d), error_spec(d, ff), error_spec(ff, d)]
        + [tower(4, 8, d), tower(8, ff), tower(8, d)],
        out_specs=[
            pl.BlockSpec((GROUP, TOK, d), lambda i: (jnp.minimum(i, nqs - 1), 0, 0)),
            pl.BlockSpec((GROUP, TOK, d), lambda i: (jnp.maximum(i - nqs, 0), 0, 0)),
            tower(4, d, d),
            tower(d, ff),
            tower(ff, d),
            whole_spec(8, width // 2),
            whole_spec(8, width // 2),
        ],
        out_shape=[
            jax.ShapeDtypeStruct((nqu, TOK, d), F32),
            jax.ShapeDtypeStruct((npu, TOK, d), F32),
            jax.ShapeDtypeStruct((2, 4, d, d), F32),
            jax.ShapeDtypeStruct((2, d, ff), F32),
            jax.ShapeDtypeStruct((2, ff, d), F32),
            jax.ShapeDtypeStruct((8, width // 2), F32),
            jax.ShapeDtypeStruct((8, width // 2), F32),
        ],
        scratch_shapes=[
            pltpu.VMEM((8, width), F32),
            pltpu.VMEM((d, 3 * d), BF16),
            pltpu.VMEM((d, d), BF16),
            pltpu.VMEM((d, ff), BF16),
            pltpu.VMEM((ff, d), BF16),
            pltpu.VMEM((2 * d, 128), F32),
            pltpu.VMEM((GROUP, d, heads * TOK), BF16),
            pltpu.VMEM((GROUP, heads, TOK, TOK), F32),
            pltpu.VMEM((GROUP, heads, TOK, TOK), BF16),
            pltpu.VMEM((3 * d, span), BF16),
            pltpu.VMEM((d + ONES, 3 * d), F32),
            pltpu.VMEM((d + ONES, d), F32),
            pltpu.VMEM((d + ONES, ff), F32),
            pltpu.VMEM((ff + ONES, d), F32),
            pltpu.VMEM((4 * d, 128), F32),
        ],
        compiler_params=pltpu.CompilerParams(vmem_limit_bytes=VMEM_LIMIT),
        name="backward",
    )(index, gp, *saved, attn, w_in, w_out, gains, attn_err, in_err, out_err, *starts)


def right_kernel(outer, index, left_mine, left_other, attn_m, in_m, out_m, basis, right_mine, right_other, vector, left, right):
    d, ff = in_m.shape[1:]
    core = core_of(index, outer)
    join_halves(core, left, left_mine, left_other)
    vector[...] = left[:, 10 * d + 2 * ff :]
    places = [(j * d, d) for j in range(8)] + [(8 * d + t * d, d) for t in range(2)] + [(10 * d + t * ff, ff) for t in range(2)]
    blocks = [left[:, at : at + size] for at, size in places]
    for j in range(8):
        for b, block in enumerate(blocks):
            order = lax.broadcasted_iota(jnp.int32, (8, 1), 0)
            column = block[j : j + 1, :]
            dots = jnp.sum(block * column, axis=1, keepdims=True)
            scale = lax.rsqrt(dots[j : j + 1, :] + 1e-06)
            unit = column * scale
            step = jnp.where(order > j, dots * scale, 0.0)
            blocks[b] = jnp.where(order == j, unit, block - step * unit)
    for (at, size), block in zip(places, blocks):
        basis[:, at : at + size] = block
    for j in range(8):
        right[:, j * d : (j + 1) * d] = right_rows(blocks[j], attn_m[j // 4, j % 4])
    for t in range(2):
        right[:, 8 * d + t * ff : 8 * d + (t + 1) * ff] = right_rows(blocks[8 + t], in_m[t])
        right[:, 8 * d + 2 * ff + t * d : 8 * d + 2 * ff + (t + 1) * d] = right_rows(blocks[10 + t], out_m[t])
    part_halves(core, right, right_mine, right_other)


def right_factors(outer, index, left_mine, left_other, attn_m, in_m, out_m):
    d, ff = in_m.shape[1:]
    vmem = pl.BlockSpec(memory_space=pltpu.VMEM)
    width = 10 * d + 2 * ff
    rows = functools.partial(jax.ShapeDtypeStruct, dtype=F32)
    return pl.pallas_call(
        functools.partial(right_kernel, outer),
        in_specs=[pl.BlockSpec(memory_space=pltpu.SMEM)] + [vmem] * 5,
        out_specs=[vmem] * 4,
        out_shape=[rows((8, width)), rows((8, width // 2)), rows((8, width // 2)), rows((8, 3 * d))],
        scratch_shapes=[pltpu.VMEM((8, width + 3 * d), F32), pltpu.VMEM((8, width), F32)],
        compiler_params=pltpu.CompilerParams(vmem_limit_bytes=VMEM_LIMIT),
        name="right",
    )(index, left_mine, left_other, attn_m, in_m, out_m)


def update_kernel(
    replicas, outer, index, basis, right_mine, right_other, vector, gains, biases, gain_mom, bias_mom,
    attn_m, in_m, out_m, attn, w_in, w_out, attn_mom, in_mom, out_mom,
    attn_new, in_new, out_new, attn_mom_new, in_mom_new, out_mom_new, attn_err, in_err, out_err,
    gains_new, biases_new, gain_mom_new, bias_mom_new, attn_factor, in_factor, out_factor, norm_out,
    right, clip_s,
):
    i = pl.program_id(0)
    d = attn.shape[2]
    ff = (right.shape[1] - 10 * d) // 2
    t, c = i // 4, i % 4

    @pl.when(i == 0)
    def _():
        join_halves(core_of(index, outer), right, right_mine, right_other)
        for j in range(8):
            attn_factor[j // 4, j % 4] = right[:, j * d : (j + 1) * d]
        for s in range(2):
            in_factor[s] = right[:, 8 * d + s * ff : 8 * d + (s + 1) * ff]
            out_factor[s] = right[:, 8 * d + 2 * ff + s * d : 8 * d + 2 * ff + (s + 1) * d]
        places = [((j * d, d), (j * d, d)) for j in range(8)]
        places += [((8 * d + s * d, d), (8 * d + s * ff, ff)) for s in range(2)]
        places += [((10 * d + s * ff, ff), (8 * d + 2 * ff + s * d, d)) for s in range(2)]
        total = jnp.zeros((8, 8), F32)
        for (b_at, b_size), (r_at, r_size) in places:
            b = basis[:, b_at : b_at + b_size]
            r = right[:, r_at : r_at + r_size]
            total = total + mm_nt(b, b, HIGHEST) * mm_nt(r, r, HIGHEST)
        sums = vector[...]
        square = jnp.sum(jnp.sum(total, axis=1, keepdims=True), axis=0, keepdims=True)
        square = square + jnp.sum(jnp.sum(sums * sums, axis=1, keepdims=True), axis=0, keepdims=True)
        norm = jnp.sqrt(jnp.broadcast_to(square, (8, 128)))
        norm_out[0] = norm[0, 0]
        clip_s[...] = jnp.minimum(1.0, CLIP_NORM / norm)
        held = clip_s[0:1, 0:1]
        for s in range(2):
            for v in range(12):
                at = s * 12 + v
                reduced = vector[at // 3 : at // 3 + 1, (at % 3) * d : (at % 3 + 1) * d]
                if v < 2:
                    moved = MOMENTUM_DECAY * gain_mom[s, v : v + 1, :] + held * reduced
                    gain_mom_new[s, v : v + 1, :] = moved
                    gains_new[s, v : v + 1, :] = gains[s, v : v + 1, :] - LEARNING_RATE * moved
                else:
                    over = slice((v - 2) * d, (v - 1) * d)
                    moved = MOMENTUM_DECAY * bias_mom[s : s + 1, over] + held * reduced
                    bias_mom_new[s : s + 1, over] = moved
                    biases_new[s : s + 1, over] = biases[s : s + 1, over] - LEARNING_RATE * moved

    clip = clip_s[0:1, 0:1]

    def step(b_at, r_at, merged, weight, moment, weight_new, moment_new, error):
        b1, b2, b3 = split_three(basis[:, pl.ds(pl.multiple_of(b_at, 128), d)])
        r1, r2, r3 = split_three(right[:, pl.ds(pl.multiple_of(r_at, 128), d)])
        approx = mm_tn(jnp.concatenate([b1, b1, b2, b1, b2, b3], axis=0), jnp.concatenate([r1, r2, r1, r3, r2, r1], axis=0))
        moved = MOMENTUM_DECAY * moment + clip * approx
        moment_new[...] = moved.reshape(moment_new.shape)
        weight_new[...] = (weight - LEARNING_RATE * moved).reshape(weight_new.shape)
        error[...] = (merged - approx * (1.0 / replicas)).reshape(error.shape)

    step(i * d, i * d, attn_m[0, 0], attn[0, 0], attn_mom[0, 0], attn_new, attn_mom_new, attn_err)
    step((8 + t) * d, 8 * d + t * ff + c * d, in_m[0], w_in[0], in_mom[0], in_new, in_mom_new, in_err)
    step(10 * d + t * ff + c * d, 8 * d + 2 * ff + t * d, out_m[0], w_out[0], out_mom[0], out_new, out_mom_new, out_err)


def update(replicas, outer, index, basis, right_mine, right_other, vector, gains, biases, gain_mom, bias_mom, merged, weights, moments):
    d, ff = weights[1].shape[1:]
    a_spec = pl.BlockSpec((1, 1, d, d), lambda i: (i // 4, i % 4, 0, 0))
    i_spec = pl.BlockSpec((1, d, d), lambda i: (i // 4, 0, i % 4))
    o_spec = pl.BlockSpec((1, d, d), lambda i: (i // 4, i % 4, 0))
    ae_spec = pl.BlockSpec((1, 1, 1, d, d), lambda i: (0, i // 4, i % 4, 0, 0))
    ie_spec = pl.BlockSpec((1, 1, d, d), lambda i: (0, i // 4, 0, i % 4))
    oe_spec = pl.BlockSpec((1, 1, d, d), lambda i: (0, i // 4, i % 4, 0))
    rows = functools.partial(jax.ShapeDtypeStruct, dtype=F32)
    small = (basis, right_mine, right_other, vector, gains, biases, gain_mom, bias_mom)
    finals = [gains.shape, biases.shape] * 2 + [(2, 4, 8, d), (2, 8, ff), (2, 8, d)]
    return pl.pallas_call(
        functools.partial(update_kernel, replicas, outer),
        grid=(8,),
        in_specs=[pl.BlockSpec(memory_space=pltpu.SMEM)] + [whole_spec(*a.shape) for a in small] + [a_spec, i_spec, o_spec] * 3,
        out_specs=[a_spec, i_spec, o_spec] * 2
        + [ae_spec, ie_spec, oe_spec]
        + [whole_spec(*shape) for shape in finals]
        + [pl.BlockSpec(memory_space=pltpu.SMEM)],
        out_shape=[rows(a.shape) for a in weights * 2]
        + [rows((1,) + a.shape) for a in weights]
        + [rows(shape) for shape in finals]
        + [rows((1,))],
        scratch_shapes=[pltpu.VMEM(basis.shape, F32), pltpu.VMEM((8, 128), F32)],
        compiler_params=pltpu.CompilerParams(vmem_limit_bytes=VMEM_LIMIT),
        name="update",
    )(index, *small, *merged, *weights, *moments)


def swap_with(x, axis, mask):
    return lax.ppermute(x, axis, [(i, i ^ mask) for i in range(lax.axis_size(axis))])


def sum_halves(mine, other):
    mine = mine + swap_with(other, "dp", 1)
    size = lax.axis_size("dp")
    if size == 8:
        steps = [("dp", (2, 4, 6))]
    else:
        steps = [("dp", (1 << b,)) for b in range(1, size.bit_length() - 1)]
    steps.append(("outer", tuple(range(1, lax.axis_size("outer")))))
    for axis, masks in steps:
        sent = mine.astype(SEND)
        for got in [swap_with(sent, axis, mask) for mask in masks]:
            mine = mine + got.astype(F32)
    return mine, swap_with(mine, "dp", 1)


def per_device(
    questions, passages, q_lengths, p_lengths, positives, pos_counts, attn, w_in, w_out, gains, biases, attn_mom, w_in_mom,
    w_out_mom, gain_mom, bias_mom, attn_err, w_in_err, w_out_err, attn_start, w_in_start, w_out_start,
):
    devices = lax.axis_size("dp") * lax.axis_size("outer")
    d, ff = w_in.shape[1:]
    xq = questions.reshape(-1, TOK, d)
    xp = passages.reshape(-1, TOK, d)
    nqu, npu = xq.shape[0], xp.shape[0]
    index = (lax.axis_index("dp") * lax.axis_size("outer") + lax.axis_index("outer")).astype(jnp.int32).reshape(1)
    *saved, pooled, units = forward(
        devices, q_lengths, p_lengths, xq, xp, attn, w_in, w_out, gains, biases, positives.T, pos_counts.reshape(1, -1)
    )
    units = lax.all_to_all(units, AXES, 0, 0)
    loss, gp = contrast(nqu, npu, positives.shape[1], index, q_lengths, p_lengths, units, pooled)
    starts = [jnp.swapaxes(start, -1, -2) for start in (attn_start, w_in_start, w_out_start)]
    outer = lax.axis_size("outer")
    qgrad, pgrad, attn_m, in_m, out_m, *left = backward(
        nqu // GROUP, npu // GROUP, outer, index, gp, saved, attn, w_in, w_out, gains, attn_err, w_in_err, w_out_err, starts
    )
    basis, *right, vector = right_factors(outer, index, *sum_halves(*left), attn_m, in_m, out_m)
    *new, attn_factor, in_factor, out_factor, norm = update(
        devices, outer, index, basis, *sum_halves(*right), vector, gains, biases, gain_mom, bias_mom,
        (attn_m, in_m, out_m), (attn, w_in, w_out), (attn_mom, w_in_mom, w_out_mom),
    )
    weights_new, moments_new, errors_new, vectors_new = new[:3], new[3:6], new[6:9], new[9:]
    factors = [jnp.swapaxes(factor, -1, -2) for factor in (attn_factor, in_factor, out_factor)]
    return (
        loss.reshape(-1), qgrad.reshape(questions.shape), pgrad.reshape(passages.shape),
        *weights_new, *vectors_new[:2], *moments_new, *vectors_new[2:], *errors_new, *factors, norm.reshape(()),
    )


def solution(mesh):
    split = ("dp", "outer")
    share = P(split)
    return jax.shard_map(
        per_device,
        mesh=mesh,
        in_specs=(share,) * 6 + (P(),) * 10 + (share,) * 3 + (P(),) * 3,
        out_specs=(share,) * 3 + (P(),) * 10 + (share,) * 3 + (P(),) * 4,
        check_vma=False,
    )
```

time: 203 us -> 156 us (0.77)
  Pallas kernels: 126 us -> 92.1 us
  starting transfers between devices: 30 us -> 24.7 us
  local copies, waits for them, and re-layouts: 7.02 us -> 1.99 us
  other arithmetic: 5.89 us -> 1.89 us
  waiting for transfers between devices: 31.6 us -> 33.7 us
    pallas_call x5, Pallas kernels: 126 us -> 92.1 us  [the longest x1 34 us: forward(): pl.pallas_call(functools.partial(forward_kernel, nqs), grid_spec=pltpu.Pr...]
    all_to_all x1 -> x0, starting transfers between devices: 7.3 us -> none  [per_device(): lax.all_to_all(jnp.broadcast_to(lists[None], (devices,) + lists.shape), A...]
    concatenate x4 -> x0, other arithmetic: 2.71 us -> none  [the longest x3 2.01 us: sum_over(): return jnp.concatenate([low, high], axis=1)]
    slice x4 -> x0, local copies, waits for them, and re-layouts: 2.43 us -> none  [the longest x1 1.2 us: per_device(): grad_norm = norm[0, 0]]
  transfers between devices with their start and end apart: 18 -> 17, of which waited for: 13 -> 13; matrix products, arithmetic and copies ran while one was open for 1% -> 0% of each run, Pallas kernels for 24% -> 0%
where the time goes in v2:
time: 156 us; the launch traced here: 155 us
  Pallas kernels  92.1 us (59%)
  waiting for transfers between devices  33.7 us (22%)
  starting transfers between devices  24.7 us (16%)
  local copies, waits for them, and re-layouts  1.99 us (1%)
  other arithmetic  1.89 us (1%)
    pallas_call x1, Pallas kernels, forward(): pl.pallas_call(functools.partial(forward_kernel, nqs), grid_spec=pltpu.Pr...  34 us
    pallas_call x1, Pallas kernels, backward(): pl.pallas_call(functools.partial(backward_kernel, nqs, outer), grid=(step...  33.2 us
    ppermute x16, waiting for transfers between devices, swap_with(): lax.ppermute(x, axis, [(i, i ^ mask) for i in range(lax.axis_size(axis))])  22.9 us
    ppermute x16, starting transfers between devices, swap_with(): lax.ppermute(x, axis, [(i, i ^ mask) for i in range(lax.axis_size(axis))])  17.2 us
    pallas_call x1, Pallas kernels, update(): pl.pallas_call(functools.partial(update_kernel, replicas, outer), grid=(8...  16.4 us
    all_to_all x1, waiting for transfers between devices, per_device(): units = lax.all_to_all(units, AXES, 0, 0)  10.8 us
    all_to_all x1, starting transfers between devices, per_device(): units = lax.all_to_all(units, AXES, 0, 0)  7.51 us
    pallas_call x1, Pallas kernels, right_factors(): pl.pallas_call(functools.partial(right_kernel, outer), in_specs=[pl.Block...  5.71 us
  transfers between devices with their start and end apart: 17, of which 13 were waited for; matrix products, arithmetic and copies ran while one was open for 0% of the time, Pallas kernels for 0%

profile of v2, /device:TPU:0, one launch (start us, length us, event | category | flops | bytes accessed | tf_op | source)
XLA Modules:
  0.0 155.3 jit_solution(10043984139797135898)
XLA Ops:
  0.7 34.0 %forward.1 = (bf16[5,272,512]{2,1,0:T(8,128)(2,1)}, bf16[5,512,512]{2,1,0:T(8,128)(2,1)}, bf16[5,512,256]{2,1,0:T(8,128)(2,1)}, bf16[5,2,4,256,256]{4,3,2,1,0:T(...) custom-call(s32[8]{0:T(128)} %qlen.3, s32[8]{0:T(128)} %plen.3, ...), custom_call_target="tpu_custom_call" | custom-call | tf_op jit(solution)/shard_map/forward/pallas_call | solution.py:273
  34.7 7.5 %all-to-all-start = ((bf16[32,40,128]{2,1,0:T(8,128)(2,1)}), bf16[32,40,128]{2,1,0:T(8,128)(2,1)S(1)}, u32[]{:S(2)}, u32[]{:S(2)}) async-start(bf16[32,40,128]{2,1,0:T(8,128)(2,1)} %get-tuple-element.64), calls=%async_computation | async-start | bytes 655360 | tf_op jit(solution)/shard_map/all_to_all | solution.py:787
  42.2 10.8 %all-to-all-done.units = bf16[32,40,128]{2,1,0:T(8,128)(2,1)S(1)} async-done(((bf16[32,40,128]{2,1,0:T(8,128)(2,1)}), bf16[32,40,128]{2,1,0:T(8,128)(2,1)S(1)}, u32[]{:S(2)}, u32[]{:S(2)}) %all-to-all-start) | async-done | bytes 327712 | tf_op jit(solution)/shard_map/all_to_all | solution.py:787
  53.0 0.0 copy-start
  53.0 0.7 copy-done
  53.7 2.9 %contrast.1 = (f32[1,8]{1,0:T(1,128)}, bf16[10,48,256]{2,1,0:T(8,128)(2,1)}) custom-call(s32[1]{0:T(128)} %bitcast.index, s32[8]{0:T(128)} %qlen.3, s32[8]{0:T(128)} %plen.3, bf16[32,40,128]{2,1,0:T(8,128)(2,1)} %copy-done, f32[16,256]{1,0:T(8,128)} %get-tuple-element.65.pooled), custom_call_target="tpu_custom_call" | custom-call | tf_op jit(solution)/shard_map/contrast/pallas_call | solution.py:364
  56.6 33.2 %backward.1 = (f32[2,256,256]{2,1,0:T(8,128)}, f32[8,256,256]{2,1,0:T(8,128)}, f32[2,4,256,256]{3,2,1,0:T(8,128)}, f32[2,256,1024]{2,1,0:T(8,128)}, f32[2,1024,2...) custom-call(s32[1]{0:T(128)} %bitcast.index, bf16[10,48,256]{2,1,0:T(8,128)(2,1)} %get-tuple-element.67.gp, ...), custom_call_target="tpu_custom_call" | custom-call | tf_op jit(solution)/shard_map/backward/pallas_call | solution.py:571
  89.8 0.9 collective-permute-start
  90.7 1.1 collective-permute-done
  91.8 0.9 add.46
  92.7 1.1 collective-permute-start.3
  93.8 1.5 collective-permute-start.2
  95.3 1.0 collective-permute-start.1
  96.3 2.8 %collective-permute-done.3 = f32[8,2688]{1,0:T(8,128)S(1)} collective-permute-done((f32[8,2688]{1,0:T(8,128)S(1)}, f32[8,2688]{1,0:T(8,128)S(1)}, u32[]{:S(2)}, u32[]{:S(2)}) %collective-permute-start.3) | collective-permute-done | bytes 86048 | tf_op jit(solution)/shard_map/ppermute | solution.py:756
  99.1 1.1 collective-permute-done.2
  100.2 0.0 collective-permute-done.1
  100.2 1.7 %collective-permute-start.6 = (f32[8,2688]{1,0:T(8,128)S(1)}, f32[8,2688]{1,0:T(8,128)S(1)}, u32[]{:S(2)}, u32[]{:S(2)}) collective-permute-start(f32[8,2688]{1,0:T(8,128)S(1)} %add_add_fusion.1), channel_id=1, source_target_pairs={{0,3},{1,2},{2,1},{3,0},{4,7},{5,6},{6,5},{7,4},{8,11},{9,10},{10,... | collective-permute-start | bytes 258056 | tf_op jit(solution)/shard_map/ppermute | solution.py:756
  101.9 0.6 collective-permute-start.5
  102.6 2.1 %collective-permute-start.4 = (f32[8,2688]{1,0:T(8,128)S(1)}, f32[8,2688]{1,0:T(8,128)S(1)}, u32[]{:S(2)}, u32[]{:S(2)}) collective-permute-start(f32[8,2688]{1,0:T(8,128)S(1)} %add_add_fusion.1), channel_id=1, source_target_pairs={{0,1},{1,0},{2,3},{3,2},{4,5},{5,4},{6,7},{7,6},{8,9},{9,8},{10,11... | collective-permute-start | bytes 258056 | tf_op jit(solution)/shard_map/ppermute | solution.py:756
  104.7 2.8 %collective-permute-done.6 = f32[8,2688]{1,0:T(8,128)S(1)} collective-permute-done((f32[8,2688]{1,0:T(8,128)S(1)}, f32[8,2688]{1,0:T(8,128)S(1)}, u32[]{:S(2)}, u32[]{:S(2)}) %collective-permute-start.6) | collective-permute-done | bytes 86048 | tf_op jit(solution)/shard_map/ppermute | solution.py:756
  107.5 3.1 %collective-permute-done.5 = f32[8,2688]{1,0:T(8,128)S(1)} collective-permute-done((f32[8,2688]{1,0:T(8,128)S(1)}, f32[8,2688]{1,0:T(8,128)S(1)}, u32[]{:S(2)}, u32[]{:S(2)}) %collective-permute-start.5) | collective-permute-done | bytes 86048 | tf_op jit(solution)/shard_map/ppermute | solution.py:756
  110.6 0.0 collective-permute-done.4
  110.6 0.0 copy-start.1
  110.6 0.1 collective-permute-start.7
  110.7 1.3 collective-permute-done.7.left_other
  112.0 0.0 copy-done.1
  112.0 0.6 copy-done.3
  112.6 5.7 %right.1 = (f32[8,4608]{1,0:T(8,128)}, f32[8,2304]{1,0:T(8,128)}, f32[8,2304]{1,0:T(8,128)}, f32[8,768]{1,0:T(8,128)}) custom-call(s32[1]{0:T(128)} %bitcast.index, f32[8,2688]{1,0:T(8,128)} %copy-done.1, f32[8,2688]{1,0:T(8,128)} %copy-done.3, f32[2,4,256,256]{3,2,1,0:T(8,128)} %get-tuple-element.84.attn_m, f32[2,256,1024]{2,1,0:T(8,128)} %get-tuple-element.85.in_m, ...), custom_call_target="tpu_custom_call" | custom-call | tf_op jit(solution)/shard_map/right/pallas_call | solution.py:650
  118.3 0.2 collective-permute-start.8
  118.5 1.3 collective-permute-done.8
  119.8 0.9 add.53
  120.7 1.2 collective-permute-start.11
  121.9 1.2 collective-permute-start.10
  123.2 1.1 collective-permute-start.9
  124.2 2.3 %collective-permute-done.11 = f32[8,2304]{1,0:T(8,128)S(1)} collective-permute-done((f32[8,2304]{1,0:T(8,128)S(1)}, f32[8,2304]{1,0:T(8,128)S(1)}, u32[]{:S(2)}, u32[]{:S(2)}) %collective-permute-start.11) | collective-permute-done | bytes 73760 | tf_op jit(solution)/shard_map/ppermute | solution.py:756
  126.5 1.1 collective-permute-done.10
  127.5 0.0 collective-permute-done.9
  127.6 1.7 %collective-permute-start.14 = (f32[8,2304]{1,0:T(8,128)S(1)}, f32[8,2304]{1,0:T(8,128)S(1)}, u32[]{:S(2)}, u32[]{:S(2)}) collective-permute-start(f32[8,2304]{1,0:T(8,128)S(1)} %add_add_fusion.3), channel_id=1, source_target_pairs={{0,3},{1,2},{2,1},{3,0},{4,7},{5,6},{6,5},{7,4},{8,11},{9,10},{10,... | collective-permute-start | bytes 221192 | tf_op jit(solution)/shard_map/ppermute | solution.py:756
  129.3 0.0 collective-permute-start.13
  129.3 2.8 %collective-permute-start.12 = (f32[8,2304]{1,0:T(8,128)S(1)}, f32[8,2304]{1,0:T(8,128)S(1)}, u32[]{:S(2)}, u32[]{:S(2)}) collective-permute-start(f32[8,2304]{1,0:T(8,128)S(1)} %add_add_fusion.3), channel_id=1, source_target_pairs={{0,1},{1,0},{2,3},{3,2},{4,5},{5,4},{6,7},{7,6},{8,9},{9,8},{10,11... | collective-permute-start | bytes 221192 | tf_op jit(solution)/shard_map/ppermute | solution.py:756
  132.0 2.6 %collective-permute-done.14 = f32[8,2304]{1,0:T(8,128)S(1)} collective-permute-done((f32[8,2304]{1,0:T(8,128)S(1)}, f32[8,2304]{1,0:T(8,128)S(1)}, u32[]{:S(2)}, u32[]{:S(2)}) %collective-permute-start.14) | collective-permute-done | bytes 73760 | tf_op jit(solution)/shard_map/ppermute | solution.py:756
  134.6 2.2 %collective-permute-done.13 = f32[8,2304]{1,0:T(8,128)S(1)} collective-permute-done((f32[8,2304]{1,0:T(8,128)S(1)}, f32[8,2304]{1,0:T(8,128)S(1)}, u32[]{:S(2)}, u32[]{:S(2)}) %collective-permute-start.13) | collective-permute-done | bytes 73760 | tf_op jit(solution)/shard_map/ppermute | solution.py:756
  136.8 0.0 collective-permute-done.12
  136.8 0.1 collective-permute-start.15
  136.9 1.2 collective-permute-done.15.right_other
  138.2 0.0 copy-done.2
  138.2 0.6 copy-done.4
  138.8 16.4 %update.1 = (f32[2,4,256,256]{3,2,1,0:T(8,128)}, f32[2,256,1024]{2,1,0:T(8,128)}, f32[2,1024,256]{2,1,0:T(8,128)}, f32[2,4,256,256]{3,2,1,0:T(8,128)}, f32[2,256...) custom-call(s32[1]{0:T(128)} %bitcast.index, ...), custom_call_target="tpu_custom_call" | custom-call | tf_op jit(solution)/shard_map/update/pallas_call | solution.py:737
  (7 shorter events, 0.1 us)
Async XLA Ops:
  34.7 18.3 %all-to-all-start = ((bf16[32,40,128]{2,1,0:T(8,128)(2,1)}), bf16[32,40,128]{2,1,0:T(8,128)(2,1)S(1)}, u32[]{:S(2)}, u32[]{:S(2)}) async-start(bf16[32,40,128]{2,1,0:T(8,128)(2,1)} %get-tuple-element.64), calls=%async_computation | async-start | bytes 655360 | tf_op jit(solution)/shard_map/all_to_all | solution.py:787
  53.0 0.7 copy-start
  89.8 2.0 %collective-permute-start = (f32[8,2688]{1,0:T(8,128)}, f32[8,2688]{1,0:T(8,128)S(1)}, u32[]{:S(2)}, u32[]{:S(2)}) collective-permute-start(f32[8,2688]{1,0:T(8,128)} %get-tuple-element.83), channel_id=1, source_target_pairs={{0,4},{4,0},{8,12},{12,8},{16,20},{20,16},{24,28},{28,24},{1,5},{5... | collective-permute-start | bytes 258056 | tf_op jit(solution)/shard_map/ppermute | solution.py:756
  92.7 6.4 %collective-permute-start.3 = (f32[8,2688]{1,0:T(8,128)S(1)}, f32[8,2688]{1,0:T(8,128)S(1)}, u32[]{:S(2)}, u32[]{:S(2)}) collective-permute-start(f32[8,2688]{1,0:T(8,128)S(1)} %add.46), channel_id=1, source_target_pairs={{0,24},{4,28},{8,16},{12,20},{16,8},{20,12},{24,0},{28,4},{1,25},{... | collective-permute-start | bytes 258056 | tf_op jit(solution)/shard_map/ppermute | solution.py:756
  93.8 6.4 %collective-permute-start.2 = (f32[8,2688]{1,0:T(8,128)S(1)}, f32[8,2688]{1,0:T(8,128)S(1)}, u32[]{:S(2)}, u32[]{:S(2)}) collective-permute-start(f32[8,2688]{1,0:T(8,128)S(1)} %add.46), channel_id=1, source_target_pairs={{0,16},{4,20},{8,24},{12,28},{16,0},{20,4},{24,8},{28,12},{1,17},{... | collective-permute-start | bytes 258056 | tf_op jit(solution)/shard_map/ppermute | solution.py:756
  95.3 4.9 %collective-permute-start.1 = (f32[8,2688]{1,0:T(8,128)S(1)}, f32[8,2688]{1,0:T(8,128)S(1)}, u32[]{:S(2)}, u32[]{:S(2)}) collective-permute-start(f32[8,2688]{1,0:T(8,128)S(1)} %add.46), channel_id=1, source_target_pairs={{0,8},{4,12},{8,0},{12,4},{16,24},{20,28},{24,16},{28,20},{1,9},{5... | collective-permute-start | bytes 258056 | tf_op jit(solution)/shard_map/ppermute | solution.py:756
  100.2 7.3 %collective-permute-start.6 = (f32[8,2688]{1,0:T(8,128)S(1)}, f32[8,2688]{1,0:T(8,128)S(1)}, u32[]{:S(2)}, u32[]{:S(2)}) collective-permute-start(f32[8,2688]{1,0:T(8,128)S(1)} %add_add_fusion.1), channel_id=1, source_target_pairs={{0,3},{1,2},{2,1},{3,0},{4,7},{5,6},{6,5},{7,4},{8,11},{9,10},{10,... | collective-permute-start | bytes 258056 | tf_op jit(solution)/shard_map/ppermute | solution.py:756
  101.9 8.6 %collective-permute-start.5 = (f32[8,2688]{1,0:T(8,128)S(1)}, f32[8,2688]{1,0:T(8,128)S(1)}, u32[]{:S(2)}, u32[]{:S(2)}) collective-permute-start(f32[8,2688]{1,0:T(8,128)S(1)} %add_add_fusion.1), channel_id=1, source_target_pairs={{0,2},{1,3},{2,0},{3,1},{4,6},{5,7},{6,4},{7,5},{8,10},{9,11},{10,... | collective-permute-start | bytes 258056 | tf_op jit(solution)/shard_map/ppermute | solution.py:756
  102.6 8.0 %collective-permute-start.4 = (f32[8,2688]{1,0:T(8,128)S(1)}, f32[8,2688]{1,0:T(8,128)S(1)}, u32[]{:S(2)}, u32[]{:S(2)}) collective-permute-start(f32[8,2688]{1,0:T(8,128)S(1)} %add_add_fusion.1), channel_id=1, source_target_pairs={{0,1},{1,0},{2,3},{3,2},{4,5},{5,4},{6,7},{7,6},{8,9},{9,8},{10,11... | collective-permute-start | bytes 258056 | tf_op jit(solution)/shard_map/ppermute | solution.py:756
  110.6 1.4 copy-start.1
  110.6 1.3 collective-permute-start.7
  112.0 0.6 copy-start.3
  118.3 1.5 collective-permute-start.8
  120.7 5.8 %collective-permute-start.11 = (f32[8,2304]{1,0:T(8,128)S(1)}, f32[8,2304]{1,0:T(8,128)S(1)}, u32[]{:S(2)}, u32[]{:S(2)}) collective-permute-start(f32[8,2304]{1,0:T(8,128)S(1)} %add.53), channel_id=1, source_target_pairs={{0,24},{4,28},{8,16},{12,20},{16,8},{20,12},{24,0},{28,4},{1,25},{... | collective-permute-start | bytes 221192 | tf_op jit(solution)/shard_map/ppermute | solution.py:756
  121.9 5.6 %collective-permute-start.10 = (f32[8,2304]{1,0:T(8,128)S(1)}, f32[8,2304]{1,0:T(8,128)S(1)}, u32[]{:S(2)}, u32[]{:S(2)}) collective-permute-start(f32[8,2304]{1,0:T(8,128)S(1)} %add.53), channel_id=1, source_target_pairs={{0,16},{4,20},{8,24},{12,28},{16,0},{20,4},{24,8},{28,12},{1,17},{... | collective-permute-start | bytes 221192 | tf_op jit(solution)/shard_map/ppermute | solution.py:756
  123.2 4.4 %collective-permute-start.9 = (f32[8,2304]{1,0:T(8,128)S(1)}, f32[8,2304]{1,0:T(8,128)S(1)}, u32[]{:S(2)}, u32[]{:S(2)}) collective-permute-start(f32[8,2304]{1,0:T(8,128)S(1)} %add.53), channel_id=1, source_target_pairs={{0,8},{4,12},{8,0},{12,4},{16,24},{20,28},{24,16},{28,20},{1,9},{5... | collective-permute-start | bytes 221192 | tf_op jit(solution)/shard_map/ppermute | solution.py:756
  127.6 7.1 %collective-permute-start.14 = (f32[8,2304]{1,0:T(8,128)S(1)}, f32[8,2304]{1,0:T(8,128)S(1)}, u32[]{:S(2)}, u32[]{:S(2)}) collective-permute-start(f32[8,2304]{1,0:T(8,128)S(1)} %add_add_fusion.3), channel_id=1, source_target_pairs={{0,3},{1,2},{2,1},{3,0},{4,7},{5,6},{6,5},{7,4},{8,11},{9,10},{10,... | collective-permute-start | bytes 221192 | tf_op jit(solution)/shard_map/ppermute | solution.py:756
  129.3 7.5 %collective-permute-start.13 = (f32[8,2304]{1,0:T(8,128)S(1)}, f32[8,2304]{1,0:T(8,128)S(1)}, u32[]{:S(2)}, u32[]{:S(2)}) collective-permute-start(f32[8,2304]{1,0:T(8,128)S(1)} %add_add_fusion.3), channel_id=1, source_target_pairs={{0,2},{1,3},{2,0},{3,1},{4,6},{5,7},{6,4},{7,5},{8,10},{9,11},{10,... | collective-permute-start | bytes 221192 | tf_op jit(solution)/shard_map/ppermute | solution.py:756
  129.3 7.5 %collective-permute-start.12 = (f32[8,2304]{1,0:T(8,128)S(1)}, f32[8,2304]{1,0:T(8,128)S(1)}, u32[]{:S(2)}, u32[]{:S(2)}) collective-permute-start(f32[8,2304]{1,0:T(8,128)S(1)} %add_add_fusion.3), channel_id=1, source_target_pairs={{0,1},{1,0},{2,3},{3,2},{4,5},{5,4},{6,7},{7,6},{8,9},{9,8},{10,11... | collective-permute-start | bytes 221192 | tf_op jit(solution)/shard_map/ppermute | solution.py:756
  136.8 1.3 copy-start.2
  136.8 1.3 collective-permute-start.15
  138.2 0.6 copy-start.4

commit v3 on v2

--- a/solution.py
+++ b/solution.py
@@ -26,7 +26,7 @@
 F32 = jnp.float32
 BF16 = jnp.bfloat16
 VMEM_LIMIT = 56 << 20
-SEND = F32
+SEND = BF16
 
 
 def mm(a, b, precision=None):
@@ -588,9 +588,9 @@
         out_shape=[
             jax.ShapeDtypeStruct((nqu, TOK, d), F32),
             jax.ShapeDtypeStruct((npu, TOK, d), F32),
-            jax.ShapeDtypeStruct((2, 4, d, d), F32),
-            jax.ShapeDtypeStruct((2, d, ff), F32),
-            jax.ShapeDtypeStruct((2, ff, d), F32),
+            pltpu.VMEM((2, 4, d, d), F32),
+            pltpu.VMEM((2, d, ff), F32),
+            pltpu.VMEM((2, ff, d), F32),
             jax.ShapeDtypeStruct((8, width // 2), F32),
             jax.ShapeDtypeStruct((8, width // 2), F32),
         ],
@@ -611,7 +611,7 @@
             pltpu.VMEM((ff + ONES, d), F32),
             pltpu.VMEM((4 * d, 128), F32),
         ],
-        compiler_params=pltpu.CompilerParams(vmem_limit_bytes=VMEM_LIMIT),
+        compiler_params=pltpu.CompilerParams(vmem_limit_bytes=50 << 20),
         name="backward",
     )(index, gp, *saved, attn, w_in, w_out, gains, attn_err, in_err, out_err, *starts)
 
@@ -653,7 +653,7 @@
         out_specs=[vmem] * 4,
         out_shape=[rows((8, width)), rows((8, width // 2)), rows((8, width // 2)), rows((8, 3 * d))],
         scratch_shapes=[pltpu.VMEM((8, width + 3 * d), F32), pltpu.VMEM((8, width), F32)],
-        compiler_params=pltpu.CompilerParams(vmem_limit_bytes=VMEM_LIMIT),
+        compiler_params=pltpu.CompilerParams(vmem_limit_bytes=12 << 20),
         name="right",
     )(index, left_mine, left_other, attn_m, in_m, out_m)
 
@@ -747,9 +747,13 @@
         + [rows(shape) for shape in finals]
         + [rows((1,))],
         scratch_shapes=[pltpu.VMEM(basis.shape, F32), pltpu.VMEM((8, 128), F32)],
-        compiler_params=pltpu.CompilerParams(vmem_limit_bytes=VMEM_LIMIT),
+        compiler_params=pltpu.CompilerParams(vmem_limit_bytes=14 << 20),
         name="update",
     )(index, *small, *merged, *weights, *moments)
+
+
+def in_vmem(*arrays):
+    return tuple(pltpu.with_memory_space_constraint(a, pltpu.VMEM) for a in arrays)
 
 
 def swap_with(x, axis, mask):
@@ -766,6 +770,7 @@
     steps.append(("outer", tuple(range(1, lax.axis_size("outer")))))
     for axis, masks in steps:
         sent = mine.astype(SEND)
+        mine = sent.astype(F32)
         for got in [swap_with(sent, axis, mask) for mask in masks]:
             mine = mine + got.astype(F32)
     return mine, swap_with(mine, "dp", 1)
@@ -785,16 +790,20 @@
         devices, q_lengths, p_lengths, xq, xp, attn, w_in, w_out, gains, biases, positives.T, pos_counts.reshape(1, -1)
     )
     units = lax.all_to_all(units, AXES, 0, 0)
-    loss, gp = contrast(nqu, npu, positives.shape[1], index, q_lengths, p_lengths, units, pooled)
+    loss, gp = contrast(nqu, npu, positives.shape[1], index, q_lengths, p_lengths, *in_vmem(units), pooled)
     starts = [jnp.swapaxes(start, -1, -2) for start in (attn_start, w_in_start, w_out_start)]
     outer = lax.axis_size("outer")
     qgrad, pgrad, attn_m, in_m, out_m, *left = backward(
         nqu // GROUP, npu // GROUP, outer, index, gp, saved, attn, w_in, w_out, gains, attn_err, w_in_err, w_out_err, starts
     )
-    basis, *right, vector = right_factors(outer, index, *sum_halves(*left), attn_m, in_m, out_m)
+    weights = (attn, w_in, w_out)
+    moments = (attn_mom, w_in_mom, w_out_mom)
+    merged = in_vmem(attn_m, in_m, out_m)
+    held = in_vmem(*weights, *moments)
+    basis, *right, vector = right_factors(outer, index, *sum_halves(*left), *merged)
     *new, attn_factor, in_factor, out_factor, norm = update(
         devices, outer, index, basis, *sum_halves(*right), vector, gains, biases, gain_mom, bias_mom,
-        (attn_m, in_m, out_m), (attn, w_in, w_out), (attn_mom, w_in_mom, w_out_mom),
+        merged, held[:3], held[3:],
     )
     weights_new, moments_new, errors_new, vectors_new = new[:3], new[3:6], new[6:9], new[9:]
     factors = [jnp.swapaxes(factor, -1, -2) for factor in (attn_factor, in_factor, out_factor)]

time: 156 us -> 134 us (0.86)
  Pallas kernels: 92.1 us -> 79.9 us
  waiting for transfers between devices: 33.7 us -> 27 us
  local copies, waits for them, and re-layouts: 1.99 us -> 0.04 us
    pallas_call x1, Pallas kernels: 16.4 us -> 8.81 us  [update(): pl.pallas_call(functools.partial(update_kernel, replicas, outer), grid=(8...]
    ppermute x16, waiting for transfers between devices: 22.9 us -> 16.2 us  [swap_with(): lax.ppermute(x, axis, [(i, i ^ mask) for i in range(lax.axis_size(axis))])]
    pallas_call x1, Pallas kernels: 5.71 us -> 2.08 us  [right_factors(): pl.pallas_call(functools.partial(right_kernel, outer), in_specs=[pl.Block...]
    unnamed x10 -> x20, local copies, waits for them, and re-layouts: 1.99 us -> 0.04 us
    add x2 -> x0, other arithmetic: 1.8 us -> none  [sum_halves(): mine = mine + swap_with(other, 'dp', 1)]
  transfers between devices with their start and end apart: 17 -> 17, of which waited for: 13 -> 16; matrix products, arithmetic and copies ran while one was open for 0% -> 0% of each run, Pallas kernels for 0% -> 0%
where the time goes in v3:
time: 134 us
  Pallas kernels  79.9 us (60%)
  waiting for transfers between devices  27 us (20%)
  starting transfers between devices  24.8 us (19%)
    pallas_call x1, Pallas kernels, forward(): pl.pallas_call(functools.partial(forward_kernel, nqs), grid_spec=pltpu.Pr...  34 us
    pallas_call x1, Pallas kernels, backward(): pl.pallas_call(functools.partial(backward_kernel, nqs, outer), grid=(step...  32.4 us
    ppermute x16, starting transfers between devices, swap_with(): lax.ppermute(x, axis, [(i, i ^ mask) for i in range(lax.axis_size(axis))])  17.3 us
    ppermute x16, waiting for transfers between devices, swap_with(): lax.ppermute(x, axis, [(i, i ^ mask) for i in range(lax.axis_size(axis))])  16.2 us
    all_to_all x1, waiting for transfers between devices, per_device(): units = lax.all_to_all(units, AXES, 0, 0)  10.8 us
    pallas_call x1, Pallas kernels, update(): pl.pallas_call(functools.partial(update_kernel, replicas, outer), grid=(8...  8.81 us
    all_to_all x1, starting transfers between devices, per_device(): units = lax.all_to_all(units, AXES, 0, 0)  7.51 us
  transfers between devices with their start and end apart: 17, of which 16 were waited for; matrix products, arithmetic and copies ran while one was open for 0% of the time, Pallas kernels for 0%

profile of v3, /device:TPU:0, one launch (start us, length us, event | category | flops | bytes accessed | tf_op | source)
XLA Modules:
  0.0 133.6 jit_solution(7644882675689402780)
XLA Ops:
  0.7 34.0 %forward.1 = (bf16[5,272,512]{2,1,0:T(8,128)(2,1)}, bf16[5,512,512]{2,1,0:T(8,128)(2,1)}, bf16[5,512,256]{2,1,0:T(8,128)(2,1)}, bf16[5,2,4,256,256]{4,3,2,1,0:T(...) custom-call(s32[8]{0:T(128)} %qlen.3, s32[8]{0:T(128)} %plen.3, ...), custom_call_target="tpu_custom_call" | custom-call | tf_op jit(solution)/shard_map/forward/pallas_call | solution.py:273
  34.7 7.5 %all-to-all-start = ((bf16[32,40,128]{2,1,0:T(8,128)(2,1)}), bf16[32,40,128]{2,1,0:T(8,128)(2,1)S(1)}, u32[]{:S(2)}, u32[]{:S(2)}) async-start(bf16[32,40,128]{2,1,0:T(8,128)(2,1)} %get-tuple-element.64), calls=%async_computation | async-start | bytes 655360 | tf_op jit(solution)/shard_map/all_to_all | solution.py:792
  42.2 10.8 %all-to-all-done.units = bf16[32,40,128]{2,1,0:T(8,128)(2,1)S(1)} async-done(((bf16[32,40,128]{2,1,0:T(8,128)(2,1)}), bf16[32,40,128]{2,1,0:T(8,128)(2,1)S(1)}, u32[]{:S(2)}, u32[]{:S(2)}) %all-to-all-start) | async-done | bytes 327712 | tf_op jit(solution)/shard_map/all_to_all | solution.py:792
  53.0 2.6 %contrast.1 = (f32[1,8]{1,0:T(1,128)}, bf16[10,48,256]{2,1,0:T(8,128)(2,1)}) custom-call(s32[1]{0:T(128)} %bitcast.index, s32[8]{0:T(128)} %qlen.3, s32[8]{0:T(128)} %plen.3, bf16[32,40,128]{2,1,0:T(8,128)(2,1)S(1)} %all-to-all-done.units, f32[16,256]{1,0:T(8,128)} %get-tuple-element.65.pooled), custom_call_target="tpu_custom_call" | custom-call | tf_op jit(solution)/shard_map/contrast/pallas_call | solution.py:364
  55.6 32.4 %backward.1 = (f32[2,256,256]{2,1,0:T(8,128)}, f32[8,256,256]{2,1,0:T(8,128)}, f32[2,4,256,256]{3,2,1,0:T(8,128)S(1)}, f32[2,256,1024]{2,1,0:T(8,128)S(1)}, f32[...) custom-call(s32[1]{0:T(128)} %bitcast.index, bf16[10,48,256]{2,1,0:T(8,128)(2,1)} %get-tuple-element.67.gp, ...), custom_call_target="tpu_custom_call" | custom-call | tf_op jit(solution)/shard_map/backward/pallas_call | solution.py:571
  88.0 0.9 collective-permute-start
  88.9 1.1 collective-permute-done
  90.0 0.9 add_convert_fusion.1
  90.9 1.1 collective-permute-start.3
  92.0 1.5 %collective-permute-start.2 = (bf16[8,2688]{1,0:T(8,128)(2,1)S(1)}, bf16[8,2688]{1,0:T(8,128)(2,1)S(1)}, u32[]{:S(2)}, u32[]{:S(2)}) collective-permute-start(bf16[8,2688]{1,0:T(8,128)(2,1)S(1)} %add_convert_fusion.1), channel_id=1, source_target_pairs={{0,16},{4,20},{8,24},{12,28},{16,0},{20,4},{24,8},{28,12},{1,17},{... | collective-permute-start | bytes 129032 | tf_op jit(solution)/shard_map/ppermute | solution.py:760
  93.5 1.0 collective-permute-start.1
  94.5 1.5 %collective-permute-done.3 = bf16[8,2688]{1,0:T(8,128)(2,1)S(1)} collective-permute-done((bf16[8,2688]{1,0:T(8,128)(2,1)S(1)}, bf16[8,2688]{1,0:T(8,128)(2,1)S(1)}, u32[]{:S(2)}, u32[]{:S(2)}) %collective-permute-start.3) | collective-permute-done | bytes 43040 | tf_op jit(solution)/shard_map/ppermute | solution.py:760
  96.0 0.5 collective-permute-done.2
  96.5 1.0 collective-permute-done.1
  97.6 2.0 %collective-permute-start.6 = (bf16[8,2688]{1,0:T(8,128)(2,1)S(1)}, bf16[8,2688]{1,0:T(8,128)(2,1)S(1)}, u32[]{:S(2)}, u32[]{:S(2)}) collective-permute-start(bf16[8,2688]{1,0:T(8,128)(2,1)S(1)} %add_convert_fusion), channel_id=1, source_target_pairs={{0,3},{1,2},{2,1},{3,0},{4,7},{5,6},{6,5},{7,4},{8,11},{9,10},{10,... | collective-permute-start | bytes 129032 | tf_op jit(solution)/shard_map/ppermute | solution.py:760
  99.6 0.2 collective-permute-start.5
  99.9 2.2 %collective-permute-start.4 = (bf16[8,2688]{1,0:T(8,128)(2,1)S(1)}, bf16[8,2688]{1,0:T(8,128)(2,1)S(1)}, u32[]{:S(2)}, u32[]{:S(2)}) collective-permute-start(bf16[8,2688]{1,0:T(8,128)(2,1)S(1)} %add_convert_fusion), channel_id=1, source_target_pairs={{0,1},{1,0},{2,3},{3,2},{4,5},{5,4},{6,7},{7,6},{8,9},{9,8},{10,11... | collective-permute-start | bytes 129032 | tf_op jit(solution)/shard_map/ppermute | solution.py:760
  102.0 1.7 %collective-permute-done.6 = bf16[8,2688]{1,0:T(8,128)(2,1)S(1)} collective-permute-done((bf16[8,2688]{1,0:T(8,128)(2,1)S(1)}, bf16[8,2688]{1,0:T(8,128)(2,1)S(1)}, u32[]{:S(2)}, u32[]{:S(2)}) %collective-permute-start.6) | collective-permute-done | bytes 43040 | tf_op jit(solution)/shard_map/ppermute | solution.py:760
  103.7 0.9 collective-permute-done.5
  104.6 0.0 collective-permute-done.4
  104.6 0.1 collective-permute-start.7
  104.7 1.3 collective-permute-done.7.left_other
  106.0 0.0 copy-start.7
  106.0 0.0 copy-start.8
  106.0 0.0 copy-start.9
  106.0 2.1 %right.1 = (f32[8,4608]{1,0:T(8,128)S(1)}, f32[8,2304]{1,0:T(8,128)S(1)}, f32[8,2304]{1,0:T(8,128)S(1)}, f32[8,768]{1,0:T(8,128)S(1)}) custom-call(s32[1]{0:T(128)} %bitcast.index, f32[8,2688]{1,0:T(8,128)S(1)} %convert_add_fusion.left_mine, f32[8,2688]{1,0:T(8,128)S(1)} %collective-permute-done.7.left_other, ...), custom_call_target="tpu_custom_call" | custom-call | tf_op jit(solution)/shard_map/right/pallas_call | solution.py:650
  108.1 0.2 collective-permute-start.8
  108.3 1.1 collective-permute-done.8
  109.4 1.5 %collective-permute-start.11 = (bf16[8,2304]{1,0:T(8,128)(2,1)S(1)}, bf16[8,2304]{1,0:T(8,128)(2,1)S(1)}, u32[]{:S(2)}, u32[]{:S(2)}) collective-permute-start(bf16[8,2304]{1,0:T(8,128)(2,1)S(1)} %add_convert_fusion.3), channel_id=1, source_target_pairs={{0,24},{4,28},{8,16},{12,20},{16,8},{20,12},{24,0},{28,4},{1,25},{... | collective-permute-start | bytes 110600 | tf_op jit(solution)/shard_map/ppermute | solution.py:760
  111.0 1.2 collective-permute-start.10
  112.2 0.8 collective-permute-start.9
  113.0 1.4 %collective-permute-done.11 = bf16[8,2304]{1,0:T(8,128)(2,1)S(1)} collective-permute-done((bf16[8,2304]{1,0:T(8,128)(2,1)S(1)}, bf16[8,2304]{1,0:T(8,128)(2,1)S(1)}, u32[]{:S(2)}, u32[]{:S(2)}) %collective-permute-start.11) | collective-permute-done | bytes 36896 | tf_op jit(solution)/shard_map/ppermute | solution.py:760
  114.4 0.6 collective-permute-done.10
  114.9 1.2 collective-permute-done.9
  116.1 1.9 %collective-permute-start.14 = (bf16[8,2304]{1,0:T(8,128)(2,1)S(1)}, bf16[8,2304]{1,0:T(8,128)(2,1)S(1)}, u32[]{:S(2)}, u32[]{:S(2)}) collective-permute-start(bf16[8,2304]{1,0:T(8,128)(2,1)S(1)} %add_convert_fusion.2), channel_id=1, source_target_pairs={{0,3},{1,2},{2,1},{3,0},{4,7},{5,6},{6,5},{7,4},{8,11},{9,10},{10,... | collective-permute-start | bytes 110600 | tf_op jit(solution)/shard_map/ppermute | solution.py:760
  118.0 0.9 collective-permute-start.13
  118.9 1.7 %collective-permute-start.12 = (bf16[8,2304]{1,0:T(8,128)(2,1)S(1)}, bf16[8,2304]{1,0:T(8,128)(2,1)S(1)}, u32[]{:S(2)}, u32[]{:S(2)}) collective-permute-start(bf16[8,2304]{1,0:T(8,128)(2,1)S(1)} %add_convert_fusion.2), channel_id=1, source_target_pairs={{0,1},{1,0},{2,3},{3,2},{4,5},{5,4},{6,7},{7,6},{8,9},{9,8},{10,11... | collective-permute-start | bytes 110600 | tf_op jit(solution)/shard_map/ppermute | solution.py:760
  120.6 1.4 %collective-permute-done.14 = bf16[8,2304]{1,0:T(8,128)(2,1)S(1)} collective-permute-done((bf16[8,2304]{1,0:T(8,128)(2,1)S(1)}, bf16[8,2304]{1,0:T(8,128)(2,1)S(1)}, u32[]{:S(2)}, u32[]{:S(2)}) %collective-permute-start.14) | collective-permute-done | bytes 36896 | tf_op jit(solution)/shard_map/ppermute | solution.py:760
  122.0 1.1 collective-permute-done.13
  123.0 0.2 collective-permute-done.12
  123.3 0.1 collective-permute-start.15
  123.4 1.3 collective-permute-done.15.right_other
  124.6 0.0 copy-done.3
  124.6 0.0 copy-done.4
  124.6 0.0 copy-done.5
  124.6 0.0 copy-done
  124.6 0.0 copy-done.1
  124.7 8.8 %update.1 = (f32[2,4,256,256]{3,2,1,0:T(8,128)}, f32[2,256,1024]{2,1,0:T(8,128)}, f32[2,1024,256]{2,1,0:T(8,128)}, f32[2,4,256,256]{3,2,1,0:T(8,128)}, f32[2,256...) custom-call(s32[1]{0:T(128)} %bitcast.index, ...), custom_call_target="tpu_custom_call" | custom-call | tf_op jit(solution)/shard_map/update/pallas_call | solution.py:737
  (17 shorter events, 0.1 us)
Async XLA Ops:
  34.7 18.3 %all-to-all-start = ((bf16[32,40,128]{2,1,0:T(8,128)(2,1)}), bf16[32,40,128]{2,1,0:T(8,128)(2,1)S(1)}, u32[]{:S(2)}, u32[]{:S(2)}) async-start(bf16[32,40,128]{2,1,0:T(8,128)(2,1)} %get-tuple-element.64), calls=%async_computation | async-start | bytes 655360 | tf_op jit(solution)/shard_map/all_to_all | solution.py:792
  55.6 69.0 %copy-start.3 = (f32[2,4,256,256]{3,2,1,0:T(8,128)S(1)}, f32[2,4,256,256]{3,2,1,0:T(8,128)}, u32[]{:S(2)}) copy-start(f32[2,4,256,256]{3,2,1,0:T(8,128)} %attn_mom.1) | copy-start | bytes 6291460
  55.6 69.0 %copy-start.4 = (f32[2,256,1024]{2,1,0:T(8,128)S(1)}, f32[2,256,1024]{2,1,0:T(8,128)}, u32[]{:S(2)}) copy-start(f32[2,256,1024]{2,1,0:T(8,128)} %in_mom.1) | copy-start | bytes 6291460
  55.6 69.0 %copy-start.5 = (f32[2,1024,256]{2,1,0:T(8,128)S(1)}, f32[2,1024,256]{2,1,0:T(8,128)}, u32[]{:S(2)}) copy-start(f32[2,1024,256]{2,1,0:T(8,128)} %out_mom.1) | copy-start | bytes 6291460
  88.0 2.0 %collective-permute-start = (f32[8,2688]{1,0:T(8,128)}, f32[8,2688]{1,0:T(8,128)S(1)}, u32[]{:S(2)}, u32[]{:S(2)}) collective-permute-start(f32[8,2688]{1,0:T(8,128)} %get-tuple-element.83), channel_id=1, source_target_pairs={{0,4},{4,0},{8,12},{12,8},{16,20},{20,16},{24,28},{28,24},{1,5},{5... | collective-permute-start | bytes 258056 | tf_op jit(solution)/shard_map/ppermute | solution.py:760
  90.9 5.1 %collective-permute-start.3 = (bf16[8,2688]{1,0:T(8,128)(2,1)S(1)}, bf16[8,2688]{1,0:T(8,128)(2,1)S(1)}, u32[]{:S(2)}, u32[]{:S(2)}) collective-permute-start(bf16[8,2688]{1,0:T(8,128)(2,1)S(1)} %add_convert_fusion.1), channel_id=1, source_target_pairs={{0,24},{4,28},{8,16},{12,20},{16,8},{20,12},{24,0},{28,4},{1,25},{... | collective-permute-start | bytes 129032 | tf_op jit(solution)/shard_map/ppermute | solution.py:760
  92.0 4.5 %collective-permute-start.2 = (bf16[8,2688]{1,0:T(8,128)(2,1)S(1)}, bf16[8,2688]{1,0:T(8,128)(2,1)S(1)}, u32[]{:S(2)}, u32[]{:S(2)}) collective-permute-start(bf16[8,2688]{1,0:T(8,128)(2,1)S(1)} %add_convert_fusion.1), channel_id=1, source_target_pairs={{0,16},{4,20},{8,24},{12,28},{16,0},{20,4},{24,8},{28,12},{1,17},{... | collective-permute-start | bytes 129032 | tf_op jit(solution)/shard_map/ppermute | solution.py:760
  93.5 4.0 %collective-permute-start.1 = (bf16[8,2688]{1,0:T(8,128)(2,1)S(1)}, bf16[8,2688]{1,0:T(8,128)(2,1)S(1)}, u32[]{:S(2)}, u32[]{:S(2)}) collective-permute-start(bf16[8,2688]{1,0:T(8,128)(2,1)S(1)} %add_convert_fusion.1), channel_id=1, source_target_pairs={{0,8},{4,12},{8,0},{12,4},{16,24},{20,28},{24,16},{28,20},{1,9},{5... | collective-permute-start | bytes 129032 | tf_op jit(solution)/shard_map/ppermute | solution.py:760
  97.6 6.1 %collective-permute-start.6 = (bf16[8,2688]{1,0:T(8,128)(2,1)S(1)}, bf16[8,2688]{1,0:T(8,128)(2,1)S(1)}, u32[]{:S(2)}, u32[]{:S(2)}) collective-permute-start(bf16[8,2688]{1,0:T(8,128)(2,1)S(1)} %add_convert_fusion), channel_id=1, source_target_pairs={{0,3},{1,2},{2,1},{3,0},{4,7},{5,6},{6,5},{7,4},{8,11},{9,10},{10,... | collective-permute-start | bytes 129032 | tf_op jit(solution)/shard_map/ppermute | solution.py:760
  99.6 5.0 %collective-permute-start.5 = (bf16[8,2688]{1,0:T(8,128)(2,1)S(1)}, bf16[8,2688]{1,0:T(8,128)(2,1)S(1)}, u32[]{:S(2)}, u32[]{:S(2)}) collective-permute-start(bf16[8,2688]{1,0:T(8,128)(2,1)S(1)} %add_convert_fusion), channel_id=1, source_target_pairs={{0,2},{1,3},{2,0},{3,1},{4,6},{5,7},{6,4},{7,5},{8,10},{9,11},{10,... | collective-permute-start | bytes 129032 | tf_op jit(solution)/shard_map/ppermute | solution.py:760
  99.9 4.7 %collective-permute-start.4 = (bf16[8,2688]{1,0:T(8,128)(2,1)S(1)}, bf16[8,2688]{1,0:T(8,128)(2,1)S(1)}, u32[]{:S(2)}, u32[]{:S(2)}) collective-permute-start(bf16[8,2688]{1,0:T(8,128)(2,1)S(1)} %add_convert_fusion), channel_id=1, source_target_pairs={{0,1},{1,0},{2,3},{3,2},{4,5},{5,4},{6,7},{7,6},{8,9},{9,8},{10,11... | collective-permute-start | bytes 129032 | tf_op jit(solution)/shard_map/ppermute | solution.py:760
  104.6 1.3 %collective-permute-start.7 = (f32[8,2688]{1,0:T(8,128)S(1)}, f32[8,2688]{1,0:T(8,128)S(1)}, u32[]{:S(2)}, u32[]{:S(2)}) collective-permute-start(f32[8,2688]{1,0:T(8,128)S(1)} %convert_add_fusion.left_mine), channel_id=1, source_target_pairs={{0,4},{4,0},{8,12},{12,8},{16,20},{20,16},{24,28},{28,24},{1,5},{5... | collective-permute-start | bytes 258056 | tf_op jit(solution)/shard_map/ppermute | solution.py:760
  106.0 18.6 %copy-start = (f32[2,4,256,256]{3,2,1,0:T(8,128)S(1)}, f32[2,4,256,256]{3,2,1,0:T(8,128)}, u32[]{:S(2)}) copy-start(f32[2,4,256,256]{3,2,1,0:T(8,128)} %attn.5) | copy-start | bytes 6291460
  106.0 18.6 %copy-start.1 = (f32[2,256,1024]{2,1,0:T(8,128)S(1)}, f32[2,256,1024]{2,1,0:T(8,128)}, u32[]{:S(2)}) copy-start(f32[2,256,1024]{2,1,0:T(8,128)} %w_in.5) | copy-start | bytes 6291460
  106.0 18.7 %copy-start.2 = (f32[2,1024,256]{2,1,0:T(8,128)S(1)}, f32[2,1024,256]{2,1,0:T(8,128)}, u32[]{:S(2)}) copy-start(f32[2,1024,256]{2,1,0:T(8,128)} %w_out.5) | copy-start | bytes 6291460
  106.0 18.7 %copy-start.6 = (f32[2,2560]{1,0:T(2,128)S(1)}, f32[2,2560]{1,0:T(2,128)}, u32[]{:S(2)}) copy-start(f32[2,2560]{1,0:T(2,128)} %biases.3) | copy-start | bytes 61444
  106.0 18.7 %copy-start.7 = (f32[2,2,256]{2,1,0:T(2,128)S(1)}, f32[2,2,256]{2,1,0:T(2,128)}, u32[]{:S(2)}) copy-start(f32[2,2,256]{2,1,0:T(2,128)} %gains.5) | copy-start | bytes 12292
  106.0 18.7 %copy-start.8 = (f32[2,2560]{1,0:T(2,128)S(1)}, f32[2,2560]{1,0:T(2,128)}, u32[]{:S(2)}) copy-start(f32[2,2560]{1,0:T(2,128)} %bias_mom.1) | copy-start | bytes 61444
  106.0 18.7 %copy-start.9 = (f32[2,2,256]{2,1,0:T(2,128)S(1)}, f32[2,2,256]{2,1,0:T(2,128)}, u32[]{:S(2)}) copy-start(f32[2,2,256]{2,1,0:T(2,128)} %gain_mom.1) | copy-start | bytes 12292
  108.1 1.3 collective-permute-start.8
  109.4 4.9 %collective-permute-start.11 = (bf16[8,2304]{1,0:T(8,128)(2,1)S(1)}, bf16[8,2304]{1,0:T(8,128)(2,1)S(1)}, u32[]{:S(2)}, u32[]{:S(2)}) collective-permute-start(bf16[8,2304]{1,0:T(8,128)(2,1)S(1)} %add_convert_fusion.3), channel_id=1, source_target_pairs={{0,24},{4,28},{8,16},{12,20},{16,8},{20,12},{24,0},{28,4},{1,25},{... | collective-permute-start | bytes 110600 | tf_op jit(solution)/shard_map/ppermute | solution.py:760
  111.0 4.0 %collective-permute-start.10 = (bf16[8,2304]{1,0:T(8,128)(2,1)S(1)}, bf16[8,2304]{1,0:T(8,128)(2,1)S(1)}, u32[]{:S(2)}, u32[]{:S(2)}) collective-permute-start(bf16[8,2304]{1,0:T(8,128)(2,1)S(1)} %add_convert_fusion.3), channel_id=1, source_target_pairs={{0,16},{4,20},{8,24},{12,28},{16,0},{20,4},{24,8},{28,12},{1,17},{... | collective-permute-start | bytes 110600 | tf_op jit(solution)/shard_map/ppermute | solution.py:760
  112.2 4.0 %collective-permute-start.9 = (bf16[8,2304]{1,0:T(8,128)(2,1)S(1)}, bf16[8,2304]{1,0:T(8,128)(2,1)S(1)}, u32[]{:S(2)}, u32[]{:S(2)}) collective-permute-start(bf16[8,2304]{1,0:T(8,128)(2,1)S(1)} %add_convert_fusion.3), channel_id=1, source_target_pairs={{0,8},{4,12},{8,0},{12,4},{16,24},{20,28},{24,16},{28,20},{1,9},{5... | collective-permute-start | bytes 110600 | tf_op jit(solution)/shard_map/ppermute | solution.py:760
  116.1 5.8 %collective-permute-start.14 = (bf16[8,2304]{1,0:T(8,128)(2,1)S(1)}, bf16[8,2304]{1,0:T(8,128)(2,1)S(1)}, u32[]{:S(2)}, u32[]{:S(2)}) collective-permute-start(bf16[8,2304]{1,0:T(8,128)(2,1)S(1)} %add_convert_fusion.2), channel_id=1, source_target_pairs={{0,3},{1,2},{2,1},{3,0},{4,7},{5,6},{6,5},{7,4},{8,11},{9,10},{10,... | collective-permute-start | bytes 110600 | tf_op jit(solution)/shard_map/ppermute | solution.py:760
  118.0 5.0 %collective-permute-start.13 = (bf16[8,2304]{1,0:T(8,128)(2,1)S(1)}, bf16[8,2304]{1,0:T(8,128)(2,1)S(1)}, u32[]{:S(2)}, u32[]{:S(2)}) collective-permute-start(bf16[8,2304]{1,0:T(8,128)(2,1)S(1)} %add_convert_fusion.2), channel_id=1, source_target_pairs={{0,2},{1,3},{2,0},{3,1},{4,6},{5,7},{6,4},{7,5},{8,10},{9,11},{10,... | collective-permute-start | bytes 110600 | tf_op jit(solution)/shard_map/ppermute | solution.py:760
  118.9 4.4 %collective-permute-start.12 = (bf16[8,2304]{1,0:T(8,128)(2,1)S(1)}, bf16[8,2304]{1,0:T(8,128)(2,1)S(1)}, u32[]{:S(2)}, u32[]{:S(2)}) collective-permute-start(bf16[8,2304]{1,0:T(8,128)(2,1)S(1)} %add_convert_fusion.2), channel_id=1, source_target_pairs={{0,1},{1,0},{2,3},{3,2},{4,5},{5,4},{6,7},{7,6},{8,9},{9,8},{10,11... | collective-permute-start | bytes 110600 | tf_op jit(solution)/shard_map/ppermute | solution.py:760
  123.3 1.3 collective-permute-start.15

commit v4 on v3

v4 whole, which is shorter than its diff:
```python
import functools
import math

import jax
import jax.numpy as jnp
from jax import lax
from jax.experimental import pallas as pl
from jax.experimental.pallas import tpu as pltpu
from jax.sharding import PartitionSpec as P

HEAD = 64
TOK = 256
GROUP = 2
PART = 64
ONES = 16

NORM_EPSILON = 1e-06
UNIT_EPSILON = 1e-06
SCORE_SCALE = 20.0
MOMENTUM_DECAY = 0.9
LEARNING_RATE = 10.0
CLIP_NORM = 2.0
MASKED_SCORE = -1e30
HIGHEST = lax.Precision.HIGHEST
AXES = ("dp", "outer")
F32 = jnp.float32
BF16 = jnp.bfloat16
VMEM_LIMIT = 56 << 20
FORWARD_VMEM = 20 << 20
BACKWARD_VMEM = 20 << 20
SEND = BF16


def mm(a, b, precision=None):
    return lax.dot_general(a, b, (((1,), (0,)), ((), ())), precision=precision, preferred_element_type=F32)


def mm_nt(a, b, precision=None):
    return lax.dot_general(a, b, (((1,), (1,)), ((), ())), precision=precision, preferred_element_type=F32)


def mm_tn(a, b, precision=None):
    return lax.dot_general(a, b, (((0,), (0,)), ((), ())), precision=precision, preferred_element_type=F32)


def wide(column):
    return jnp.concatenate([column] * (GROUP * TOK // 128), axis=1)


def split_two(v):
    high = v.astype(BF16)
    return high, (v - high.astype(F32)).astype(BF16)


def split_three(v):
    high = v.astype(BF16)
    rest = v - high.astype(F32)
    middle = rest.astype(BF16)
    return high, middle, (rest - middle.astype(F32)).astype(BF16)


def norm_columns(hidden, gain, shift):
    share = 1.0 / hidden.shape[0]
    center = hidden - jnp.sum(hidden, axis=0, keepdims=True) * share
    inverse = lax.rsqrt(jnp.sum(center * center, axis=0, keepdims=True) * share + NORM_EPSILON)
    normed = center * inverse
    return normed * gain + shift, normed, inverse


def norm_columns_back(grad, normed, inverse, gain):
    share = 1.0 / grad.shape[0]
    scaled = grad * gain
    mean = jnp.sum(scaled, axis=0, keepdims=True) * share
    along = jnp.sum(scaled * normed, axis=0, keepdims=True) * share
    return inverse * (scaled - mean - normed * along)


def gelu_and_slope(u):
    phi = 0.5 + 0.5 * lax.erf(u * 0.5**0.5)
    bell = jnp.exp(u * u * -0.5) * (0.5 / math.pi) ** 0.5
    return u * phi, phi + u * bell


def forward_kernel(
    nqs, qlen, plen, xq, xp, attn, w_in, w_out, gains, biases, lists, counts,
    x_out, qk_out, v_out, p_out, ctx_out, n1_out, first_out, slope_out, act_out, n2_out, inv1_out, inv2_out, live_out, wqkv_out, wo_out, win_out, wout_out, pooled_out, units_out,
    wproj, wo_t, win_t, wout_t, bias_bc, gain_bc, qblk, xs, away, score_s, first_s, first_low_s, turn,
):
    i = pl.program_id(0)
    steps = pl.num_programs(0) - 1
    d = xs.shape[1]
    ff = win_t.shape[0]
    heads = d // HEAD
    segs = TOK // HEAD
    span = GROUP * TOK
    late = jnp.maximum(i - 1, 0)

    def tower(group):
        return jnp.where(group < nqs, 0, 1)

    def eye():
        return (lax.broadcasted_iota(jnp.int32, (d, d), 0) == lax.broadcasted_iota(jnp.int32, (d, d), 1)).astype(F32).astype(BF16)

    def spread(at, row):
        bias_bc[at : at + d, :] = jnp.broadcast_to(row, (128, d)).T

    @pl.when(i == 0)
    def _():
        qblk[...] = jnp.zeros_like(qblk)

    @pl.when((i == 0) | (i == nqs))
    def _():
        one = eye()
        t = tower(i)
        for j in range(3):
            low = attn[0, j].astype(BF16)
            wqkv_out[t, :, j * d : (j + 1) * d] = low
            wproj[j * d : (j + 1) * d, :] = mm_nt(one, low).astype(BF16)
            if j:
                wproj[(3 + j) * d : (4 + j) * d, :] = low
        wproj[3 * d : 4 * d, :] = one
        low = attn[0, 3].astype(BF16)
        wo_out[t] = low
        wo_t[...] = mm_nt(one, low).astype(BF16)
        for c in range(4):
            spread(c * d, biases[pl.ds(t, 1), c * d : (c + 1) * d])
        gain_bc[0:d, :] = jnp.broadcast_to(gains[t, 0:1, :], (128, d)).T

    @pl.when((i == 1) | (i == nqs + 1))
    def _():
        one = eye()
        t = tower(late)
        for c in range(ff // d):
            at = slice(c * d, (c + 1) * d)
            low = w_in[0, :, at].astype(BF16)
            win_out[t, :, at] = low
            win_t[at, :] = mm_nt(one, low).astype(BF16)
            low = w_out[0, at, :].astype(BF16)
            wout_out[t, at, :] = low
            wout_t[:, at] = mm_nt(one, low).astype(BF16)
        for c in range(4, bias_bc.shape[0] // d):
            spread(c * d, biases[pl.ds(t, 1), c * d : (c + 1) * d])
        gain_bc[d : 2 * d, :] = jnp.broadcast_to(gains[t, 1:2, :], (128, d)).T

    @pl.when(i < nqs)
    def _():
        xs[...] = xq[...].reshape(span, d)

    @pl.when(i >= nqs)
    def _():
        xs[...] = xp[...].reshape(span, d)

    def length_of(group, u, segment):
        base = (jnp.minimum(group, nqs - 1) * GROUP + u) * segs
        out = jnp.full(segment.shape, qlen[base + segs - 1], jnp.int32)
        for s in range(segs - 1):
            out = jnp.where(segment == s, qlen[base + s], out)
        return jnp.where(group < nqs, out, plen[jnp.clip(group - nqs, 0, steps - nqs - 1) * GROUP + u])

    def bias(at, size):
        return wide(bias_bc[at : at + size, :])

    def attention_parts():
        is_q = i < nqs
        key = lax.broadcasted_iota(jnp.int32, (TOK, TOK), 0)
        ask = lax.broadcasted_iota(jnp.int32, (TOK, TOK), 1)
        key_col = lax.broadcasted_iota(jnp.int32, (TOK, 1), 0)
        far = is_q & ((key // HEAD) != (ask // HEAD))
        for u in range(GROUP):
            dead = jnp.where(is_q, key_col % HEAD, key_col) >= length_of(i, u, key_col // HEAD)
            away[u] = jnp.where(far | dead, MASKED_SCORE, 0.0)
        x = xs[...]
        q_t = (mm_nt(wproj[0:d, :], x) + bias(0, d)).astype(BF16)
        qk_out[i, 0:d, :] = q_t
        for u in range(GROUP):
            for h in range(heads):
                piece = q_t[h * HEAD : (h + 1) * HEAD, u * TOK : (u + 1) * TOK]
                qblk[u, h * HEAD : (h + 1) * HEAD, h * TOK : (h + 1) * TOK] = piece * BF16(HEAD**-0.5)
        k_row = mm(x, wproj[4 * d : 5 * d, :]).astype(BF16)
        yield
        v_t = (mm_nt(wproj[2 * d : 3 * d, :], x) + bias(d, d)).astype(BF16)
        for u in range(GROUP):
            for h in range(heads):
                score_s[u, h] = mm(k_row[u * TOK : (u + 1) * TOK, :], qblk[u, :, h * TOK : (h + 1) * TOK])
            yield
        qk_out[i, d : 2 * d, :] = mm_nt(wproj[d : 2 * d, :], x).astype(BF16)
        v_out[i] = (mm(x, wproj[5 * d : 6 * d, :]) + biases[pl.ds(tower(i), 1), d : 2 * d]).astype(BF16)
        x_t = mm_nt(wproj[3 * d : 4 * d, :], x)
        x_out[i, 0:d, :] = x_t.astype(BF16)
        yield
        for u in range(GROUP):
            for h in range(heads):
                scores = score_s[u, h] + away[u]
                exponent = jnp.exp(scores - jnp.max(scores, axis=0, keepdims=True))
                probs = exponent * (1.0 / jnp.sum(exponent, axis=0, keepdims=True))
                p_out[i, u, h] = probs.astype(BF16)
                at = slice(h * HEAD, (h + 1) * HEAD)
                over = slice(u * TOK, (u + 1) * TOK)
                ctx_out[i, at, over] = mm(v_t[at, over], p_out[i, u, h]).astype(BF16)
                if h % 2:
                    yield
        hidden = x_t + (mm(wo_t[...], ctx_out[i, 0:d, :]) + bias(2 * d, d))
        first, n1, inv1 = norm_columns(hidden, wide(gain_bc[0:d, :]), bias(3 * d, d))
        n1_out[i] = n1
        inv1_out[i] = jnp.broadcast_to(inv1, (8, span))
        ones = jnp.ones((ONES, span), BF16)
        x_out[i, d:, :] = ones
        ctx_out[i, d:, :] = ones
        first_out[i, d:, :] = ones
        yield
        first_low = first.astype(BF16)
        first_out[i, 0:d, :] = first_low
        first_low_s[...] = first_low
        first_s[...] = first

    def feed_parts():
        is_q = late < nqs
        first_low = first_low_s[...]
        hidden = first_s[...] + bias(4 * d, d)
        for c in range(ff // d):
            at = slice(c * d, (c + 1) * d)
            for half in range(2):
                rows = slice(c * d + half * (d // 2), c * d + (half + 1) * (d // 2))
                upper = mm(win_t[rows, :], first_low) + bias(6 * d + rows.start, d // 2)
                active, slope = gelu_and_slope(upper)
                slope_out[late, rows, :] = slope
                act_out[late, rows, :] = active.astype(BF16)
                yield
            hidden = hidden + mm(wout_t[:, at], act_out[late, at, :])
        second, n2, inv2 = norm_columns(hidden, wide(gain_bc[d : 2 * d, :]), bias(5 * d, d))
        n2_out[late] = n2
        inv2_out[late] = jnp.broadcast_to(inv2, (8, span))
        act_out[late, ff:, :] = jnp.ones((ONES, span), BF16)
        second_high, second_low = split_two(second)
        row = lax.broadcasted_iota(jnp.int32, (16, TOK), 0)
        token = lax.broadcasted_iota(jnp.int32, (16, TOK), 1)
        owner = jnp.where(is_q, token // HEAD, 0)
        place = jnp.where(is_q, token % HEAD, token)
        seg_row = lax.broadcasted_iota(jnp.int32, (16, 1), 0)
        for u in range(GROUP):
            over = slice(u * TOK, (u + 1) * TOK)
            live = ((place < length_of(late, u, token // HEAD)) & (row == owner)).astype(F32).astype(BF16)
            live_out[late, :, over] = live
            pooled = mm_nt(live, second_high[:, over]) + mm_nt(live, second_low[:, over])
            pooled = pooled / length_of(late, u, seg_row).astype(F32)

            @pl.when(is_q)
            def _(pooled=pooled, u=u):
                for s in range(segs):
                    pooled_out[pl.ds((late * GROUP + u) * segs + s, 1), :] = pooled[s : s + 1, :]

            @pl.when(jnp.logical_not(is_q))
            def _(pooled=pooled, u=u):
                pooled_out[pl.ds(nqs * GROUP * segs + (late - nqs) * GROUP + u, 1), :] = pooled[0:1, :]

    def in_turn(*kinds):
        running = [kind() for kind in kinds]
        while running:
            running = [parts for parts in running if next(parts, running) is not running]

    @pl.when(i == 0)
    def _():
        in_turn(attention_parts)

    @pl.when((i > 0) & (i < steps))
    def _():
        in_turn(feed_parts, attention_parts)

    @pl.when(i == steps)
    def _():
        in_turn(feed_parts)
        rows = pooled_out[...]
        unit = rows * lax.rsqrt(jnp.sum(rows * rows, axis=1, keepdims=True) + UNIT_EPSILON)
        slots, own = lists.shape
        turn[...] = jnp.zeros_like(turn)
        turn[0:slots, 0:own] = (lists[...] // PART).astype(F32)
        turn[slots : 2 * slots, 0:own] = (lists[...] % PART).astype(F32)
        turn[2 * slots : 2 * slots + 1, 0:own] = counts[...].astype(F32)
        extra = turn[...].T[0:own, :]
        sent = jnp.concatenate([unit[:, c * 128 : (c + 1) * 128] for c in range(d // 128)] + [extra], axis=0)
        units_out[0] = sent.astype(BF16)


def step_spec(*shape):
    return pl.BlockSpec((1,) + shape, lambda i, *_: (i,) + (0,) * len(shape))


def tower_spec(nqs, *shape):
    return pl.BlockSpec((1,) + shape, lambda i, *_: (jnp.where(i < nqs, 0, 1),) + (0,) * len(shape))


def whole_spec(*shape):
    return pl.BlockSpec(shape, lambda i, *_: (0,) * len(shape))


def forward(q_lengths, p_lengths, xq, xp, attn, w_in, w_out, gains, biases, positives, counts):
    nqs, nps = xq.shape[0] // GROUP, xp.shape[0] // GROUP
    steps = nqs + nps
    span = GROUP * TOK
    d, ff = w_in.shape[1:]
    heads = d // HEAD
    seqs = q_lengths.shape[0] + xp.shape[0]
    sent = seqs * d // 128 + positives.shape[1]
    early = [
        ((d + ONES, span), BF16),
        ((2 * d, span), BF16),
        ((span, d), BF16),
        ((GROUP, heads, TOK, TOK), BF16),
        ((d + ONES, span), BF16),
        ((d, span), F32),
        ((d + ONES, span), BF16),
    ]
    later = [((ff, span), F32), ((ff + ONES, span), BF16), ((d, span), F32)]
    rows = [((8, span), F32), ((8, span), F32), ((16, span), BF16)]
    outs = early + later + rows

    def second_tower_spec(*shape):
        return pl.BlockSpec((1,) + shape, lambda i, *_: (jnp.where(i - 1 < nqs, 0, 1),) + (0,) * len(shape))

    kept = [pltpu.VMEM((steps,) + shape, kind) for shape, kind in outs]
    kept += [pltpu.VMEM((2,) + shape, BF16) for shape in ((d, 3 * d), (d, d), (d, ff), (ff, d))]
    kept += [pltpu.VMEM((seqs, d), F32)]
    direct = pl.BlockSpec(memory_space=pltpu.VMEM)
    return pl.pallas_call(
        functools.partial(forward_kernel, nqs),
        grid_spec=pltpu.PrefetchScalarGridSpec(
            num_scalar_prefetch=2,
            grid=(steps + 1,),
            in_specs=[
                pl.BlockSpec((GROUP, TOK, d), lambda i, *_: (jnp.minimum(i, nqs - 1), 0, 0)),
                pl.BlockSpec((GROUP, TOK, d), lambda i, *_: (jnp.clip(i - nqs, 0, nps - 1), 0, 0)),
                tower_spec(nqs, 4, d, d),
                second_tower_spec(d, ff),
                second_tower_spec(ff, d),
                whole_spec(2, 2, d),
                whole_spec(2, biases.shape[1]),
                whole_spec(*positives.shape),
                whole_spec(1, positives.shape[1]),
            ],
            out_specs=[direct] * (len(kept) + 1),
            scratch_shapes=[
                pltpu.VMEM((6 * d, d), BF16),
                pltpu.VMEM((d, d), BF16),
                pltpu.VMEM((ff, d), BF16),
                pltpu.VMEM((d, ff), BF16),
                pltpu.VMEM((biases.shape[1], 128), F32),
                pltpu.VMEM((2 * d, 128), F32),
                pltpu.VMEM((GROUP, d, heads * TOK), BF16),
                pltpu.VMEM((span, d), BF16),
                pltpu.VMEM((GROUP, TOK, TOK), F32),
                pltpu.VMEM((GROUP, heads, TOK, TOK), F32),
                pltpu.VMEM((d, span), F32),
                pltpu.VMEM((d, span), BF16),
                pltpu.VMEM((128, 128), F32),
            ],
        ),
        out_shape=kept + [jax.ShapeDtypeStruct((1, sent, 128), BF16)],
        compiler_params=pltpu.CompilerParams(vmem_limit_bytes=FORWARD_VMEM),
        name="forward",
    )(q_lengths, p_lengths, xq, xp, attn, w_in, w_out, gains, biases, positives, counts)


def contrast_kernel(
    nqu, slots, dp, outer, qlen, plen, near, far, pooled, loss_out, gp_out, low_rows, gup_rows, gp_rows, turn
):
    devices = dp * outer
    seqs, d = pooled.shape
    own = qlen.shape[0]
    pown = seqs - own
    both = jnp.concatenate([near[...], far[...]], axis=0).astype(F32)
    parts = range(0, seqs * d // 128, seqs)
    uq = jnp.concatenate([both[:, at : at + own, :] for at in parts], axis=2).reshape(devices * own, d).astype(BF16)
    up = jnp.concatenate([both[:, at + own : at + seqs, :] for at in parts], axis=2).reshape(devices * pown, d).astype(BF16)
    lists = both[:, seqs * d // 128 :, :].reshape(devices * own, 128)
    scores = SCORE_SCALE * mm_nt(uq, up)
    place = lax.broadcasted_iota(jnp.int32, (1, devices * pown), 1)
    block = place // pown
    along = ((block // outer) % (dp // 2)) * 2 + block // (devices // 2)
    device = (lax.axis_index("dp") ^ along) * outer + (lax.axis_index("outer") ^ (block % outer))
    columns = (device * pown + place % pown).astype(F32)
    positive = None
    for k in range(slots):
        listed = lists[:, k : k + 1] * PART + lists[:, slots + k : slots + k + 1]
        hit = (listed == columns) & (lists[:, 2 * slots : 2 * slots + 1] > k)
        positive = hit if positive is None else positive | hit
    highest = jnp.max(scores, axis=1, keepdims=True)
    whole = highest + jnp.log(jnp.sum(jnp.exp(scores - highest), axis=1, keepdims=True))
    chosen = jnp.where(positive, scores, MASKED_SCORE)
    top = jnp.max(chosen, axis=1, keepdims=True)
    within = top + jnp.log(jnp.sum(jnp.exp(chosen - top), axis=1, keepdims=True))
    low = (SCORE_SCALE * (jnp.exp(scores - whole) - jnp.exp(chosen - within))).astype(BF16)
    low_rows[:, : scores.shape[1]] = low.astype(F32)
    low_rows[:, scores.shape[1] :] = jnp.broadcast_to(whole - within, (scores.shape[0], 128))
    turn[...] = jnp.zeros_like(turn)
    turn[0:own, :] = low_rows[0:own, scores.shape[1] :]
    loss_out[...] = turn[...].T[0:1, 0:own]
    grad_q = mm(low_rows[0:own, : scores.shape[1]].astype(BF16), up)
    gup_rows[...] = mm_tn(low, uq)
    grad_p = gup_rows[0:pown, :]
    grad = jnp.concatenate([grad_q, grad_p], axis=0)
    rows = pooled[...]
    inverse = lax.rsqrt(jnp.sum(rows * rows, axis=1, keepdims=True) + UNIT_EPSILON)
    grad = inverse * grad - inverse * inverse * inverse * rows * jnp.sum(rows * grad, axis=1, keepdims=True)
    segs = own // nqu
    gp_rows[...] = jnp.zeros_like(gp_rows)
    for s in range(own):
        gp_rows[s // segs, s % segs : s % segs + 1, :] = grad[s : s + 1, :] / jnp.full((1, d), qlen[s], jnp.int32).astype(F32)
    for s in range(pown):
        gp_rows[nqu + s, 0:1, :] = grad[own + s : own + s + 1, :] / jnp.full((1, d), plen[s], jnp.int32).astype(F32)
    for term, value in enumerate(split_three(gp_rows[...])):
        gp_out[:, term * 16 : (term + 1) * 16, :] = value


def contrast(nqu, npu, slots, dp, outer, q_lengths, p_lengths, near, far, pooled):
    devices = dp * outer
    seqs, d = pooled.shape
    own = q_lengths.shape[0]
    passages = devices * (seqs - own)
    vmem = pl.BlockSpec(memory_space=pltpu.VMEM)
    return pl.pallas_call(
        functools.partial(contrast_kernel, nqu, slots, dp, outer),
        in_specs=[pl.BlockSpec(memory_space=pltpu.SMEM)] * 2 + [vmem] * 3,
        out_specs=[vmem, vmem],
        out_shape=[jax.ShapeDtypeStruct((1, own), F32), pltpu.VMEM((nqu + npu, 48, d), BF16)],
        scratch_shapes=[
            pltpu.VMEM((devices * own, passages + 128), F32),
            pltpu.VMEM((passages, d), F32),
            pltpu.VMEM((nqu + npu, 16, d), F32),
            pltpu.VMEM((128, 128), F32),
        ],
        compiler_params=pltpu.CompilerParams(vmem_limit_bytes=min(VMEM_LIMIT, (6 << 20) + 32 * devices * own * passages)),
        name="contrast",
    )(q_lengths, p_lengths, near, far, pooled)


def left_rows(start_t, matrix):
    s_high, s_low = split_two(start_t)
    m_high, m_low = split_two(matrix)
    both = mm_nt(jnp.concatenate([s_high, s_low], axis=0), m_high)
    return both[:8] + both[8:] + mm_nt(jnp.concatenate([s_high, s_high], axis=0), m_low)[:8]


def right_rows(basis, matrix):
    b_high, b_low = split_two(basis)
    m_high, m_low = split_two(matrix)
    both = mm(jnp.concatenate([b_high, b_low], axis=0), m_high)
    return both[:8] + both[8:] + mm(jnp.concatenate([b_high, b_high], axis=0), m_low)[:8]


def own_core():
    return lax.axis_index("dp") % 2


def part_halves(core, whole, mine, other):
    half = whole.shape[1] // 2
    for c in range(2):

        @pl.when(core == c)
        def _(c=c):
            mine[...] = whole[:, c * half : (c + 1) * half]
            other[...] = whole[:, (1 - c) * half : (2 - c) * half]


def join_halves(core, whole, mine, other):
    half = whole.shape[1] // 2
    for c in range(2):

        @pl.when(core == c)
        def _(c=c):
            whole[:, c * half : (c + 1) * half] = mine[...]
            whole[:, (1 - c) * half : (2 - c) * half] = other[...]


def backward_kernel(
    nqs, gp, x_in, qk_in, v_in, p_in, ctx_in, n1_in, first_in, slope_in, act_in, n2_in, inv1_in, inv2_in, live_in,
    wqkv, wo, win, wout, gains, attn_err, in_err, out_err, attn_start, in_start, out_start,
    qgrad, pgrad, attn_m, in_m, out_m, left_mine, left_other,
    left, gain_bc, gz, gp_s, graw_s, gqkv, acc_qkv, acc_o, acc_in, acc_out, acc_gain, err_sems,
):
    i = pl.program_id(0)
    last = pl.num_programs(0) - 1
    is_q = i < nqs
    t = jnp.where(is_q, 0, 1)
    d = wo.shape[1]
    ff = wout.shape[1]
    errors = [
        pltpu.make_async_copy(source.at[0, tower], target.at[tower], err_sems.at[tower, k])
        for tower in range(2)
        for k, (source, target) in enumerate(((attn_err, attn_m), (in_err, in_m), (out_err, out_m)))
    ]
    heads = d // HEAD
    span = GROUP * TOK

    @pl.when(i == 0)
    def _():
        for copy in errors:
            copy.start()
        gz[...] = jnp.zeros_like(gz)

    @pl.when((i == 0) | (i == nqs))
    def _():
        for c in range(2):
            row = gains[t, c : c + 1, :]
            gain_bc[c * d : (c + 1) * d, :] = jnp.broadcast_to(row, (128, d)).T
        acc_qkv[...] = jnp.zeros_like(acc_qkv)
        acc_o[...] = jnp.zeros_like(acc_o)
        acc_in[...] = jnp.zeros_like(acc_in)
        acc_out[...] = jnp.zeros_like(acc_out)
        acc_gain[...] = jnp.zeros_like(acc_gain)

    def add_gain(at, value):
        total = value[:, :128]
        for c in range(1, span // 128):
            total = total + value[:, c * 128 : (c + 1) * 128]
        acc_gain[at * d : (at + 1) * d, :] += total

    pieces = []
    for u in range(GROUP):
        live = live_in[i, :, u * TOK : (u + 1) * TOK]
        pieces.append(mm_tn(gp[i * GROUP + u], jnp.concatenate([live, live, live], axis=0)))
    grad_second = jnp.concatenate(pieces, axis=1)
    n2 = n2_in[i]
    grad_two = norm_columns_back(grad_second, n2, inv2_in[i, 0:1, :], wide(gain_bc[d : 2 * d, :]))
    down_low = grad_two.astype(BF16)
    grad_first = grad_two
    for c in range(ff // d):
        at = slice(c * d, (c + 1) * d)
        up_low = (mm(wout[t, at, :], down_low) * slope_in[i, at, :]).astype(BF16)
        acc_in[:, at] += mm_nt(first_in[i], up_low)
        grad_first = grad_first + mm(win[t, :, at], up_low)
    add_gain(1, grad_second * n2)
    add_gain(3, grad_second)
    n1 = n1_in[i]
    grad_one = norm_columns_back(grad_first, n1, inv1_in[i, 0:1, :], wide(gain_bc[0:d, :]))
    branch_low = grad_one.astype(BF16)
    grad_context = mm(wo[t], branch_low).astype(BF16)
    for u in range(GROUP):
        for h in range(heads):
            at = slice(h * HEAD, (h + 1) * HEAD)
            gz[u, at, h * TOK : (h + 1) * TOK] = grad_context[at, u * TOK : (u + 1) * TOK]
    for u in range(GROUP):
        for h in range(heads):
            gp_s[u, h] = mm(v_in[i, u * TOK : (u + 1) * TOK, :], gz[u, :, h * TOK : (h + 1) * TOK])
    acc_out[...] += mm_nt(act_in[i], down_low)
    add_gain(0, grad_first * n1)
    add_gain(2, grad_first)
    acc_o[...] += mm_nt(ctx_in[i], branch_low)
    for u in range(GROUP):
        for h in range(heads):
            probs = p_in[i, u, h].astype(F32)
            grad_probs = gp_s[u, h]
            inner = jnp.sum(grad_probs * probs, axis=0, keepdims=True)
            graw_s[u, h] = (probs * (grad_probs - inner) * HEAD**-0.5).astype(BF16)
    for u in range(GROUP):
        over = slice(u * TOK, (u + 1) * TOK)
        for h in range(heads):
            at = slice(h * HEAD, (h + 1) * HEAD)
            later = slice(d + h * HEAD, d + (h + 1) * HEAD)
            last_at = slice(2 * d + h * HEAD, 2 * d + (h + 1) * HEAD)
            gqkv[last_at, over] = mm_nt(grad_context[at, over], p_in[i, u, h]).astype(BF16)
            gqkv[at, over] = mm(qk_in[i, later, over], graw_s[u, h]).astype(BF16)
            gqkv[later, over] = mm_nt(qk_in[i, at, over], graw_s[u, h]).astype(BF16)
    acc_qkv[...] += mm_nt(x_in[i], gqkv[...])
    result = (grad_one + mm(wqkv[t], gqkv[...])).T.reshape(GROUP, TOK, d)

    @pl.when(is_q)
    def _():
        qgrad[...] = result

    @pl.when(jnp.logical_not(is_q))
    def _():
        pgrad[...] = result

    @pl.when((i == nqs - 1) | (i == last))
    def _():
        for tower in range(2):

            @pl.when(t == tower)
            def _(tower=tower):
                for copy in errors[3 * tower : 3 * tower + 3]:
                    copy.wait()

        base_in = 8 * d
        base_out = base_in + 2 * d
        base_vec = base_out + 2 * ff
        for j in range(4):
            grad = acc_o[0:d, :] if j == 3 else acc_qkv[0:d, j * d : (j + 1) * d]
            merged = grad + attn_m[t, j]
            attn_m[t, j] = merged
            left[:, pl.ds(pl.multiple_of((t * 4 + j) * d, 128), d)] = left_rows(attn_start[t, j], merged)
        merged = acc_in[0:d, :] + in_m[t]
        in_m[t] = merged
        left[:, pl.ds(pl.multiple_of(base_in + t * d, 128), d)] = left_rows(in_start[t], merged)
        merged = acc_out[0:ff, :] + out_m[t]
        out_m[t] = merged
        left[:, pl.ds(pl.multiple_of(base_out + t * ff, 128), ff)] = left_rows(out_start[t], merged)
        sums = mm_nt(jnp.ones((8, 128), F32), acc_gain[...], HIGHEST)

        def vectors():
            yield sums[0:1, 0:d]
            yield sums[0:1, d : 2 * d]
            yield acc_qkv[d : d + 1, 0:d]
            yield acc_qkv[d : d + 1, 2 * d : 3 * d]
            yield acc_o[d : d + 1, :]
            yield sums[0:1, 2 * d : 3 * d]
            yield acc_out[ff : ff + 1, :]
            yield sums[0:1, 3 * d : 4 * d]
            for c in range(ff // d):
                yield acc_in[d : d + 1, c * d : (c + 1) * d]

        for tower in range(2):

            @pl.when(t == tower)
            def _(tower=tower):
                for v, vector in enumerate(vectors()):
                    at = tower * 12 + v
                    left[at // 3 : at // 3 + 1, base_vec + (at % 3) * d : base_vec + (at % 3 + 1) * d] = vector

    @pl.when(i == last)
    def _():
        part_halves(own_core(), left, left_mine, left_other)


def backward(nqs, nps, gp, saved, low_weights, gains, errors, starts):
    steps = nqs + nps
    nqu, npu = nqs * GROUP, nps * GROUP
    span = GROUP * TOK
    d, ff = errors[1].shape[2:]
    heads = d // HEAD
    width = 8 * d + 2 * d + 2 * ff + 3 * d
    direct = pl.BlockSpec(memory_space=pltpu.VMEM)
    far = pl.BlockSpec(memory_space=pl.ANY)
    return pl.pallas_call(
        functools.partial(backward_kernel, nqs),
        grid=(steps,),
        in_specs=[direct] * (len(saved) + 6) + [far] * 3 + [direct] * 3,
        out_specs=[
            pl.BlockSpec((GROUP, TOK, d), lambda i: (jnp.minimum(i, nqs - 1), 0, 0)),
            pl.BlockSpec((GROUP, TOK, d), lambda i: (jnp.maximum(i - nqs, 0), 0, 0)),
        ]
        + [direct] * 5,
        out_shape=[
            jax.ShapeDtypeStruct((nqu, TOK, d), F32),
            jax.ShapeDtypeStruct((npu, TOK, d), F32),
            pltpu.VMEM((2, 4, d, d), F32),
            pltpu.VMEM((2, d, ff), F32),
            pltpu.VMEM((2, ff, d), F32),
            jax.ShapeDtypeStruct((8, width // 2), F32),
            jax.ShapeDtypeStruct((8, width // 2), F32),
        ],
        scratch_shapes=[
            pltpu.VMEM((8, width), F32),
            pltpu.VMEM((2 * d, 128), F32),
            pltpu.VMEM((GROUP, d, heads * TOK), BF16),
            pltpu.VMEM((GROUP, heads, TOK, TOK), F32),
            pltpu.VMEM((GROUP, heads, TOK, TOK), BF16),
            pltpu.VMEM((3 * d, span), BF16),
            pltpu.VMEM((d + ONES, 3 * d), F32),
            pltpu.VMEM((d + ONES, d), F32),
            pltpu.VMEM((d + ONES, ff), F32),
            pltpu.VMEM((ff + ONES, d), F32),
            pltpu.VMEM((4 * d, 128), F32),
            pltpu.SemaphoreType.DMA((2, 3)),
        ],
        compiler_params=pltpu.CompilerParams(vmem_limit_bytes=BACKWARD_VMEM),
        name="backward",
    )(gp, *saved, *low_weights, gains, *errors, *starts)


def right_kernel(left_mine, left_other, attn_m, in_m, out_m, _, basis, right_mine, right_other, vector, left, right):
    d, ff = in_m.shape[1:]
    core = own_core()
    join_halves(core, left, left_mine, left_other)
    vector[...] = left[:, 10 * d + 2 * ff :]
    places = [(j * d, d) for j in range(8)] + [(8 * d + t * d, d) for t in range(2)] + [(10 * d + t * ff, ff) for t in range(2)]
    blocks = [left[:, at : at + size] for at, size in places]
    for j in range(8):
        for b, block in enumerate(blocks):
            order = lax.broadcasted_iota(jnp.int32, (8, 1), 0)
            column = block[j : j + 1, :]
            dots = jnp.sum(block * column, axis=1, keepdims=True)
            scale = lax.rsqrt(dots[j : j + 1, :] + 1e-06)
            unit = column * scale
            step = jnp.where(order > j, dots * scale, 0.0)
            blocks[b] = jnp.where(order == j, unit, block - step * unit)
    for (at, size), block in zip(places, blocks):
        basis[:, at : at + size] = block
    for j in range(8):
        right[:, j * d : (j + 1) * d] = right_rows(blocks[j], attn_m[j // 4, j % 4])
    for t in range(2):
        right[:, 8 * d + t * ff : 8 * d + (t + 1) * ff] = right_rows(blocks[8 + t], in_m[t])
        right[:, 8 * d + 2 * ff + t * d : 8 * d + 2 * ff + (t + 1) * d] = right_rows(blocks[10 + t], out_m[t])
    part_halves(core, right, right_mine, right_other)


def right_factors(left_mine, left_other, attn_m, in_m, out_m, earlier):
    d, ff = in_m.shape[1:]
    vmem = pl.BlockSpec(memory_space=pltpu.VMEM)
    width = 10 * d + 2 * ff
    rows = functools.partial(jax.ShapeDtypeStruct, dtype=F32)
    return pl.pallas_call(
        right_kernel,
        in_specs=[vmem] * 6,
        out_specs=[vmem] * 4,
        out_shape=[rows((8, width)), rows((8, width // 2)), rows((8, width // 2)), rows((8, 3 * d))],
        scratch_shapes=[pltpu.VMEM((8, width + 3 * d), F32), pltpu.VMEM((8, width), F32)],
        compiler_params=pltpu.CompilerParams(vmem_limit_bytes=12 << 20),
        name="right",
    )(left_mine, left_other, attn_m, in_m, out_m, earlier)


def update_kernel(
    replicas, basis, right_mine, right_other, vector, gains, biases, gain_mom, bias_mom,
    attn_m, in_m, out_m, attn, w_in, w_out, attn_mom, in_mom, out_mom,
    attn_new, in_new, out_new, attn_mom_new, in_mom_new, out_mom_new, attn_err, in_err, out_err,
    gains_new, biases_new, gain_mom_new, bias_mom_new, attn_factor, in_factor, out_factor, norm_out,
    right, clip_s,
):
    i = pl.program_id(0)
    d = attn.shape[2]
    ff = (right.shape[1] - 10 * d) // 2
    t, c = i // 4, i % 4

    @pl.when(i == 0)
    def _():
        join_halves(own_core(), right, right_mine, right_other)
        for j in range(8):
            attn_factor[j // 4, j % 4] = right[:, j * d : (j + 1) * d]
        for s in range(2):
            in_factor[s] = right[:, 8 * d + s * ff : 8 * d + (s + 1) * ff]
            out_factor[s] = right[:, 8 * d + 2 * ff + s * d : 8 * d + 2 * ff + (s + 1) * d]
        places = [((j * d, d), (j * d, d)) for j in range(8)]
        places += [((8 * d + s * d, d), (8 * d + s * ff, ff)) for s in range(2)]
        places += [((10 * d + s * ff, ff), (8 * d + 2 * ff + s * d, d)) for s in range(2)]
        total = jnp.zeros((8, 8), F32)
        for (b_at, b_size), (r_at, r_size) in places:
            b = basis[:, b_at : b_at + b_size]
            r = right[:, r_at : r_at + r_size]
            total = total + mm_nt(b, b, HIGHEST) * mm_nt(r, r, HIGHEST)
        sums = vector[...]
        square = jnp.sum(jnp.sum(total, axis=1, keepdims=True), axis=0, keepdims=True)
        square = square + jnp.sum(jnp.sum(sums * sums, axis=1, keepdims=True), axis=0, keepdims=True)
        norm = jnp.sqrt(jnp.broadcast_to(square, (8, 128)))
        norm_out[0] = norm[0, 0]
        clip_s[...] = jnp.minimum(1.0, CLIP_NORM / norm)
        held = clip_s[0:1, 0:1]
        for s in range(2):
            for v in range(12):
                at = s * 12 + v
                reduced = vector[at // 3 : at // 3 + 1, (at % 3) * d : (at % 3 + 1) * d]
                if v < 2:
                    moved = MOMENTUM_DECAY * gain_mom[s, v : v + 1, :] + held * reduced
                    gain_mom_new[s, v : v + 1, :] = moved
                    gains_new[s, v : v + 1, :] = gains[s, v : v + 1, :] - LEARNING_RATE * moved
                else:
                    over = slice((v - 2) * d, (v - 1) * d)
                    moved = MOMENTUM_DECAY * bias_mom[s : s + 1, over] + held * reduced
                    bias_mom_new[s : s + 1, over] = moved
                    biases_new[s : s + 1, over] = biases[s : s + 1, over] - LEARNING_RATE * moved

    clip = clip_s[0:1, 0:1]

    def step(b_at, r_at, merged, weight, moment, weight_new, moment_new, error):
        b1, b2, b3 = split_three(basis[:, pl.ds(pl.multiple_of(b_at, 128), d)])
        r1, r2, r3 = split_three(right[:, pl.ds(pl.multiple_of(r_at, 128), d)])
        approx = mm_tn(jnp.concatenate([b1, b1, b2, b1, b2, b3], axis=0), jnp.concatenate([r1, r2, r1, r3, r2, r1], axis=0))
        moved = MOMENTUM_DECAY * moment + clip * approx
        moment_new[...] = moved.reshape(moment_new.shape)
        weight_new[...] = (weight - LEARNING_RATE * moved).reshape(weight_new.shape)
        error[...] = (merged - approx * (1.0 / replicas)).reshape(error.shape)

    step(i * d, i * d, attn_m[0, 0], attn[0, 0], attn_mom[0, 0], attn_new, attn_mom_new, attn_err)
    step((8 + t) * d, 8 * d + t * ff + c * d, in_m[0], w_in[0], in_mom[0], in_new, in_mom_new, in_err)
    step(10 * d + t * ff + c * d, 8 * d + 2 * ff + t * d, out_m[0], w_out[0], out_mom[0], out_new, out_mom_new, out_err)


def update(replicas, basis, right_mine, right_other, vector, gains, biases, gain_mom, bias_mom, merged, weights, moments):
    d, ff = weights[1].shape[1:]
    a_spec = pl.BlockSpec((1, 1, d, d), lambda i: (i // 4, i % 4, 0, 0))
    i_spec = pl.BlockSpec((1, d, d), lambda i: (i // 4, 0, i % 4))
    o_spec = pl.BlockSpec((1, d, d), lambda i: (i // 4, i % 4, 0))
    ae_spec = pl.BlockSpec((1, 1, 1, d, d), lambda i: (0, i // 4, i % 4, 0, 0))
    ie_spec = pl.BlockSpec((1, 1, d, d), lambda i: (0, i // 4, 0, i % 4))
    oe_spec = pl.BlockSpec((1, 1, d, d), lambda i: (0, i // 4, i % 4, 0))
    rows = functools.partial(jax.ShapeDtypeStruct, dtype=F32)
    small = (basis, right_mine, right_other, vector, gains, biases, gain_mom, bias_mom)
    finals = [gains.shape, biases.shape] * 2 + [(2, 4, 8, d), (2, 8, ff), (2, 8, d)]
    return pl.pallas_call(
        functools.partial(update_kernel, replicas),
        grid=(8,),
        in_specs=[whole_spec(*a.shape) for a in small] + [a_spec, i_spec, o_spec] * 3,
        out_specs=[a_spec, i_spec, o_spec] * 2
        + [ae_spec, ie_spec, oe_spec]
        + [whole_spec(*shape) for shape in finals]
        + [pl.BlockSpec(memory_space=pltpu.SMEM)],
        out_shape=[rows(a.shape) for a in weights * 2]
        + [rows((1,) + a.shape) for a in weights]
        + [rows(shape) for shape in finals]
        + [rows((1,))],
        scratch_shapes=[pltpu.VMEM(basis.shape, F32), pltpu.VMEM((8, 128), F32)],
        compiler_params=pltpu.CompilerParams(vmem_limit_bytes=14 << 20),
        name="update",
    )(*small, *merged, *weights, *moments)


def in_vmem(*arrays):
    return tuple(pltpu.with_memory_space_constraint(a, pltpu.VMEM) for a in arrays)


def hold_kernel(count, _, *refs):
    sources, targets, sems = refs[:count], refs[count : 2 * count], refs[2 * count]
    copies = [pltpu.make_async_copy(source, target, sems.at[k]) for k, (source, target) in enumerate(zip(sources, targets))]
    for copy in copies:
        copy.start()
    for copy in copies:
        copy.wait()


def hold(after, arrays):
    size = sum(4 * math.prod(a.shape) for a in arrays)
    return pl.pallas_call(
        functools.partial(hold_kernel, len(arrays)),
        in_specs=[pl.BlockSpec(memory_space=pl.ANY)] * (1 + len(arrays)),
        out_specs=[pl.BlockSpec(memory_space=pltpu.VMEM)] * len(arrays),
        out_shape=[pltpu.VMEM(a.shape, a.dtype) for a in arrays],
        scratch_shapes=[pltpu.SemaphoreType.DMA((len(arrays),))],
        compiler_params=pltpu.CompilerParams(vmem_limit_bytes=1 << 20),
        cost_estimate=pl.CostEstimate(flops=0, bytes_accessed=2 * size, transcendentals=0),
        name="hold",
    )(after, *(pltpu.with_memory_space_constraint(a, pltpu.HBM) for a in arrays))


def swap_with(x, axis, mask):
    return lax.ppermute(x, axis, [(i, i ^ mask) for i in range(lax.axis_size(axis))])


def chip_steps():
    size = lax.axis_size("dp")
    if size == 8:
        return [("dp", (2, 4, 6))]
    return [("dp", (1 << b,)) for b in range(1, size.bit_length() - 1)]


def outer_step():
    return ("outer", tuple(range(1, lax.axis_size("outer"))))


def gather_blocks(x):
    for axis, masks in [outer_step()] + chip_steps():
        x = jnp.concatenate([x] + [swap_with(x, axis, mask) for mask in masks], axis=0)
    return x, swap_with(x, "dp", 1)


def sum_halves(mine, other, beside=()):
    held = []
    mine = mine + swap_with(other, "dp", 1)
    for axis, masks in chip_steps() + [outer_step()]:
        sent = mine.astype(SEND)
        if beside and axis == "outer":
            held = in_vmem(*hold(sent, beside))
        mine = sent.astype(F32)
        for got in [swap_with(sent, axis, mask) for mask in masks]:
            mine = mine + got.astype(F32)
    return mine, swap_with(mine, "dp", 1), *held


def per_device(
    questions, passages, q_lengths, p_lengths, positives, pos_counts, attn, w_in, w_out, gains, biases, attn_mom, w_in_mom,
    w_out_mom, gain_mom, bias_mom, attn_err, w_in_err, w_out_err, attn_start, w_in_start, w_out_start,
):
    devices = lax.axis_size("dp") * lax.axis_size("outer")
    d, ff = w_in.shape[1:]
    xq = questions.reshape(-1, TOK, d)
    xp = passages.reshape(-1, TOK, d)
    nqu, npu = xq.shape[0], xp.shape[0]
    *saved, wqkv, wo, win, wout, pooled, units = forward(
        q_lengths, p_lengths, xq, xp, attn, w_in, w_out, gains, biases, positives.T, pos_counts.reshape(1, -1)
    )
    dp, outer = lax.axis_size("dp"), lax.axis_size("outer")
    near, far = gather_blocks(units)
    loss, gp = contrast(nqu, npu, positives.shape[1], dp, outer, q_lengths, p_lengths, *in_vmem(near, far, pooled))
    starts = [jnp.swapaxes(start, -1, -2) for start in (attn_start, w_in_start, w_out_start)]
    qgrad, pgrad, attn_m, in_m, out_m, *left = backward(
        nqu // GROUP, npu // GROUP, *in_vmem(gp), in_vmem(*saved), in_vmem(wqkv, wo, win, wout), gains,
        (attn_err, w_in_err, w_out_err), starts,
    )
    weights = (attn, w_in, w_out)
    moments = (attn_mom, w_in_mom, w_out_mom)
    merged = in_vmem(attn_m, in_m, out_m)
    *left, mom_a, mom_b, mom_c = sum_halves(*left, beside=moments)
    basis, *right, vector = right_factors(*left, *merged, mom_a)
    held = in_vmem(*weights) + (mom_a, mom_b, mom_c)
    *new, attn_factor, in_factor, out_factor, norm = update(
        devices, basis, *sum_halves(*right), vector, gains, biases, gain_mom, bias_mom,
        merged, held[:3], held[3:],
    )
    weights_new, moments_new, errors_new, vectors_new = new[:3], new[3:6], new[6:9], new[9:]
    factors = [jnp.swapaxes(factor, -1, -2) for factor in (attn_factor, in_factor, out_factor)]
    return (
        loss.reshape(-1), qgrad.reshape(questions.shape), pgrad.reshape(passages.shape),
        *weights_new, *vectors_new[:2], *moments_new, *vectors_new[2:], *errors_new, *factors, norm.reshape(()),
    )


def solution(mesh):
    split = ("dp", "outer")
    share = P(split)
    return jax.shard_map(
        per_device,
        mesh=mesh,
        in_specs=(share,) * 6 + (P(),) * 10 + (share,) * 3 + (P(),) * 3,
        out_specs=(share,) * 3 + (P(),) * 10 + (share,) * 3 + (P(),) * 4,
        check_vma=False,
    )
```

time: 134 us -> 124 us (0.925)
  Pallas kernels: 79.9 us -> 69.5 us
  waiting for transfers between devices: 27 us -> 25.4 us
    all_to_all x1 -> x0, waiting for transfers between devices: 10.8 us -> none  [per_device(): units = lax.all_to_all(units, AXES, 0, 0)]
    ppermute x16 -> x23, waiting for transfers between devices: 16.2 us -> 25.4 us  [swap_with(): lax.ppermute(x, axis, [(i, i ^ mask) for i in range(lax.axis_size(axis))])]
    ppermute x16 -> x23, starting transfers between devices: 17.3 us -> 26.1 us  [swap_with(): lax.ppermute(x, axis, [(i, i ^ mask) for i in range(lax.axis_size(axis))])]
    pallas_call x1, Pallas kernels: 34 us -> 26.4 us  [forward(): pl.pallas_call(functools.partial(forward_kernel, nqs), grid_spec=pltpu.Pr...]
    all_to_all x1 -> x0, starting transfers between devices: 7.51 us -> none  [per_device(): units = lax.all_to_all(units, AXES, 0, 0)]
    pallas_call x4 -> x5, Pallas kernels: 45.9 us -> 43.2 us  [the longest x1 27.4 us: backward(): pl.pallas_call(functools.partial(backward_kernel, nqs), grid=(steps,), in...]
  transfers between devices with their start and end apart: 17 -> 23, of which waited for: 16 -> 19; matrix products, arithmetic and copies ran while one was open for 0% -> 1% of each run, Pallas kernels for 0% -> 2%
where the time goes in v4:
time: 124 us
  Pallas kernels  69.5 us (56%)
  starting transfers between devices  26.1 us (21%)
  waiting for transfers between devices  25.4 us (20%)
    pallas_call x1, Pallas kernels, backward(): pl.pallas_call(functools.partial(backward_kernel, nqs), grid=(steps,), in...  27.4 us
    pallas_call x1, Pallas kernels, forward(): pl.pallas_call(functools.partial(forward_kernel, nqs), grid_spec=pltpu.Pr...  26.4 us
    ppermute x23, starting transfers between devices, swap_with(): lax.ppermute(x, axis, [(i, i ^ mask) for i in range(lax.axis_size(axis))])  26.1 us
    ppermute x23, waiting for transfers between devices, swap_with(): lax.ppermute(x, axis, [(i, i ^ mask) for i in range(lax.axis_size(axis))])  25.4 us
    pallas_call x1, Pallas kernels, update(): pl.pallas_call(functools.partial(update_kernel, replicas), grid=(8,), in_...  8.81 us
    pallas_call x1, Pallas kernels, hold(): pl.pallas_call(functools.partial(hold_kernel, len(arrays)), in_specs=[pl....  2.89 us
  transfers between devices with their start and end apart: 23, of which 19 were waited for; matrix products, arithmetic and copies ran while one was open for 1% of the time, Pallas kernels for 2%

profile of v4, /device:TPU:0, one launch (start us, length us, event | category | flops | bytes accessed | tf_op | source)
XLA Modules:
  0.0 123.9 jit_solution(10873243056820711702)
XLA Ops:
  0.7 26.4 %forward.1 = (bf16[5,272,512]{2,1,0:T(8,128)(2,1)S(1)}, bf16[5,512,512]{2,1,0:T(8,128)(2,1)S(1)}, bf16[5,512,256]{2,1,0:T(8,128)(2,1)S(1)}, bf16[5,2,4,256,256]{...) custom-call(s32[8]{0:T(128)} %qlen.3, s32[8]{0:T(128)} %plen.3, ...), custom_call_target="tpu_custom_call" | custom-call | tf_op jit(solution)/shard_map/forward/pallas_call | solution.py:324
  27.0 3.0 %collective-permute-start = (bf16[1,40,128]{2,1,0:T(8,128)(2,1)}, bf16[1,40,128]{2,1,0:T(8,128)(2,1)S(1)}, u32[]{:S(2)}, u32[]{:S(2)}) collective-permute-start(bf16[1,40,128]{2,1,0:T(8,128)(2,1)} %get-tuple-element.72), channel_id=1, source_target_pairs={{0,1},{1,0},{2,3},{3,2},{4,5},{5,4},{6,7},{7,6},{8,9},{9,8},{10,11... | collective-permute-start | bytes 30728 | tf_op jit(solution)/shard_map/ppermute | solution.py:834
  30.1 2.6 %collective-permute-start.1 = (bf16[1,40,128]{2,1,0:T(8,128)(2,1)}, bf16[1,40,128]{2,1,0:T(8,128)(2,1)S(1)}, u32[]{:S(2)}, u32[]{:S(2)}) collective-permute-start(bf16[1,40,128]{2,1,0:T(8,128)(2,1)} %get-tuple-element.72), channel_id=1, source_target_pairs={{0,2},{1,3},{2,0},{3,1},{4,6},{5,7},{6,4},{7,5},{8,10},{9,11},{10,... | collective-permute-start | bytes 30728 | tf_op jit(solution)/shard_map/ppermute | solution.py:834
  32.7 0.8 constant_dynamic-update-slice_fusion.3
  33.5 1.4 %collective-permute-done.1 = bf16[1,40,128]{2,1,0:T(8,128)(2,1)S(1)} collective-permute-done((bf16[1,40,128]{2,1,0:T(8,128)(2,1)}, bf16[1,40,128]{2,1,0:T(8,128)(2,1)S(1)}, u32[]{:S(2)}, u32[]{:S(2)}) %collective-permute-start.1) | collective-permute-done | bytes 10272 | tf_op jit(solution)/shard_map/ppermute | solution.py:834
  34.9 3.5 %collective-permute-done.2 = bf16[1,40,128]{2,1,0:T(8,128)(2,1)S(1)} collective-permute-done((bf16[1,40,128]{2,1,0:T(8,128)(2,1)}, bf16[1,40,128]{2,1,0:T(8,128)(2,1)S(1)}, u32[]{:S(2)}, u32[]{:S(2)}) %collective-permute-start.2) | collective-permute-done | bytes 10272 | tf_op jit(solution)/shard_map/ppermute | solution.py:834
  38.4 1.5 %collective-permute-start.3 = (bf16[4,40,128]{2,1,0:T(8,128)(2,1)S(1)}, bf16[4,40,128]{2,1,0:T(8,128)(2,1)S(1)}, u32[]{:S(2)}, u32[]{:S(2)}) collective-permute-start(bf16[4,40,128]{2,1,0:T(8,128)(2,1)S(1)} %get-tuple-element.124), channel_id=1, source_target_pairs={{0,8},{4,12},{8,0},{12,4},{16,24},{20,28},{24,16},{28,20},{1,9},{5... | collective-permute-start | bytes 122888 | tf_op jit(solution)/shard_map/ppermute | solution.py:834
  39.9 1.5 %collective-permute-start.4 = (bf16[4,40,128]{2,1,0:T(8,128)(2,1)S(1)}, bf16[4,40,128]{2,1,0:T(8,128)(2,1)S(1)}, u32[]{:S(2)}, u32[]{:S(2)}) collective-permute-start(bf16[4,40,128]{2,1,0:T(8,128)(2,1)S(1)} %get-tuple-element.124), channel_id=1, source_target_pairs={{0,16},{4,20},{8,24},{12,28},{16,0},{20,4},{24,8},{28,12},{1,17},{... | collective-permute-start | bytes 122888 | tf_op jit(solution)/shard_map/ppermute | solution.py:834
  41.4 0.5 collective-permute-start.5
  41.9 0.5 collective-permute-done.3
  42.4 1.5 %collective-permute-done.4 = bf16[4,40,128]{2,1,0:T(8,128)(2,1)S(1)} collective-permute-done((bf16[4,40,128]{2,1,0:T(8,128)(2,1)S(1)}, bf16[4,40,128]{2,1,0:T(8,128)(2,1)S(1)}, u32[]{:S(2)}, u32[]{:S(2)}) %collective-permute-start.4) | collective-permute-done | bytes 40992 | tf_op jit(solution)/shard_map/ppermute | solution.py:834
  43.9 2.4 %collective-permute-done.5 = bf16[4,40,128]{2,1,0:T(8,128)(2,1)S(1)} collective-permute-done((bf16[4,40,128]{2,1,0:T(8,128)(2,1)S(1)}, bf16[4,40,128]{2,1,0:T(8,128)(2,1)S(1)}, u32[]{:S(2)}, u32[]{:S(2)}) %collective-permute-start.5) | collective-permute-done | bytes 40992 | tf_op jit(solution)/shard_map/ppermute | solution.py:834
  46.3 0.1 collective-permute-start.6
  46.4 1.4 %collective-permute-done.6.far = bf16[16,40,128]{2,1,0:T(8,128)(2,1)S(1)} collective-permute-done((bf16[16,40,128]{2,1,0:T(8,128)(2,1)S(1)}, bf16[16,40,128]{2,1,0:T(8,128)(2,1)S(1)}, u32[]{:S(2)}, u32[]{:S(2)}) %collective-permute-start.6) | collective-permute-done | bytes 163872 | tf_op jit(solution)/shard_map/ppermute | solution.py:834
  47.8 2.0 %contrast.1 = (f32[1,8]{1,0:T(1,128)}, bf16[10,48,256]{2,1,0:T(8,128)(2,1)S(1)}) custom-call(s32[8]{0:T(128)S(1)} %copy-done.7, s32[8]{0:T(128)S(1)} %copy-done.8, bf16[16,40,128]{2,1,0:T(8,128)(2,1)S(1)} %constant_dynamic-update-slice_fusion.4.near, bf16[16,40,128]{2,1,0:T(8,128)(2,1)S(1)} %collective-permute-done.6.far, f32[16,256]{1,0:T(8,128)S(1)} %get-tuple-element.73.pooled), custom_call_target="tpu_custom_call" | custom-call | tf_op jit(solution)/shard_map/contrast/pallas_call | solution.py:420
  49.8 27.4 %backward.1 = (f32[2,256,256]{2,1,0:T(8,128)}, f32[8,256,256]{2,1,0:T(8,128)}, f32[2,4,256,256]{3,2,1,0:T(8,128)S(1)}, f32[2,256,1024]{2,1,0:T(8,128)S(1)}, f32[...) custom-call(bf16[10,48,256]{2,1,0:T(8,128)(2,1)S(1)} %get-tuple-element.75.gp, ...), custom_call_target="tpu_custom_call" | custom-call | tf_op jit(solution)/shard_map/backward/pallas_call | solution.py:633
  77.2 0.2 collective-permute-start.7
  77.4 1.3 %collective-permute-done.7 = f32[8,2688]{1,0:T(8,128)S(1)} collective-permute-done((f32[8,2688]{1,0:T(8,128)}, f32[8,2688]{1,0:T(8,128)S(1)}, u32[]{:S(2)}, u32[]{:S(2)}) %collective-permute-start.7) | collective-permute-done | bytes 86048 | tf_op jit(solution)/shard_map/ppermute | solution.py:834
  78.7 0.9 add_convert_fusion.1
  79.6 0.5 collective-permute-start.10
  80.2 1.5 %collective-permute-start.9 = (bf16[8,2688]{1,0:T(8,128)(2,1)S(1)}, bf16[8,2688]{1,0:T(8,128)(2,1)S(1)}, u32[]{:S(2)}, u32[]{:S(2)}) collective-permute-start(bf16[8,2688]{1,0:T(8,128)(2,1)S(1)} %add_convert_fusion.1), channel_id=1, source_target_pairs={{0,16},{4,20},{8,24},{12,28},{16,0},{20,4},{24,8},{28,12},{1,17},{... | collective-permute-start | bytes 129032 | tf_op jit(solution)/shard_map/ppermute | solution.py:834
  81.7 1.5 %collective-permute-start.8 = (bf16[8,2688]{1,0:T(8,128)(2,1)S(1)}, bf16[8,2688]{1,0:T(8,128)(2,1)S(1)}, u32[]{:S(2)}, u32[]{:S(2)}) collective-permute-start(bf16[8,2688]{1,0:T(8,128)(2,1)S(1)} %add_convert_fusion.1), channel_id=1, source_target_pairs={{0,8},{4,12},{8,0},{12,4},{16,24},{20,28},{24,16},{28,20},{1,9},{5... | collective-permute-start | bytes 129032 | tf_op jit(solution)/shard_map/ppermute | solution.py:834
  83.2 1.6 %collective-permute-done.10 = bf16[8,2688]{1,0:T(8,128)(2,1)S(1)} collective-permute-done((bf16[8,2688]{1,0:T(8,128)(2,1)S(1)}, bf16[8,2688]{1,0:T(8,128)(2,1)S(1)}, u32[]{:S(2)}, u32[]{:S(2)}) %collective-permute-start.10) | collective-permute-done | bytes 43040 | tf_op jit(solution)/shard_map/ppermute | solution.py:834
  84.7 1.0 collective-permute-done.8
  85.7 0.3 collective-permute-start.13
  86.0 4.2 %collective-permute-start.11 = (bf16[8,2688]{1,0:T(8,128)(2,1)S(1)}, bf16[8,2688]{1,0:T(8,128)(2,1)S(1)}, u32[]{:S(2)}, u32[]{:S(2)}) collective-permute-start(bf16[8,2688]{1,0:T(8,128)(2,1)S(1)} %add_convert_fusion._), channel_id=1, source_target_pairs={{0,1},{1,0},{2,3},{3,2},{4,5},{5,4},{6,7},{7,6},{8,9},{9,8},{10,11... | collective-permute-start | bytes 129032 | tf_op jit(solution)/shard_map/ppermute | solution.py:834
  90.2 1.4 %collective-permute-done.13 = bf16[8,2688]{1,0:T(8,128)(2,1)S(1)} collective-permute-done((bf16[8,2688]{1,0:T(8,128)(2,1)S(1)}, bf16[8,2688]{1,0:T(8,128)(2,1)S(1)}, u32[]{:S(2)}, u32[]{:S(2)}) %collective-permute-start.13) | collective-permute-done | bytes 43040 | tf_op jit(solution)/shard_map/ppermute | solution.py:834
  91.6 0.6 collective-permute-done.11
  92.2 0.1 collective-permute-start.14
  92.3 2.9 %hold.1 = (f32[2,4,256,256]{3,2,1,0:T(8,128)S(1)}, f32[2,256,1024]{2,1,0:T(8,128)S(1)}, f32[2,1024,256]{2,1,0:T(8,128)S(1)}) custom-call(bf16[8,2688]{1,0:T(8,128)(2,1)S(1)} %add_convert_fusion._, f32[2,4,256,256]{3,2,1,0:T(8,128)} %refs_0_.1, f32[2,256,1024]{2,1,0:T(8,128)} %refs_1_.1, f32[2,1024,256]{2,1,0:T(8,128)} %refs_2_.1), custom_call_target="tpu_custom_call" | custom-call | bytes 12582912 | tf_op jit(solution)/shard_map/hold/pallas_call | solution.py:821
  95.3 2.1 %right.1 = (f32[8,4608]{1,0:T(8,128)S(1)}, f32[8,2304]{1,0:T(8,128)S(1)}, f32[8,2304]{1,0:T(8,128)S(1)}, f32[8,768]{1,0:T(8,128)S(1)}) custom-call(f32[8,2688]{1,0:T(8,128)S(1)} %convert_add_fusion.left_mine, f32[8,2688]{1,0:T(8,128)S(1)} %collective-permute-done.14.left_other, f32[2,4,256,256]{3,2,1,0:T(8,128)S(1)} %get-tuple-element.97.attn_m, ...), custom_call_target="tpu_custom_call" | custom-call | tf_op jit(solution)/shard_map/right/pallas_call | solution.py:701
  97.4 0.6 collective-permute-start.15
  98.0 0.9 collective-permute-done.15
  98.9 1.5 %collective-permute-start.18 = (bf16[8,2304]{1,0:T(8,128)(2,1)S(1)}, bf16[8,2304]{1,0:T(8,128)(2,1)S(1)}, u32[]{:S(2)}, u32[]{:S(2)}) collective-permute-start(bf16[8,2304]{1,0:T(8,128)(2,1)S(1)} %add_convert_fusion.3), channel_id=1, source_target_pairs={{0,24},{4,28},{8,16},{12,20},{16,8},{20,12},{24,0},{28,4},{1,25},{... | collective-permute-start | bytes 110600 | tf_op jit(solution)/shard_map/ppermute | solution.py:834
  100.4 1.5 %collective-permute-start.17 = (bf16[8,2304]{1,0:T(8,128)(2,1)S(1)}, bf16[8,2304]{1,0:T(8,128)(2,1)S(1)}, u32[]{:S(2)}, u32[]{:S(2)}) collective-permute-start(bf16[8,2304]{1,0:T(8,128)(2,1)S(1)} %add_convert_fusion.3), channel_id=1, source_target_pairs={{0,16},{4,20},{8,24},{12,28},{16,0},{20,4},{24,8},{28,12},{1,17},{... | collective-permute-start | bytes 110600 | tf_op jit(solution)/shard_map/ppermute | solution.py:834
  101.9 0.5 collective-permute-start.16
  102.4 1.4 %collective-permute-done.18 = bf16[8,2304]{1,0:T(8,128)(2,1)S(1)} collective-permute-done((bf16[8,2304]{1,0:T(8,128)(2,1)S(1)}, bf16[8,2304]{1,0:T(8,128)(2,1)S(1)}, u32[]{:S(2)}, u32[]{:S(2)}) %collective-permute-start.18) | collective-permute-done | bytes 36896 | tf_op jit(solution)/shard_map/ppermute | solution.py:834
  103.8 0.5 collective-permute-done.17
  104.4 1.5 %collective-permute-done.16 = bf16[8,2304]{1,0:T(8,128)(2,1)S(1)} collective-permute-done((bf16[8,2304]{1,0:T(8,128)(2,1)S(1)}, bf16[8,2304]{1,0:T(8,128)(2,1)S(1)}, u32[]{:S(2)}, u32[]{:S(2)}) %collective-permute-start.16) | collective-permute-done | bytes 36896 | tf_op jit(solution)/shard_map/ppermute | solution.py:834
  105.9 2.4 %collective-permute-start.21 = (bf16[8,2304]{1,0:T(8,128)(2,1)S(1)}, bf16[8,2304]{1,0:T(8,128)(2,1)S(1)}, u32[]{:S(2)}, u32[]{:S(2)}) collective-permute-start(bf16[8,2304]{1,0:T(8,128)(2,1)S(1)} %add_convert_fusion.2), channel_id=1, source_target_pairs={{0,3},{1,2},{2,1},{3,0},{4,7},{5,6},{6,5},{7,4},{8,11},{9,10},{10,... | collective-permute-start | bytes 110600 | tf_op jit(solution)/shard_map/ppermute | solution.py:834
  108.3 1.1 collective-permute-start.20
  109.4 0.9 collective-permute-start.19
  110.3 1.7 %collective-permute-done.21 = bf16[8,2304]{1,0:T(8,128)(2,1)S(1)} collective-permute-done((bf16[8,2304]{1,0:T(8,128)(2,1)S(1)}, bf16[8,2304]{1,0:T(8,128)(2,1)S(1)}, u32[]{:S(2)}, u32[]{:S(2)}) %collective-permute-start.21) | collective-permute-done | bytes 36896 | tf_op jit(solution)/shard_map/ppermute | solution.py:834
  112.1 1.1 collective-permute-done.20
  113.2 0.4 collective-permute-done.19
  113.6 0.1 collective-permute-start.22
  113.7 1.3 %collective-permute-done.22.right_other = f32[8,2304]{1,0:T(8,128)S(1)} collective-permute-done((f32[8,2304]{1,0:T(8,128)S(1)}, f32[8,2304]{1,0:T(8,128)S(1)}, u32[]{:S(2)}, u32[]{:S(2)}) %collective-permute-start.22) | collective-permute-done | bytes 73760 | tf_op jit(solution)/shard_map/ppermute | solution.py:834
  115.0 8.8 %update.1 = (f32[2,4,256,256]{3,2,1,0:T(8,128)}, f32[2,256,1024]{2,1,0:T(8,128)}, f32[2,1024,256]{2,1,0:T(8,128)}, f32[2,4,256,256]{3,2,1,0:T(8,128)}, f32[2,256...) custom-call(f32[8,4608]{1,0:T(8,128)S(1)} %get-tuple-element.101.bas, ...), custom_call_target="tpu_custom_call" | custom-call | tf_op jit(solution)/shard_map/update/pallas_call | solution.py:788
  (35 shorter events, 0.2 us)
Async XLA Ops:
  0.7 47.1 %copy-start.7 = (s32[8]{0:T(128)S(1)}, s32[8]{0:T(128)}, u32[]{:S(2)}) copy-start(s32[8]{0:T(128)} %qlen.3) | copy-start | bytes 100
  0.7 47.1 %copy-start.8 = (s32[8]{0:T(128)S(1)}, s32[8]{0:T(128)}, u32[]{:S(2)}) copy-start(s32[8]{0:T(128)} %plen.3) | copy-start | bytes 100
  27.0 6.4 %collective-permute-start = (bf16[1,40,128]{2,1,0:T(8,128)(2,1)}, bf16[1,40,128]{2,1,0:T(8,128)(2,1)S(1)}, u32[]{:S(2)}, u32[]{:S(2)}) collective-permute-start(bf16[1,40,128]{2,1,0:T(8,128)(2,1)} %get-tuple-element.72), channel_id=1, source_target_pairs={{0,1},{1,0},{2,3},{3,2},{4,5},{5,4},{6,7},{7,6},{8,9},{9,8},{10,11... | collective-permute-start | bytes 30728 | tf_op jit(solution)/shard_map/ppermute | solution.py:834
  30.1 4.8 %collective-permute-start.1 = (bf16[1,40,128]{2,1,0:T(8,128)(2,1)}, bf16[1,40,128]{2,1,0:T(8,128)(2,1)S(1)}, u32[]{:S(2)}, u32[]{:S(2)}) collective-permute-start(bf16[1,40,128]{2,1,0:T(8,128)(2,1)} %get-tuple-element.72), channel_id=1, source_target_pairs={{0,2},{1,3},{2,0},{3,1},{4,6},{5,7},{6,4},{7,5},{8,10},{9,11},{10,... | collective-permute-start | bytes 30728 | tf_op jit(solution)/shard_map/ppermute | solution.py:834
  32.7 5.7 %collective-permute-start.2 = (bf16[1,40,128]{2,1,0:T(8,128)(2,1)}, bf16[1,40,128]{2,1,0:T(8,128)(2,1)S(1)}, u32[]{:S(2)}, u32[]{:S(2)}) collective-permute-start(bf16[1,40,128]{2,1,0:T(8,128)(2,1)} %get-tuple-element.72), channel_id=1, source_target_pairs={{0,3},{1,2},{2,1},{3,0},{4,7},{5,6},{6,5},{7,4},{8,11},{9,10},{10,... | collective-permute-start | bytes 30728 | tf_op jit(solution)/shard_map/ppermute | solution.py:834
  38.4 4.0 %collective-permute-start.3 = (bf16[4,40,128]{2,1,0:T(8,128)(2,1)S(1)}, bf16[4,40,128]{2,1,0:T(8,128)(2,1)S(1)}, u32[]{:S(2)}, u32[]{:S(2)}) collective-permute-start(bf16[4,40,128]{2,1,0:T(8,128)(2,1)S(1)} %get-tuple-element.124), channel_id=1, source_target_pairs={{0,8},{4,12},{8,0},{12,4},{16,24},{20,28},{24,16},{28,20},{1,9},{5... | collective-permute-start | bytes 122888 | tf_op jit(solution)/shard_map/ppermute | solution.py:834
  39.9 4.0 %collective-permute-start.4 = (bf16[4,40,128]{2,1,0:T(8,128)(2,1)S(1)}, bf16[4,40,128]{2,1,0:T(8,128)(2,1)S(1)}, u32[]{:S(2)}, u32[]{:S(2)}) collective-permute-start(bf16[4,40,128]{2,1,0:T(8,128)(2,1)S(1)} %get-tuple-element.124), channel_id=1, source_target_pairs={{0,16},{4,20},{8,24},{12,28},{16,0},{20,4},{24,8},{28,12},{1,17},{... | collective-permute-start | bytes 122888 | tf_op jit(solution)/shard_map/ppermute | solution.py:834
  41.4 4.9 %collective-permute-start.5 = (bf16[4,40,128]{2,1,0:T(8,128)(2,1)S(1)}, bf16[4,40,128]{2,1,0:T(8,128)(2,1)S(1)}, u32[]{:S(2)}, u32[]{:S(2)}) collective-permute-start(bf16[4,40,128]{2,1,0:T(8,128)(2,1)S(1)} %get-tuple-element.124), channel_id=1, source_target_pairs={{0,24},{4,28},{8,16},{12,20},{16,8},{20,12},{24,0},{28,4},{1,25},{... | collective-permute-start | bytes 122888 | tf_op jit(solution)/shard_map/ppermute | solution.py:834
  46.3 1.5 %collective-permute-start.6 = (bf16[16,40,128]{2,1,0:T(8,128)(2,1)S(1)}, bf16[16,40,128]{2,1,0:T(8,128)(2,1)S(1)}, u32[]{:S(2)}, u32[]{:S(2)}) collective-permute-start(bf16[16,40,128]{2,1,0:T(8,128)(2,1)S(1)} %constant_dynamic-update-slice_fusion.4.near), channel_id=1, source_target_pairs={{0,4},{4,0},{8,12},{12,8},{16,20},{20,16},{24,28},{28,24},{1,5},{5... | collective-permute-start | bytes 491528 | tf_op jit(solution)/shard_map/ppermute | solution.py:834
  77.2 1.6 %collective-permute-start.7 = (f32[8,2688]{1,0:T(8,128)}, f32[8,2688]{1,0:T(8,128)S(1)}, u32[]{:S(2)}, u32[]{:S(2)}) collective-permute-start(f32[8,2688]{1,0:T(8,128)} %get-tuple-element.96), channel_id=1, source_target_pairs={{0,4},{4,0},{8,12},{12,8},{16,20},{20,16},{24,28},{28,24},{1,5},{5... | collective-permute-start | bytes 258056 | tf_op jit(solution)/shard_map/ppermute | solution.py:834
  79.6 5.1 %collective-permute-start.10 = (bf16[8,2688]{1,0:T(8,128)(2,1)S(1)}, bf16[8,2688]{1,0:T(8,128)(2,1)S(1)}, u32[]{:S(2)}, u32[]{:S(2)}) collective-permute-start(bf16[8,2688]{1,0:T(8,128)(2,1)S(1)} %add_convert_fusion.1), channel_id=1, source_target_pairs={{0,24},{4,28},{8,16},{12,20},{16,8},{20,12},{24,0},{28,4},{1,25},{... | collective-permute-start | bytes 129032 | tf_op jit(solution)/shard_map/ppermute | solution.py:834
  80.2 4.6 %collective-permute-start.9 = (bf16[8,2688]{1,0:T(8,128)(2,1)S(1)}, bf16[8,2688]{1,0:T(8,128)(2,1)S(1)}, u32[]{:S(2)}, u32[]{:S(2)}) collective-permute-start(bf16[8,2688]{1,0:T(8,128)(2,1)S(1)} %add_convert_fusion.1), channel_id=1, source_target_pairs={{0,16},{4,20},{8,24},{12,28},{16,0},{20,4},{24,8},{28,12},{1,17},{... | collective-permute-start | bytes 129032 | tf_op jit(solution)/shard_map/ppermute | solution.py:834
  81.7 4.0 %collective-permute-start.8 = (bf16[8,2688]{1,0:T(8,128)(2,1)S(1)}, bf16[8,2688]{1,0:T(8,128)(2,1)S(1)}, u32[]{:S(2)}, u32[]{:S(2)}) collective-permute-start(bf16[8,2688]{1,0:T(8,128)(2,1)S(1)} %add_convert_fusion.1), channel_id=1, source_target_pairs={{0,8},{4,12},{8,0},{12,4},{16,24},{20,28},{24,16},{28,20},{1,9},{5... | collective-permute-start | bytes 129032 | tf_op jit(solution)/shard_map/ppermute | solution.py:834
  85.7 5.9 %collective-permute-start.13 = (bf16[8,2688]{1,0:T(8,128)(2,1)S(1)}, bf16[8,2688]{1,0:T(8,128)(2,1)S(1)}, u32[]{:S(2)}, u32[]{:S(2)}) collective-permute-start(bf16[8,2688]{1,0:T(8,128)(2,1)S(1)} %add_convert_fusion._), channel_id=1, source_target_pairs={{0,3},{1,2},{2,1},{3,0},{4,7},{5,6},{6,5},{7,4},{8,11},{9,10},{10,... | collective-permute-start | bytes 129032 | tf_op jit(solution)/shard_map/ppermute | solution.py:834
  86.0 5.6 %collective-permute-start.12 = (bf16[8,2688]{1,0:T(8,128)(2,1)S(1)}, bf16[8,2688]{1,0:T(8,128)(2,1)S(1)}, u32[]{:S(2)}, u32[]{:S(2)}) collective-permute-start(bf16[8,2688]{1,0:T(8,128)(2,1)S(1)} %add_convert_fusion._), channel_id=1, source_target_pairs={{0,2},{1,3},{2,0},{3,1},{4,6},{5,7},{6,4},{7,5},{8,10},{9,11},{10,... | collective-permute-start | bytes 129032 | tf_op jit(solution)/shard_map/ppermute | solution.py:834
  86.0 6.2 %collective-permute-start.11 = (bf16[8,2688]{1,0:T(8,128)(2,1)S(1)}, bf16[8,2688]{1,0:T(8,128)(2,1)S(1)}, u32[]{:S(2)}, u32[]{:S(2)}) collective-permute-start(bf16[8,2688]{1,0:T(8,128)(2,1)S(1)} %add_convert_fusion._), channel_id=1, source_target_pairs={{0,1},{1,0},{2,3},{3,2},{4,5},{5,4},{6,7},{7,6},{8,9},{9,8},{10,11... | collective-permute-start | bytes 129032 | tf_op jit(solution)/shard_map/ppermute | solution.py:834
  92.2 3.0 %collective-permute-start.14 = (f32[8,2688]{1,0:T(8,128)S(1)}, f32[8,2688]{1,0:T(8,128)S(1)}, u32[]{:S(2)}, u32[]{:S(2)}) collective-permute-start(f32[8,2688]{1,0:T(8,128)S(1)} %convert_add_fusion.left_mine), channel_id=1, source_target_pairs={{0,4},{4,0},{8,12},{12,8},{16,20},{20,16},{24,28},{28,24},{1,5},{5... | collective-permute-start | bytes 258056 | tf_op jit(solution)/shard_map/ppermute | solution.py:834
  95.2 19.7 %copy-start = (f32[2,4,256,256]{3,2,1,0:T(8,128)S(1)}, f32[2,4,256,256]{3,2,1,0:T(8,128)}, u32[]{:S(2)}) copy-start(f32[2,4,256,256]{3,2,1,0:T(8,128)} %attn.3) | copy-start | bytes 6291460
  95.2 19.7 %copy-start.1 = (f32[2,256,1024]{2,1,0:T(8,128)S(1)}, f32[2,256,1024]{2,1,0:T(8,128)}, u32[]{:S(2)}) copy-start(f32[2,256,1024]{2,1,0:T(8,128)} %w_in.3) | copy-start | bytes 6291460
  95.2 19.7 %copy-start.2 = (f32[2,1024,256]{2,1,0:T(8,128)S(1)}, f32[2,1024,256]{2,1,0:T(8,128)}, u32[]{:S(2)}) copy-start(f32[2,1024,256]{2,1,0:T(8,128)} %w_out.3) | copy-start | bytes 6291460
  95.2 19.7 %copy-start.3 = (f32[2,2560]{1,0:T(2,128)S(1)}, f32[2,2560]{1,0:T(2,128)}, u32[]{:S(2)}) copy-start(f32[2,2560]{1,0:T(2,128)} %biases.3) | copy-start | bytes 61444
  95.3 19.7 %copy-start.4 = (f32[2,2,256]{2,1,0:T(2,128)S(1)}, f32[2,2,256]{2,1,0:T(2,128)}, u32[]{:S(2)}) copy-start(f32[2,2,256]{2,1,0:T(2,128)} %gains.5) | copy-start | bytes 12292
  95.3 19.7 %copy-start.5 = (f32[2,2560]{1,0:T(2,128)S(1)}, f32[2,2560]{1,0:T(2,128)}, u32[]{:S(2)}) copy-start(f32[2,2560]{1,0:T(2,128)} %bias_mom.1) | copy-start | bytes 61444
  95.3 19.7 %copy-start.6 = (f32[2,2,256]{2,1,0:T(2,128)S(1)}, f32[2,2,256]{2,1,0:T(2,128)}, u32[]{:S(2)}) copy-start(f32[2,2,256]{2,1,0:T(2,128)} %gain_mom.1) | copy-start | bytes 12292
  97.4 1.5 %collective-permute-start.15 = (f32[8,2304]{1,0:T(8,128)S(1)}, f32[8,2304]{1,0:T(8,128)S(1)}, u32[]{:S(2)}, u32[]{:S(2)}) collective-permute-start(f32[8,2304]{1,0:T(8,128)S(1)} %get-tuple-element.103), channel_id=1, source_target_pairs={{0,4},{4,0},{8,12},{12,8},{16,20},{20,16},{24,28},{28,24},{1,5},{5... | collective-permute-start | bytes 221192 | tf_op jit(solution)/shard_map/ppermute | solution.py:834
  98.9 5.0 %collective-permute-start.18 = (bf16[8,2304]{1,0:T(8,128)(2,1)S(1)}, bf16[8,2304]{1,0:T(8,128)(2,1)S(1)}, u32[]{:S(2)}, u32[]{:S(2)}) collective-permute-start(bf16[8,2304]{1,0:T(8,128)(2,1)S(1)} %add_convert_fusion.3), channel_id=1, source_target_pairs={{0,24},{4,28},{8,16},{12,20},{16,8},{20,12},{24,0},{28,4},{1,25},{... | collective-permute-start | bytes 110600 | tf_op jit(solution)/shard_map/ppermute | solution.py:834
  100.4 4.0 %collective-permute-start.17 = (bf16[8,2304]{1,0:T(8,128)(2,1)S(1)}, bf16[8,2304]{1,0:T(8,128)(2,1)S(1)}, u32[]{:S(2)}, u32[]{:S(2)}) collective-permute-start(bf16[8,2304]{1,0:T(8,128)(2,1)S(1)} %add_convert_fusion.3), channel_id=1, source_target_pairs={{0,16},{4,20},{8,24},{12,28},{16,0},{20,4},{24,8},{28,12},{1,17},{... | collective-permute-start | bytes 110600 | tf_op jit(solution)/shard_map/ppermute | solution.py:834
  101.9 4.0 %collective-permute-start.16 = (bf16[8,2304]{1,0:T(8,128)(2,1)S(1)}, bf16[8,2304]{1,0:T(8,128)(2,1)S(1)}, u32[]{:S(2)}, u32[]{:S(2)}) collective-permute-start(bf16[8,2304]{1,0:T(8,128)(2,1)S(1)} %add_convert_fusion.3), channel_id=1, source_target_pairs={{0,8},{4,12},{8,0},{12,4},{16,24},{20,28},{24,16},{28,20},{1,9},{5... | collective-permute-start | bytes 110600 | tf_op jit(solution)/shard_map/ppermute | solution.py:834
  105.9 6.2 %collective-permute-start.21 = (bf16[8,2304]{1,0:T(8,128)(2,1)S(1)}, bf16[8,2304]{1,0:T(8,128)(2,1)S(1)}, u32[]{:S(2)}, u32[]{:S(2)}) collective-permute-start(bf16[8,2304]{1,0:T(8,128)(2,1)S(1)} %add_convert_fusion.2), channel_id=1, source_target_pairs={{0,3},{1,2},{2,1},{3,0},{4,7},{5,6},{6,5},{7,4},{8,11},{9,10},{10,... | collective-permute-start | bytes 110600 | tf_op jit(solution)/shard_map/ppermute | solution.py:834
  108.3 4.9 %collective-permute-start.20 = (bf16[8,2304]{1,0:T(8,128)(2,1)S(1)}, bf16[8,2304]{1,0:T(8,128)(2,1)S(1)}, u32[]{:S(2)}, u32[]{:S(2)}) collective-permute-start(bf16[8,2304]{1,0:T(8,128)(2,1)S(1)} %add_convert_fusion.2), channel_id=1, source_target_pairs={{0,2},{1,3},{2,0},{3,1},{4,6},{5,7},{6,4},{7,5},{8,10},{9,11},{10,... | collective-permute-start | bytes 110600 | tf_op jit(solution)/shard_map/ppermute | solution.py:834
  109.4 4.1 %collective-permute-start.19 = (bf16[8,2304]{1,0:T(8,128)(2,1)S(1)}, bf16[8,2304]{1,0:T(8,128)(2,1)S(1)}, u32[]{:S(2)}, u32[]{:S(2)}) collective-permute-start(bf16[8,2304]{1,0:T(8,128)(2,1)S(1)} %add_convert_fusion.2), channel_id=1, source_target_pairs={{0,1},{1,0},{2,3},{3,2},{4,5},{5,4},{6,7},{7,6},{8,9},{9,8},{10,11... | collective-permute-start | bytes 110600 | tf_op jit(solution)/shard_map/ppermute | solution.py:834
  113.6 1.3 %collective-permute-start.22 = (f32[8,2304]{1,0:T(8,128)S(1)}, f32[8,2304]{1,0:T(8,128)S(1)}, u32[]{:S(2)}, u32[]{:S(2)}) collective-permute-start(f32[8,2304]{1,0:T(8,128)S(1)} %convert_add_fusion.1.right_mine), channel_id=1, source_target_pairs={{0,4},{4,0},{8,12},{12,8},{16,20},{20,16},{24,28},{28,24},{1,5},{5... | collective-permute-start | bytes 221192 | tf_op jit(solution)/shard_map/ppermute | solution.py:834

commit v5 on v4

--- a/solution.py
+++ b/solution.py
@@ -76,15 +76,15 @@
 
 
 def gelu_and_slope(u):
-    phi = 0.5 + 0.5 * lax.erf(u * 0.5**0.5)
-    bell = jnp.exp(u * u * -0.5) * (0.5 / math.pi) ** 0.5
-    return u * phi, phi + u * bell
+    z = u * 0.5**0.5
+    phi = 0.5 + 0.5 * lax.erf(z)
+    return u * phi, phi + z * jnp.exp2(z * z * -math.log2(math.e)) * math.pi**-0.5
 
 
 def forward_kernel(
     nqs, qlen, plen, xq, xp, attn, w_in, w_out, gains, biases, lists, counts,
     x_out, qk_out, v_out, p_out, ctx_out, n1_out, first_out, slope_out, act_out, n2_out, inv1_out, inv2_out, live_out, wqkv_out, wo_out, win_out, wout_out, pooled_out, units_out,
-    wproj, wo_t, win_t, wout_t, bias_bc, gain_bc, qblk, xs, away, score_s, first_s, first_low_s, turn,
+    wproj, wo_t, win_t, wout_t, bias_bc, gain_bc, qblk, xs, away, score_s, first_s, first_low_s, turn, pooled_s, w_in_s, w_out_s, w_sems,
 ):
     i = pl.program_id(0)
     steps = pl.num_programs(0) - 1
@@ -104,8 +104,16 @@
     def spread(at, row):
         bias_bc[at : at + d, :] = jnp.broadcast_to(row, (128, d)).T
 
+    def feed_weights(tower_at):
+        return [
+            pltpu.make_async_copy(w_in.at[tower_at], w_in_s, w_sems.at[0]),
+            pltpu.make_async_copy(w_out.at[tower_at], w_out_s, w_sems.at[1]),
+        ]
+
     @pl.when(i == 0)
     def _():
+        for copy in feed_weights(0):
+            copy.start()
         qblk[...] = jnp.zeros_like(qblk)
 
     @pl.when((i == 0) | (i == nqs))
@@ -130,17 +138,24 @@
     def _():
         one = eye()
         t = tower(late)
+        for copy in feed_weights(t):
+            copy.wait()
         for c in range(ff // d):
             at = slice(c * d, (c + 1) * d)
-            low = w_in[0, :, at].astype(BF16)
+            low = w_in_s[:, at].astype(BF16)
             win_out[t, :, at] = low
             win_t[at, :] = mm_nt(one, low).astype(BF16)
-            low = w_out[0, at, :].astype(BF16)
+            low = w_out_s[at, :].astype(BF16)
             wout_out[t, at, :] = low
             wout_t[:, at] = mm_nt(one, low).astype(BF16)
         for c in range(4, bias_bc.shape[0] // d):
             spread(c * d, biases[pl.ds(t, 1), c * d : (c + 1) * d])
         gain_bc[d : 2 * d, :] = jnp.broadcast_to(gains[t, 1:2, :], (128, d)).T
+
+        @pl.when(i == 1)
+        def _():
+            for copy in feed_weights(1):
+                copy.start()
 
     @pl.when(i < nqs)
     def _():
@@ -157,25 +172,34 @@
             out = jnp.where(segment == s, qlen[base + s], out)
         return jnp.where(group < nqs, out, plen[jnp.clip(group - nqs, 0, steps - nqs - 1) * GROUP + u])
 
+    def dead_keys(u, place):
+        row = lax.broadcasted_iota(jnp.int32, (TOK, 1), 0)
+        return place(row) >= length_of(i, u, row // HEAD)
+
+    @pl.when(i < nqs)
+    def _():
+        key = lax.broadcasted_iota(jnp.int32, (TOK, TOK), 0)
+        ask = lax.broadcasted_iota(jnp.int32, (TOK, TOK), 1)
+        for u in range(GROUP):
+            dead = dead_keys(u, lambda row: row % HEAD) | ((key // HEAD) != (ask // HEAD))
+            away[u] = jnp.where(dead, MASKED_SCORE, 0.0)
+
+    @pl.when((i >= nqs) & (i < steps))
+    def _():
+        for u in range(GROUP):
+            away[u] = jnp.broadcast_to(jnp.where(dead_keys(u, lambda row: row), MASKED_SCORE, 0.0), (TOK, TOK))
+
     def bias(at, size):
         return wide(bias_bc[at : at + size, :])
 
     def attention_parts():
-        is_q = i < nqs
-        key = lax.broadcasted_iota(jnp.int32, (TOK, TOK), 0)
-        ask = lax.broadcasted_iota(jnp.int32, (TOK, TOK), 1)
-        key_col = lax.broadcasted_iota(jnp.int32, (TOK, 1), 0)
-        far = is_q & ((key // HEAD) != (ask // HEAD))
-        for u in range(GROUP):
-            dead = jnp.where(is_q, key_col % HEAD, key_col) >= length_of(i, u, key_col // HEAD)
-            away[u] = jnp.where(far | dead, MASKED_SCORE, 0.0)
         x = xs[...]
-        q_t = (mm_nt(wproj[0:d, :], x) + bias(0, d)).astype(BF16)
+        q_t = (mm_nt(wproj[0:d, :], x) + bias(0, d)).astype(BF16) * BF16(HEAD**-0.5)
         qk_out[i, 0:d, :] = q_t
         for u in range(GROUP):
             for h in range(heads):
                 piece = q_t[h * HEAD : (h + 1) * HEAD, u * TOK : (u + 1) * TOK]
-                qblk[u, h * HEAD : (h + 1) * HEAD, h * TOK : (h + 1) * TOK] = piece * BF16(HEAD**-0.5)
+                qblk[u, h * HEAD : (h + 1) * HEAD, h * TOK : (h + 1) * TOK] = piece
         k_row = mm(x, wproj[4 * d : 5 * d, :]).astype(BF16)
         yield
         v_t = (mm_nt(wproj[2 * d : 3 * d, :], x) + bias(d, d)).astype(BF16)
@@ -183,7 +207,7 @@
             for h in range(heads):
                 score_s[u, h] = mm(k_row[u * TOK : (u + 1) * TOK, :], qblk[u, :, h * TOK : (h + 1) * TOK])
             yield
-        qk_out[i, d : 2 * d, :] = mm_nt(wproj[d : 2 * d, :], x).astype(BF16)
+        qk_out[i, d : 2 * d, :] = mm_nt(wproj[d : 2 * d, :], x).astype(BF16) * BF16(HEAD**-0.5)
         v_out[i] = (mm(x, wproj[5 * d : 6 * d, :]) + biases[pl.ds(tower(i), 1), d : 2 * d]).astype(BF16)
         x_t = mm_nt(wproj[3 * d : 4 * d, :], x)
         x_out[i, 0:d, :] = x_t.astype(BF16)
@@ -226,7 +250,7 @@
                 slope_out[late, rows, :] = slope
                 act_out[late, rows, :] = active.astype(BF16)
                 yield
-            hidden = hidden + mm(wout_t[:, at], act_out[late, at, :])
+        hidden = hidden + mm(wout_t[...], act_out[late, 0:ff, :])
         second, n2, inv2 = norm_columns(hidden, wide(gain_bc[d : 2 * d, :]), bias(5 * d, d))
         n2_out[late] = n2
         inv2_out[late] = jnp.broadcast_to(inv2, (8, span))
@@ -242,16 +266,7 @@
             live = ((place < length_of(late, u, token // HEAD)) & (row == owner)).astype(F32).astype(BF16)
             live_out[late, :, over] = live
             pooled = mm_nt(live, second_high[:, over]) + mm_nt(live, second_low[:, over])
-            pooled = pooled / length_of(late, u, seg_row).astype(F32)
-
-            @pl.when(is_q)
-            def _(pooled=pooled, u=u):
-                for s in range(segs):
-                    pooled_out[pl.ds((late * GROUP + u) * segs + s, 1), :] = pooled[s : s + 1, :]
-
-            @pl.when(jnp.logical_not(is_q))
-            def _(pooled=pooled, u=u):
-                pooled_out[pl.ds(nqs * GROUP * segs + (late - nqs) * GROUP + u, 1), :] = pooled[0:1, :]
+            pooled_s[late * GROUP + u] = pooled / length_of(late, u, seg_row).astype(F32)
 
     def in_turn(*kinds):
         running = [kind() for kind in kinds]
@@ -264,11 +279,16 @@
 
     @pl.when((i > 0) & (i < steps))
     def _():
-        in_turn(feed_parts, attention_parts)
+        in_turn(attention_parts, feed_parts)
 
     @pl.when(i == steps)
     def _():
         in_turn(feed_parts)
+        for u in range(nqs * GROUP):
+            pooled_out[u * segs : (u + 1) * segs, :] = pooled_s[u, 0:segs, :]
+        for u in range(pooled_s.shape[0] - nqs * GROUP):
+            at = nqs * GROUP * segs + u
+            pooled_out[at : at + 1, :] = pooled_s[nqs * GROUP + u, 0:1, :]
         rows = pooled_out[...]
         unit = rows * lax.rsqrt(jnp.sum(rows * rows, axis=1, keepdims=True) + UNIT_EPSILON)
         slots, own = lists.shape
@@ -314,9 +334,6 @@
     rows = [((8, span), F32), ((8, span), F32), ((16, span), BF16)]
     outs = early + later + rows
 
-    def second_tower_spec(*shape):
-        return pl.BlockSpec((1,) + shape, lambda i, *_: (jnp.where(i - 1 < nqs, 0, 1),) + (0,) * len(shape))
-
     kept = [pltpu.VMEM((steps,) + shape, kind) for shape, kind in outs]
     kept += [pltpu.VMEM((2,) + shape, BF16) for shape in ((d, 3 * d), (d, d), (d, ff), (ff, d))]
     kept += [pltpu.VMEM((seqs, d), F32)]
@@ -330,8 +347,8 @@
                 pl.BlockSpec((GROUP, TOK, d), lambda i, *_: (jnp.minimum(i, nqs - 1), 0, 0)),
                 pl.BlockSpec((GROUP, TOK, d), lambda i, *_: (jnp.clip(i - nqs, 0, nps - 1), 0, 0)),
                 tower_spec(nqs, 4, d, d),
-                second_tower_spec(d, ff),
-                second_tower_spec(ff, d),
+                pl.BlockSpec(memory_space=pl.ANY),
+                pl.BlockSpec(memory_space=pl.ANY),
                 whole_spec(2, 2, d),
                 whole_spec(2, biases.shape[1]),
                 whole_spec(*positives.shape),
@@ -352,6 +369,10 @@
                 pltpu.VMEM((d, span), F32),
                 pltpu.VMEM((d, span), BF16),
                 pltpu.VMEM((128, 128), F32),
+                pltpu.VMEM((steps * GROUP, 16, d), F32),
+                pltpu.VMEM((d, ff), F32),
+                pltpu.VMEM((ff, d), F32),
+                pltpu.SemaphoreType.DMA((2,)),
             ],
         ),
         out_shape=kept + [jax.ShapeDtypeStruct((1, sent, 128), BF16)],
@@ -475,7 +496,7 @@
     nqs, gp, x_in, qk_in, v_in, p_in, ctx_in, n1_in, first_in, slope_in, act_in, n2_in, inv1_in, inv2_in, live_in,
     wqkv, wo, win, wout, gains, attn_err, in_err, out_err, attn_start, in_start, out_start,
     qgrad, pgrad, attn_m, in_m, out_m, left_mine, left_other,
-    left, gain_bc, gz, gp_s, graw_s, gqkv, acc_qkv, acc_o, acc_in, acc_out, acc_gain, err_sems,
+    left, gain_bc, gz, up_s, gp_s, graw_s, gqkv, acc_qkv, acc_o, acc_in, acc_out, acc_gain, err_sems,
 ):
     i = pl.program_id(0)
     last = pl.num_programs(0) - 1
@@ -526,10 +547,11 @@
     for c in range(ff // d):
         at = slice(c * d, (c + 1) * d)
         up_low = (mm(wout[t, at, :], down_low) * slope_in[i, at, :]).astype(BF16)
-        acc_in[:, at] += mm_nt(first_in[i], up_low)
-        grad_first = grad_first + mm(win[t, :, at], up_low)
+        up_s[at, :] = up_low
     add_gain(1, grad_second * n2)
     add_gain(3, grad_second)
+    acc_in[...] += mm_nt(first_in[i], up_s[...])
+    grad_first = grad_two + mm(win[t], up_s[...])
     n1 = n1_in[i]
     grad_one = norm_columns_back(grad_first, n1, inv1_in[i, 0:1, :], wide(gain_bc[0:d, :]))
     branch_low = grad_one.astype(BF16)
@@ -550,7 +572,7 @@
             probs = p_in[i, u, h].astype(F32)
             grad_probs = gp_s[u, h]
             inner = jnp.sum(grad_probs * probs, axis=0, keepdims=True)
-            graw_s[u, h] = (probs * (grad_probs - inner) * HEAD**-0.5).astype(BF16)
+            graw_s[u, h] = (probs * (grad_probs - inner)).astype(BF16)
     for u in range(GROUP):
         over = slice(u * TOK, (u + 1) * TOK)
         for h in range(heads):
@@ -652,6 +674,7 @@
             pltpu.VMEM((8, width), F32),
             pltpu.VMEM((2 * d, 128), F32),
             pltpu.VMEM((GROUP, d, heads * TOK), BF16),
+            pltpu.VMEM((ff, span), BF16),
             pltpu.VMEM((GROUP, heads, TOK, TOK), F32),
             pltpu.VMEM((GROUP, heads, TOK, TOK), BF16),
             pltpu.VMEM((3 * d, span), BF16),
@@ -667,7 +690,24 @@
     )(gp, *saved, *low_weights, gains, *errors, *starts)
 
 
-def right_kernel(left_mine, left_other, attn_m, in_m, out_m, _, basis, right_mine, right_other, vector, left, right):
+def gram(rows):
+    terms = split_three(rows)
+    high, middle, low = terms
+    left = jnp.concatenate([high, high, middle, high, middle, low], axis=1)
+    right = jnp.concatenate([high, middle, high, low, middle, high], axis=1)
+    return mm_nt(left, right)
+
+
+def right_kernel(
+    left_mine, left_other, attn_m, in_m, out_m, attn_mom, in_mom, out_mom,
+    basis, right_mine, right_other, vector, grams, attn_held, in_held, out_held, left, right, sems,
+):
+    moments = [
+        pltpu.make_async_copy(source, target, sems.at[k])
+        for k, (source, target) in enumerate(((attn_mom, attn_held), (in_mom, in_held), (out_mom, out_held)))
+    ]
+    for copy in moments:
+        copy.start()
     d, ff = in_m.shape[1:]
     core = own_core()
     join_halves(core, left, left_mine, left_other)
@@ -683,42 +723,45 @@
             unit = column * scale
             step = jnp.where(order > j, dots * scale, 0.0)
             blocks[b] = jnp.where(order == j, unit, block - step * unit)
-    for (at, size), block in zip(places, blocks):
+    for k, ((at, size), block) in enumerate(zip(places, blocks)):
         basis[:, at : at + size] = block
+        grams[k] = gram(block)
     for j in range(8):
         right[:, j * d : (j + 1) * d] = right_rows(blocks[j], attn_m[j // 4, j % 4])
     for t in range(2):
         right[:, 8 * d + t * ff : 8 * d + (t + 1) * ff] = right_rows(blocks[8 + t], in_m[t])
         right[:, 8 * d + 2 * ff + t * d : 8 * d + 2 * ff + (t + 1) * d] = right_rows(blocks[10 + t], out_m[t])
     part_halves(core, right, right_mine, right_other)
-
-
-def right_factors(left_mine, left_other, attn_m, in_m, out_m, earlier):
-    d, ff = in_m.shape[1:]
+    for copy in moments:
+        copy.wait()
+
+
+def right_factors(left_mine, left_other, merged, moments):
+    d, ff = merged[1].shape[1:]
     vmem = pl.BlockSpec(memory_space=pltpu.VMEM)
     width = 10 * d + 2 * ff
     rows = functools.partial(jax.ShapeDtypeStruct, dtype=F32)
     return pl.pallas_call(
         right_kernel,
-        in_specs=[vmem] * 6,
-        out_specs=[vmem] * 4,
-        out_shape=[rows((8, width)), rows((8, width // 2)), rows((8, width // 2)), rows((8, 3 * d))],
-        scratch_shapes=[pltpu.VMEM((8, width + 3 * d), F32), pltpu.VMEM((8, width), F32)],
+        in_specs=[vmem] * 5 + [pl.BlockSpec(memory_space=pl.ANY)] * 3,
+        out_specs=[vmem] * 8,
+        out_shape=[rows((8, width)), rows((8, width // 2)), rows((8, width // 2)), rows((8, 3 * d)), rows((12, 8, 8))]
+        + [pltpu.VMEM(a.shape, F32) for a in moments],
+        scratch_shapes=[pltpu.VMEM((8, width + 3 * d), F32), pltpu.VMEM((8, width), F32), pltpu.SemaphoreType.DMA((3,))],
         compiler_params=pltpu.CompilerParams(vmem_limit_bytes=12 << 20),
         name="right",
-    )(left_mine, left_other, attn_m, in_m, out_m, earlier)
+    )(left_mine, left_other, *merged, *(pltpu.with_memory_space_constraint(a, pltpu.HBM) for a in moments))
 
 
 def update_kernel(
-    replicas, basis, right_mine, right_other, vector, gains, biases, gain_mom, bias_mom,
+    replicas, basis, right_mine, right_other, vector, grams, gains, biases, gain_mom, bias_mom,
     attn_m, in_m, out_m, attn, w_in, w_out, attn_mom, in_mom, out_mom,
     attn_new, in_new, out_new, attn_mom_new, in_mom_new, out_mom_new, attn_err, in_err, out_err,
     gains_new, biases_new, gain_mom_new, bias_mom_new, attn_factor, in_factor, out_factor, norm_out,
     right, clip_s,
 ):
     i = pl.program_id(0)
-    d = attn.shape[2]
-    ff = (right.shape[1] - 10 * d) // 2
+    d, ff = w_in.shape[1:]
     t, c = i // 4, i % 4
 
     @pl.when(i == 0)
@@ -729,14 +772,11 @@
         for s in range(2):
             in_factor[s] = right[:, 8 * d + s * ff : 8 * d + (s + 1) * ff]
             out_factor[s] = right[:, 8 * d + 2 * ff + s * d : 8 * d + 2 * ff + (s + 1) * d]
-        places = [((j * d, d), (j * d, d)) for j in range(8)]
-        places += [((8 * d + s * d, d), (8 * d + s * ff, ff)) for s in range(2)]
-        places += [((10 * d + s * ff, ff), (8 * d + 2 * ff + s * d, d)) for s in range(2)]
+        places = [(j * d, d) for j in range(8)]
+        places += [(8 * d + s * ff, ff) for s in range(2)] + [(8 * d + 2 * ff + s * d, d) for s in range(2)]
         total = jnp.zeros((8, 8), F32)
-        for (b_at, b_size), (r_at, r_size) in places:
-            b = basis[:, b_at : b_at + b_size]
-            r = right[:, r_at : r_at + r_size]
-            total = total + mm_nt(b, b, HIGHEST) * mm_nt(r, r, HIGHEST)
+        for k, (at, size) in enumerate(places):
+            total = total + grams[k] * gram(right[:, at : at + size])
         sums = vector[...]
         square = jnp.sum(jnp.sum(total, axis=1, keepdims=True), axis=0, keepdims=True)
         square = square + jnp.sum(jnp.sum(sums * sums, axis=1, keepdims=True), axis=0, keepdims=True)
@@ -769,12 +809,13 @@
         weight_new[...] = (weight - LEARNING_RATE * moved).reshape(weight_new.shape)
         error[...] = (merged - approx * (1.0 / replicas)).reshape(error.shape)
 
-    step(i * d, i * d, attn_m[0, 0], attn[0, 0], attn_mom[0, 0], attn_new, attn_mom_new, attn_err)
-    step((8 + t) * d, 8 * d + t * ff + c * d, in_m[0], w_in[0], in_mom[0], in_new, in_mom_new, in_err)
-    step(10 * d + t * ff + c * d, 8 * d + 2 * ff + t * d, out_m[0], w_out[0], out_mom[0], out_new, out_mom_new, out_err)
-
-
-def update(replicas, basis, right_mine, right_other, vector, gains, biases, gain_mom, bias_mom, merged, weights, moments):
+    across = pl.ds(pl.multiple_of(c * d, 128), d)
+    step(i * d, i * d, attn_m[t, c], attn[t, c], attn_mom[t, c], attn_new, attn_mom_new, attn_err)
+    step((8 + t) * d, 8 * d + t * ff + c * d, in_m[t, :, across], w_in[t, :, across], in_mom[t, :, across], in_new, in_mom_new, in_err)
+    step(10 * d + t * ff + c * d, 8 * d + 2 * ff + t * d, out_m[t, across, :], w_out[t, across, :], out_mom[t, across, :], out_new, out_mom_new, out_err)
+
+
+def update(replicas, basis, right_mine, right_other, vector, grams, gains, biases, gain_mom, bias_mom, merged, weights, moments):
     d, ff = weights[1].shape[1:]
     a_spec = pl.BlockSpec((1, 1, d, d), lambda i: (i // 4, i % 4, 0, 0))
     i_spec = pl.BlockSpec((1, d, d), lambda i: (i // 4, 0, i % 4))
@@ -783,12 +824,13 @@
     ie_spec = pl.BlockSpec((1, 1, d, d), lambda i: (0, i // 4, 0, i % 4))
     oe_spec = pl.BlockSpec((1, 1, d, d), lambda i: (0, i // 4, i % 4, 0))
     rows = functools.partial(jax.ShapeDtypeStruct, dtype=F32)
-    small = (basis, right_mine, right_other, vector, gains, biases, gain_mom, bias_mom)
+    small = (basis, right_mine, right_other, vector, grams, gains, biases, gain_mom, bias_mom)
+    direct = pl.BlockSpec(memory_space=pltpu.VMEM)
     finals = [gains.shape, biases.shape] * 2 + [(2, 4, 8, d), (2, 8, ff), (2, 8, d)]
     return pl.pallas_call(
         functools.partial(update_kernel, replicas),
         grid=(8,),
-        in_specs=[whole_spec(*a.shape) for a in small] + [a_spec, i_spec, o_spec] * 3,
+        in_specs=[direct] * (len(small) + 9),
         out_specs=[a_spec, i_spec, o_spec] * 2
         + [ae_spec, ie_spec, oe_spec]
         + [whole_spec(*shape) for shape in finals]
@@ -807,29 +849,6 @@
     return tuple(pltpu.with_memory_space_constraint(a, pltpu.VMEM) for a in arrays)
 
 
-def hold_kernel(count, _, *refs):
-    sources, targets, sems = refs[:count], refs[count : 2 * count], refs[2 * count]
-    copies = [pltpu.make_async_copy(source, target, sems.at[k]) for k, (source, target) in enumerate(zip(sources, targets))]
-    for copy in copies:
-        copy.start()
-    for copy in copies:
-        copy.wait()
-
-
-def hold(after, arrays):
-    size = sum(4 * math.prod(a.shape) for a in arrays)
-    return pl.pallas_call(
-        functools.partial(hold_kernel, len(arrays)),
-        in_specs=[pl.BlockSpec(memory_space=pl.ANY)] * (1 + len(arrays)),
-        out_specs=[pl.BlockSpec(memory_space=pltpu.VMEM)] * len(arrays),
-        out_shape=[pltpu.VMEM(a.shape, a.dtype) for a in arrays],
-        scratch_shapes=[pltpu.SemaphoreType.DMA((len(arrays),))],
-        compiler_params=pltpu.CompilerParams(vmem_limit_bytes=1 << 20),
-        cost_estimate=pl.CostEstimate(flops=0, bytes_accessed=2 * size, transcendentals=0),
-        name="hold",
-    )(after, *(pltpu.with_memory_space_constraint(a, pltpu.HBM) for a in arrays))
-
-
 def swap_with(x, axis, mask):
     return lax.ppermute(x, axis, [(i, i ^ mask) for i in range(lax.axis_size(axis))])
 
@@ -851,17 +870,14 @@
     return x, swap_with(x, "dp", 1)
 
 
-def sum_halves(mine, other, beside=()):
-    held = []
+def sum_halves(mine, other):
     mine = mine + swap_with(other, "dp", 1)
     for axis, masks in chip_steps() + [outer_step()]:
         sent = mine.astype(SEND)
-        if beside and axis == "outer":
-            held = in_vmem(*hold(sent, beside))
         mine = sent.astype(F32)
         for got in [swap_with(sent, axis, mask) for mask in masks]:
             mine = mine + got.astype(F32)
-    return mine, swap_with(mine, "dp", 1), *held
+    return mine, swap_with(mine, "dp", 1)
 
 
 def per_device(
@@ -887,11 +903,10 @@
     weights = (attn, w_in, w_out)
     moments = (attn_mom, w_in_mom, w_out_mom)
     merged = in_vmem(attn_m, in_m, out_m)
-    *left, mom_a, mom_b, mom_c = sum_halves(*left, beside=moments)
-    basis, *right, vector = right_factors(*left, *merged, mom_a)
-    held = in_vmem(*weights) + (mom_a, mom_b, mom_c)
+    basis, *right, vector, grams, mom_a, mom_b, mom_c = right_factors(*sum_halves(*left), merged, moments)
+    held = in_vmem(*weights, mom_a, mom_b, mom_c)
     *new, attn_factor, in_factor, out_factor, norm = update(
-        devices, basis, *sum_halves(*right), vector, gains, biases, gain_mom, bias_mom,
+        devices, basis, *sum_halves(*right), vector, grams, gains, biases, gain_mom, bias_mom,
         merged, held[:3], held[3:],
     )
     weights_new, moments_new, errors_new, vectors_new = new[:3], new[3:6], new[6:9], new[9:]

time: 124 us -> 116 us (0.935)
  Pallas kernels: 69.5 us -> 60.4 us
  waiting for transfers between devices: 25.4 us -> 26.8 us
    pallas_call x1, Pallas kernels: 26.4 us -> 21.7 us  [forward(): pl.pallas_call(functools.partial(forward_kernel, nqs), grid_spec=pltpu.Pr...]
    pallas_call x1, Pallas kernels: 27.4 us -> 25.3 us  [backward(): pl.pallas_call(functools.partial(backward_kernel, nqs), grid=(steps,), in...]
    pallas_call x2 -> x1, Pallas kernels: 4.97 us -> 3.04 us  [right_factors(): pl.pallas_call(right_kernel, in_specs=[vmem] * 5 + [pl.BlockSpec(memory_s...]
    ppermute x23, waiting for transfers between devices: 25.4 us -> 26.8 us  [swap_with(): lax.ppermute(x, axis, [(i, i ^ mask) for i in range(lax.axis_size(axis))])]
  transfers between devices with their start and end apart: 23 -> 23, of which waited for: 19 -> 20; matrix products, arithmetic and copies ran while one was open for 1% -> 1% of each run, Pallas kernels for 2% -> 0%
where the time goes in v5:
time: 116 us
  Pallas kernels  60.4 us (52%)
  waiting for transfers between devices  26.8 us (23%)
  starting transfers between devices  25.8 us (22%)
    ppermute x23, waiting for transfers between devices, swap_with(): lax.ppermute(x, axis, [(i, i ^ mask) for i in range(lax.axis_size(axis))])  26.8 us
    ppermute x23, starting transfers between devices, swap_with(): lax.ppermute(x, axis, [(i, i ^ mask) for i in range(lax.axis_size(axis))])  25.8 us
    pallas_call x1, Pallas kernels, backward(): pl.pallas_call(functools.partial(backward_kernel, nqs), grid=(steps,), in...  25.3 us
    pallas_call x1, Pallas kernels, forward(): pl.pallas_call(functools.partial(forward_kernel, nqs), grid_spec=pltpu.Pr...  21.7 us
    pallas_call x1, Pallas kernels, update(): pl.pallas_call(functools.partial(update_kernel, replicas), grid=(8,), in_...  8.35 us
    pallas_call x1, Pallas kernels, right_factors(): pl.pallas_call(right_kernel, in_specs=[vmem] * 5 + [pl.BlockSpec(memory_s...  3.04 us
  transfers between devices with their start and end apart: 23, of which 20 were waited for; matrix products, arithmetic and copies ran while one was open for 1% of the time, Pallas kernels for 0%

profile of v5, /device:TPU:0, one launch (start us, length us, event | category | flops | bytes accessed | tf_op | source)
XLA Modules:
  0.0 115.9 jit_solution(6759617518288020316)
XLA Ops:
  0.7 21.7 %forward.1 = (bf16[5,272,512]{2,1,0:T(8,128)(2,1)S(1)}, bf16[5,512,512]{2,1,0:T(8,128)(2,1)S(1)}, bf16[5,512,256]{2,1,0:T(8,128)(2,1)S(1)}, bf16[5,2,4,256,256]{...) custom-call(s32[8]{0:T(128)} %qlen.3, s32[8]{0:T(128)} %plen.3, ...), custom_call_target="tpu_custom_call" | custom-call | tf_op jit(solution)/shard_map/forward/pallas_call | solution.py:341
  22.4 3.1 %collective-permute-start = (bf16[1,40,128]{2,1,0:T(8,128)(2,1)}, bf16[1,40,128]{2,1,0:T(8,128)(2,1)S(1)}, u32[]{:S(2)}, u32[]{:S(2)}) collective-permute-start(bf16[1,40,128]{2,1,0:T(8,128)(2,1)} %get-tuple-element.73), channel_id=1, source_target_pairs={{0,1},{1,0},{2,3},{3,2},{4,5},{5,4},{6,7},{7,6},{8,9},{9,8},{10,11... | collective-permute-start | bytes 30728 | tf_op jit(solution)/shard_map/ppermute | solution.py:853
  25.5 2.6 %collective-permute-start.1 = (bf16[1,40,128]{2,1,0:T(8,128)(2,1)}, bf16[1,40,128]{2,1,0:T(8,128)(2,1)S(1)}, u32[]{:S(2)}, u32[]{:S(2)}) collective-permute-start(bf16[1,40,128]{2,1,0:T(8,128)(2,1)} %get-tuple-element.73), channel_id=1, source_target_pairs={{0,2},{1,3},{2,0},{3,1},{4,6},{5,7},{6,4},{7,5},{8,10},{9,11},{10,... | collective-permute-start | bytes 30728 | tf_op jit(solution)/shard_map/ppermute | solution.py:853
  28.1 0.8 constant_dynamic-update-slice_fusion.3
  28.9 1.4 %collective-permute-done.1 = bf16[1,40,128]{2,1,0:T(8,128)(2,1)S(1)} collective-permute-done((bf16[1,40,128]{2,1,0:T(8,128)(2,1)}, bf16[1,40,128]{2,1,0:T(8,128)(2,1)S(1)}, u32[]{:S(2)}, u32[]{:S(2)}) %collective-permute-start.1) | collective-permute-done | bytes 10272 | tf_op jit(solution)/shard_map/ppermute | solution.py:853
  30.3 3.5 %collective-permute-done.2 = bf16[1,40,128]{2,1,0:T(8,128)(2,1)S(1)} collective-permute-done((bf16[1,40,128]{2,1,0:T(8,128)(2,1)}, bf16[1,40,128]{2,1,0:T(8,128)(2,1)S(1)}, u32[]{:S(2)}, u32[]{:S(2)}) %collective-permute-start.2) | collective-permute-done | bytes 10272 | tf_op jit(solution)/shard_map/ppermute | solution.py:853
  33.8 1.5 %collective-permute-start.3 = (bf16[4,40,128]{2,1,0:T(8,128)(2,1)S(1)}, bf16[4,40,128]{2,1,0:T(8,128)(2,1)S(1)}, u32[]{:S(2)}, u32[]{:S(2)}) collective-permute-start(bf16[4,40,128]{2,1,0:T(8,128)(2,1)S(1)} %get-tuple-element.126), channel_id=1, source_target_pairs={{0,8},{4,12},{8,0},{12,4},{16,24},{20,28},{24,16},{28,20},{1,9},{5... | collective-permute-start | bytes 122888 | tf_op jit(solution)/shard_map/ppermute | solution.py:853
  35.3 1.5 %collective-permute-start.4 = (bf16[4,40,128]{2,1,0:T(8,128)(2,1)S(1)}, bf16[4,40,128]{2,1,0:T(8,128)(2,1)S(1)}, u32[]{:S(2)}, u32[]{:S(2)}) collective-permute-start(bf16[4,40,128]{2,1,0:T(8,128)(2,1)S(1)} %get-tuple-element.126), channel_id=1, source_target_pairs={{0,16},{4,20},{8,24},{12,28},{16,0},{20,4},{24,8},{28,12},{1,17},{... | collective-permute-start | bytes 122888 | tf_op jit(solution)/shard_map/ppermute | solution.py:853
  36.8 0.5 collective-permute-start.5
  37.3 0.5 collective-permute-done.3
  37.8 1.5 %collective-permute-done.4 = bf16[4,40,128]{2,1,0:T(8,128)(2,1)S(1)} collective-permute-done((bf16[4,40,128]{2,1,0:T(8,128)(2,1)S(1)}, bf16[4,40,128]{2,1,0:T(8,128)(2,1)S(1)}, u32[]{:S(2)}, u32[]{:S(2)}) %collective-permute-start.4) | collective-permute-done | bytes 40992 | tf_op jit(solution)/shard_map/ppermute | solution.py:853
  39.3 2.4 %collective-permute-done.5 = bf16[4,40,128]{2,1,0:T(8,128)(2,1)S(1)} collective-permute-done((bf16[4,40,128]{2,1,0:T(8,128)(2,1)S(1)}, bf16[4,40,128]{2,1,0:T(8,128)(2,1)S(1)}, u32[]{:S(2)}, u32[]{:S(2)}) %collective-permute-start.5) | collective-permute-done | bytes 40992 | tf_op jit(solution)/shard_map/ppermute | solution.py:853
  41.7 0.1 collective-permute-start.6
  41.8 1.4 %collective-permute-done.6.far = bf16[16,40,128]{2,1,0:T(8,128)(2,1)S(1)} collective-permute-done((bf16[16,40,128]{2,1,0:T(8,128)(2,1)S(1)}, bf16[16,40,128]{2,1,0:T(8,128)(2,1)S(1)}, u32[]{:S(2)}, u32[]{:S(2)}) %collective-permute-start.6) | collective-permute-done | bytes 163872 | tf_op jit(solution)/shard_map/ppermute | solution.py:853
  43.2 2.0 %contrast.1 = (f32[1,8]{1,0:T(1,128)}, bf16[10,48,256]{2,1,0:T(8,128)(2,1)S(1)}) custom-call(s32[8]{0:T(128)S(1)} %copy-done.7, s32[8]{0:T(128)S(1)} %copy-done.8, bf16[16,40,128]{2,1,0:T(8,128)(2,1)S(1)} %constant_dynamic-update-slice_fusion.4.near, bf16[16,40,128]{2,1,0:T(8,128)(2,1)S(1)} %collective-permute-done.6.far, f32[16,256]{1,0:T(8,128)S(1)} %get-tuple-element.74.pooled), custom_call_target="tpu_custom_call" | custom-call | tf_op jit(solution)/shard_map/contrast/pallas_call | solution.py:441
  45.2 25.3 %backward.1 = (f32[2,256,256]{2,1,0:T(8,128)}, f32[8,256,256]{2,1,0:T(8,128)}, f32[2,4,256,256]{3,2,1,0:T(8,128)S(1)}, f32[2,256,1024]{2,1,0:T(8,128)S(1)}, f32[...) custom-call(bf16[10,48,256]{2,1,0:T(8,128)(2,1)S(1)} %get-tuple-element.76.gp, ...), custom_call_target="tpu_custom_call" | custom-call | tf_op jit(solution)/shard_map/backward/pallas_call | solution.py:655
  70.5 0.2 collective-permute-start.7
  70.7 1.3 %collective-permute-done.7 = f32[8,2688]{1,0:T(8,128)S(1)} collective-permute-done((f32[8,2688]{1,0:T(8,128)}, f32[8,2688]{1,0:T(8,128)S(1)}, u32[]{:S(2)}, u32[]{:S(2)}) %collective-permute-start.7) | collective-permute-done | bytes 86048 | tf_op jit(solution)/shard_map/ppermute | solution.py:853
  72.0 0.9 add_convert_fusion.1
  72.9 0.5 collective-permute-start.10
  73.5 1.5 %collective-permute-start.9 = (bf16[8,2688]{1,0:T(8,128)(2,1)S(1)}, bf16[8,2688]{1,0:T(8,128)(2,1)S(1)}, u32[]{:S(2)}, u32[]{:S(2)}) collective-permute-start(bf16[8,2688]{1,0:T(8,128)(2,1)S(1)} %add_convert_fusion.1), channel_id=1, source_target_pairs={{0,16},{4,20},{8,24},{12,28},{16,0},{20,4},{24,8},{28,12},{1,17},{... | collective-permute-start | bytes 129032 | tf_op jit(solution)/shard_map/ppermute | solution.py:853
  75.0 1.5 %collective-permute-start.8 = (bf16[8,2688]{1,0:T(8,128)(2,1)S(1)}, bf16[8,2688]{1,0:T(8,128)(2,1)S(1)}, u32[]{:S(2)}, u32[]{:S(2)}) collective-permute-start(bf16[8,2688]{1,0:T(8,128)(2,1)S(1)} %add_convert_fusion.1), channel_id=1, source_target_pairs={{0,8},{4,12},{8,0},{12,4},{16,24},{20,28},{24,16},{28,20},{1,9},{5... | collective-permute-start | bytes 129032 | tf_op jit(solution)/shard_map/ppermute | solution.py:853
  76.5 1.6 %collective-permute-done.10 = bf16[8,2688]{1,0:T(8,128)(2,1)S(1)} collective-permute-done((bf16[8,2688]{1,0:T(8,128)(2,1)S(1)}, bf16[8,2688]{1,0:T(8,128)(2,1)S(1)}, u32[]{:S(2)}, u32[]{:S(2)}) %collective-permute-start.10) | collective-permute-done | bytes 43040 | tf_op jit(solution)/shard_map/ppermute | solution.py:853
  78.0 1.0 collective-permute-done.8
  79.1 0.3 collective-permute-start.13
  79.3 4.2 %collective-permute-start.11 = (bf16[8,2688]{1,0:T(8,128)(2,1)S(1)}, bf16[8,2688]{1,0:T(8,128)(2,1)S(1)}, u32[]{:S(2)}, u32[]{:S(2)}) collective-permute-start(bf16[8,2688]{1,0:T(8,128)(2,1)S(1)} %add_convert_fusion), channel_id=1, source_target_pairs={{0,1},{1,0},{2,3},{3,2},{4,5},{5,4},{6,7},{7,6},{8,9},{9,8},{10,11... | collective-permute-start | bytes 129032 | tf_op jit(solution)/shard_map/ppermute | solution.py:853
  83.5 1.4 %collective-permute-done.13 = bf16[8,2688]{1,0:T(8,128)(2,1)S(1)} collective-permute-done((bf16[8,2688]{1,0:T(8,128)(2,1)S(1)}, bf16[8,2688]{1,0:T(8,128)(2,1)S(1)}, u32[]{:S(2)}, u32[]{:S(2)}) %collective-permute-start.13) | collective-permute-done | bytes 43040 | tf_op jit(solution)/shard_map/ppermute | solution.py:853
  84.9 0.6 collective-permute-done.11
  85.5 0.1 collective-permute-start.14
  85.6 1.3 %collective-permute-done.14.left_other = f32[8,2688]{1,0:T(8,128)S(1)} collective-permute-done((f32[8,2688]{1,0:T(8,128)S(1)}, f32[8,2688]{1,0:T(8,128)S(1)}, u32[]{:S(2)}, u32[]{:S(2)}) %collective-permute-start.14) | collective-permute-done | bytes 86048 | tf_op jit(solution)/shard_map/ppermute | solution.py:853
  86.9 3.0 %right.1 = (f32[8,4608]{1,0:T(8,128)S(1)}, f32[8,2304]{1,0:T(8,128)S(1)}, f32[8,2304]{1,0:T(8,128)S(1)}, f32[8,768]{1,0:T(8,128)S(1)}, f32[12,8,8]{2,1,0:T(8,128...) custom-call(f32[8,2688]{1,0:T(8,128)S(1)} %convert_add_fusion.left_mine, ...), custom_call_target="tpu_custom_call" | custom-call | tf_op jit(solution)/shard_map/right/pallas_call | solution.py:744
  90.0 0.2 collective-permute-start.15
  90.2 1.1 collective-permute-done.15
  91.3 1.5 %collective-permute-start.18 = (bf16[8,2304]{1,0:T(8,128)(2,1)S(1)}, bf16[8,2304]{1,0:T(8,128)(2,1)S(1)}, u32[]{:S(2)}, u32[]{:S(2)}) collective-permute-start(bf16[8,2304]{1,0:T(8,128)(2,1)S(1)} %add_convert_fusion.3), channel_id=1, source_target_pairs={{0,24},{4,28},{8,16},{12,20},{16,8},{20,12},{24,0},{28,4},{1,25},{... | collective-permute-start | bytes 110600 | tf_op jit(solution)/shard_map/ppermute | solution.py:853
  92.8 1.5 %collective-permute-start.17 = (bf16[8,2304]{1,0:T(8,128)(2,1)S(1)}, bf16[8,2304]{1,0:T(8,128)(2,1)S(1)}, u32[]{:S(2)}, u32[]{:S(2)}) collective-permute-start(bf16[8,2304]{1,0:T(8,128)(2,1)S(1)} %add_convert_fusion.3), channel_id=1, source_target_pairs={{0,16},{4,20},{8,24},{12,28},{16,0},{20,4},{24,8},{28,12},{1,17},{... | collective-permute-start | bytes 110600 | tf_op jit(solution)/shard_map/ppermute | solution.py:853
  94.3 0.5 collective-permute-start.16
  94.9 1.4 %collective-permute-done.18 = bf16[8,2304]{1,0:T(8,128)(2,1)S(1)} collective-permute-done((bf16[8,2304]{1,0:T(8,128)(2,1)S(1)}, bf16[8,2304]{1,0:T(8,128)(2,1)S(1)}, u32[]{:S(2)}, u32[]{:S(2)}) %collective-permute-start.18) | collective-permute-done | bytes 36896 | tf_op jit(solution)/shard_map/ppermute | solution.py:853
  96.2 0.5 collective-permute-done.17
  96.8 1.5 %collective-permute-done.16 = bf16[8,2304]{1,0:T(8,128)(2,1)S(1)} collective-permute-done((bf16[8,2304]{1,0:T(8,128)(2,1)S(1)}, bf16[8,2304]{1,0:T(8,128)(2,1)S(1)}, u32[]{:S(2)}, u32[]{:S(2)}) %collective-permute-start.16) | collective-permute-done | bytes 36896 | tf_op jit(solution)/shard_map/ppermute | solution.py:853
  98.3 2.4 %collective-permute-start.21 = (bf16[8,2304]{1,0:T(8,128)(2,1)S(1)}, bf16[8,2304]{1,0:T(8,128)(2,1)S(1)}, u32[]{:S(2)}, u32[]{:S(2)}) collective-permute-start(bf16[8,2304]{1,0:T(8,128)(2,1)S(1)} %add_convert_fusion.2), channel_id=1, source_target_pairs={{0,3},{1,2},{2,1},{3,0},{4,7},{5,6},{6,5},{7,4},{8,11},{9,10},{10,... | collective-permute-start | bytes 110600 | tf_op jit(solution)/shard_map/ppermute | solution.py:853
  100.8 1.1 collective-permute-start.20
  101.9 0.9 collective-permute-start.19
  102.8 1.8 %collective-permute-done.21 = bf16[8,2304]{1,0:T(8,128)(2,1)S(1)} collective-permute-done((bf16[8,2304]{1,0:T(8,128)(2,1)S(1)}, bf16[8,2304]{1,0:T(8,128)(2,1)S(1)}, u32[]{:S(2)}, u32[]{:S(2)}) %collective-permute-start.21) | collective-permute-done | bytes 36896 | tf_op jit(solution)/shard_map/ppermute | solution.py:853
  104.5 1.1 collective-permute-done.20
  105.6 0.4 collective-permute-done.19
  106.0 0.1 collective-permute-start.22
  106.1 1.3 %collective-permute-done.22.right_other = f32[8,2304]{1,0:T(8,128)S(1)} collective-permute-done((f32[8,2304]{1,0:T(8,128)S(1)}, f32[8,2304]{1,0:T(8,128)S(1)}, u32[]{:S(2)}, u32[]{:S(2)}) %collective-permute-start.22) | collective-permute-done | bytes 73760 | tf_op jit(solution)/shard_map/ppermute | solution.py:853
  107.4 8.3 %update.1 = (f32[2,4,256,256]{3,2,1,0:T(8,128)}, f32[2,256,1024]{2,1,0:T(8,128)}, f32[2,1024,256]{2,1,0:T(8,128)}, f32[2,4,256,256]{3,2,1,0:T(8,128)}, f32[2,256...) custom-call(f32[8,4608]{1,0:T(8,128)S(1)} %get-tuple-element.101.bas, ...), custom_call_target="tpu_custom_call" | custom-call | tf_op jit(solution)/shard_map/update/pallas_call | solution.py:830
  (34 shorter events, 0.2 us)
Async XLA Ops:
  0.7 42.5 %copy-start.7 = (s32[8]{0:T(128)S(1)}, s32[8]{0:T(128)}, u32[]{:S(2)}) copy-start(s32[8]{0:T(128)} %qlen.3) | copy-start | bytes 100
  0.7 42.5 %copy-start.8 = (s32[8]{0:T(128)S(1)}, s32[8]{0:T(128)}, u32[]{:S(2)}) copy-start(s32[8]{0:T(128)} %plen.3) | copy-start | bytes 100
  22.4 6.5 %collective-permute-start = (bf16[1,40,128]{2,1,0:T(8,128)(2,1)}, bf16[1,40,128]{2,1,0:T(8,128)(2,1)S(1)}, u32[]{:S(2)}, u32[]{:S(2)}) collective-permute-start(bf16[1,40,128]{2,1,0:T(8,128)(2,1)} %get-tuple-element.73), channel_id=1, source_target_pairs={{0,1},{1,0},{2,3},{3,2},{4,5},{5,4},{6,7},{7,6},{8,9},{9,8},{10,11... | collective-permute-start | bytes 30728 | tf_op jit(solution)/shard_map/ppermute | solution.py:853
  25.5 4.8 %collective-permute-start.1 = (bf16[1,40,128]{2,1,0:T(8,128)(2,1)}, bf16[1,40,128]{2,1,0:T(8,128)(2,1)S(1)}, u32[]{:S(2)}, u32[]{:S(2)}) collective-permute-start(bf16[1,40,128]{2,1,0:T(8,128)(2,1)} %get-tuple-element.73), channel_id=1, source_target_pairs={{0,2},{1,3},{2,0},{3,1},{4,6},{5,7},{6,4},{7,5},{8,10},{9,11},{10,... | collective-permute-start | bytes 30728 | tf_op jit(solution)/shard_map/ppermute | solution.py:853
  28.1 5.7 %collective-permute-start.2 = (bf16[1,40,128]{2,1,0:T(8,128)(2,1)}, bf16[1,40,128]{2,1,0:T(8,128)(2,1)S(1)}, u32[]{:S(2)}, u32[]{:S(2)}) collective-permute-start(bf16[1,40,128]{2,1,0:T(8,128)(2,1)} %get-tuple-element.73), channel_id=1, source_target_pairs={{0,3},{1,2},{2,1},{3,0},{4,7},{5,6},{6,5},{7,4},{8,11},{9,10},{10,... | collective-permute-start | bytes 30728 | tf_op jit(solution)/shard_map/ppermute | solution.py:853
  33.8 4.0 %collective-permute-start.3 = (bf16[4,40,128]{2,1,0:T(8,128)(2,1)S(1)}, bf16[4,40,128]{2,1,0:T(8,128)(2,1)S(1)}, u32[]{:S(2)}, u32[]{:S(2)}) collective-permute-start(bf16[4,40,128]{2,1,0:T(8,128)(2,1)S(1)} %get-tuple-element.126), channel_id=1, source_target_pairs={{0,8},{4,12},{8,0},{12,4},{16,24},{20,28},{24,16},{28,20},{1,9},{5... | collective-permute-start | bytes 122888 | tf_op jit(solution)/shard_map/ppermute | solution.py:853
  35.3 4.0 %collective-permute-start.4 = (bf16[4,40,128]{2,1,0:T(8,128)(2,1)S(1)}, bf16[4,40,128]{2,1,0:T(8,128)(2,1)S(1)}, u32[]{:S(2)}, u32[]{:S(2)}) collective-permute-start(bf16[4,40,128]{2,1,0:T(8,128)(2,1)S(1)} %get-tuple-element.126), channel_id=1, source_target_pairs={{0,16},{4,20},{8,24},{12,28},{16,0},{20,4},{24,8},{28,12},{1,17},{... | collective-permute-start | bytes 122888 | tf_op jit(solution)/shard_map/ppermute | solution.py:853
  36.8 4.9 %collective-permute-start.5 = (bf16[4,40,128]{2,1,0:T(8,128)(2,1)S(1)}, bf16[4,40,128]{2,1,0:T(8,128)(2,1)S(1)}, u32[]{:S(2)}, u32[]{:S(2)}) collective-permute-start(bf16[4,40,128]{2,1,0:T(8,128)(2,1)S(1)} %get-tuple-element.126), channel_id=1, source_target_pairs={{0,24},{4,28},{8,16},{12,20},{16,8},{20,12},{24,0},{28,4},{1,25},{... | collective-permute-start | bytes 122888 | tf_op jit(solution)/shard_map/ppermute | solution.py:853
  41.7 1.5 %collective-permute-start.6 = (bf16[16,40,128]{2,1,0:T(8,128)(2,1)S(1)}, bf16[16,40,128]{2,1,0:T(8,128)(2,1)S(1)}, u32[]{:S(2)}, u32[]{:S(2)}) collective-permute-start(bf16[16,40,128]{2,1,0:T(8,128)(2,1)S(1)} %constant_dynamic-update-slice_fusion.4.near), channel_id=1, source_target_pairs={{0,4},{4,0},{8,12},{12,8},{16,20},{20,16},{24,28},{28,24},{1,5},{5... | collective-permute-start | bytes 491528 | tf_op jit(solution)/shard_map/ppermute | solution.py:853
  70.5 1.6 %collective-permute-start.7 = (f32[8,2688]{1,0:T(8,128)}, f32[8,2688]{1,0:T(8,128)S(1)}, u32[]{:S(2)}, u32[]{:S(2)}) collective-permute-start(f32[8,2688]{1,0:T(8,128)} %get-tuple-element.97), channel_id=1, source_target_pairs={{0,4},{4,0},{8,12},{12,8},{16,20},{20,16},{24,28},{28,24},{1,5},{5... | collective-permute-start | bytes 258056 | tf_op jit(solution)/shard_map/ppermute | solution.py:853
  72.9 5.1 %collective-permute-start.10 = (bf16[8,2688]{1,0:T(8,128)(2,1)S(1)}, bf16[8,2688]{1,0:T(8,128)(2,1)S(1)}, u32[]{:S(2)}, u32[]{:S(2)}) collective-permute-start(bf16[8,2688]{1,0:T(8,128)(2,1)S(1)} %add_convert_fusion.1), channel_id=1, source_target_pairs={{0,24},{4,28},{8,16},{12,20},{16,8},{20,12},{24,0},{28,4},{1,25},{... | collective-permute-start | bytes 129032 | tf_op jit(solution)/shard_map/ppermute | solution.py:853
  73.5 4.6 %collective-permute-start.9 = (bf16[8,2688]{1,0:T(8,128)(2,1)S(1)}, bf16[8,2688]{1,0:T(8,128)(2,1)S(1)}, u32[]{:S(2)}, u32[]{:S(2)}) collective-permute-start(bf16[8,2688]{1,0:T(8,128)(2,1)S(1)} %add_convert_fusion.1), channel_id=1, source_target_pairs={{0,16},{4,20},{8,24},{12,28},{16,0},{20,4},{24,8},{28,12},{1,17},{... | collective-permute-start | bytes 129032 | tf_op jit(solution)/shard_map/ppermute | solution.py:853
  75.0 4.0 %collective-permute-start.8 = (bf16[8,2688]{1,0:T(8,128)(2,1)S(1)}, bf16[8,2688]{1,0:T(8,128)(2,1)S(1)}, u32[]{:S(2)}, u32[]{:S(2)}) collective-permute-start(bf16[8,2688]{1,0:T(8,128)(2,1)S(1)} %add_convert_fusion.1), channel_id=1, source_target_pairs={{0,8},{4,12},{8,0},{12,4},{16,24},{20,28},{24,16},{28,20},{1,9},{5... | collective-permute-start | bytes 129032 | tf_op jit(solution)/shard_map/ppermute | solution.py:853
  79.1 5.9 %collective-permute-start.13 = (bf16[8,2688]{1,0:T(8,128)(2,1)S(1)}, bf16[8,2688]{1,0:T(8,128)(2,1)S(1)}, u32[]{:S(2)}, u32[]{:S(2)}) collective-permute-start(bf16[8,2688]{1,0:T(8,128)(2,1)S(1)} %add_convert_fusion), channel_id=1, source_target_pairs={{0,3},{1,2},{2,1},{3,0},{4,7},{5,6},{6,5},{7,4},{8,11},{9,10},{10,... | collective-permute-start | bytes 129032 | tf_op jit(solution)/shard_map/ppermute | solution.py:853
  79.3 5.6 %collective-permute-start.12 = (bf16[8,2688]{1,0:T(8,128)(2,1)S(1)}, bf16[8,2688]{1,0:T(8,128)(2,1)S(1)}, u32[]{:S(2)}, u32[]{:S(2)}) collective-permute-start(bf16[8,2688]{1,0:T(8,128)(2,1)S(1)} %add_convert_fusion), channel_id=1, source_target_pairs={{0,2},{1,3},{2,0},{3,1},{4,6},{5,7},{6,4},{7,5},{8,10},{9,11},{10,... | collective-permute-start | bytes 129032 | tf_op jit(solution)/shard_map/ppermute | solution.py:853
  79.3 6.2 %collective-permute-start.11 = (bf16[8,2688]{1,0:T(8,128)(2,1)S(1)}, bf16[8,2688]{1,0:T(8,128)(2,1)S(1)}, u32[]{:S(2)}, u32[]{:S(2)}) collective-permute-start(bf16[8,2688]{1,0:T(8,128)(2,1)S(1)} %add_convert_fusion), channel_id=1, source_target_pairs={{0,1},{1,0},{2,3},{3,2},{4,5},{5,4},{6,7},{7,6},{8,9},{9,8},{10,11... | collective-permute-start | bytes 129032 | tf_op jit(solution)/shard_map/ppermute | solution.py:853
  85.5 1.3 %collective-permute-start.14 = (f32[8,2688]{1,0:T(8,128)S(1)}, f32[8,2688]{1,0:T(8,128)S(1)}, u32[]{:S(2)}, u32[]{:S(2)}) collective-permute-start(f32[8,2688]{1,0:T(8,128)S(1)} %convert_add_fusion.left_mine), channel_id=1, source_target_pairs={{0,4},{4,0},{8,12},{12,8},{16,20},{20,16},{24,28},{28,24},{1,5},{5... | collective-permute-start | bytes 258056 | tf_op jit(solution)/shard_map/ppermute | solution.py:853
  86.9 20.5 %copy-start = (f32[2,4,256,256]{3,2,1,0:T(8,128)S(1)}, f32[2,4,256,256]{3,2,1,0:T(8,128)}, u32[]{:S(2)}) copy-start(f32[2,4,256,256]{3,2,1,0:T(8,128)} %attn.3) | copy-start | bytes 6291460
  86.9 20.5 %copy-start.1 = (f32[2,256,1024]{2,1,0:T(8,128)S(1)}, f32[2,256,1024]{2,1,0:T(8,128)}, u32[]{:S(2)}) copy-start(f32[2,256,1024]{2,1,0:T(8,128)} %w_in.3) | copy-start | bytes 6291460
  86.9 20.5 %copy-start.2 = (f32[2,1024,256]{2,1,0:T(8,128)S(1)}, f32[2,1024,256]{2,1,0:T(8,128)}, u32[]{:S(2)}) copy-start(f32[2,1024,256]{2,1,0:T(8,128)} %w_out.3) | copy-start | bytes 6291460
  86.9 20.5 %copy-start.3 = (f32[2,2560]{1,0:T(2,128)S(1)}, f32[2,2560]{1,0:T(2,128)}, u32[]{:S(2)}) copy-start(f32[2,2560]{1,0:T(2,128)} %biases.3) | copy-start | bytes 61444
  86.9 20.5 %copy-start.4 = (f32[2,2,256]{2,1,0:T(2,128)S(1)}, f32[2,2,256]{2,1,0:T(2,128)}, u32[]{:S(2)}) copy-start(f32[2,2,256]{2,1,0:T(2,128)} %gains.5) | copy-start | bytes 12292
  86.9 20.5 %copy-start.5 = (f32[2,2560]{1,0:T(2,128)S(1)}, f32[2,2560]{1,0:T(2,128)}, u32[]{:S(2)}) copy-start(f32[2,2560]{1,0:T(2,128)} %bias_mom.1) | copy-start | bytes 61444
  86.9 20.5 %copy-start.6 = (f32[2,2,256]{2,1,0:T(2,128)S(1)}, f32[2,2,256]{2,1,0:T(2,128)}, u32[]{:S(2)}) copy-start(f32[2,2,256]{2,1,0:T(2,128)} %gain_mom.1) | copy-start | bytes 12292
  90.0 1.3 %collective-permute-start.15 = (f32[8,2304]{1,0:T(8,128)S(1)}, f32[8,2304]{1,0:T(8,128)S(1)}, u32[]{:S(2)}, u32[]{:S(2)}) collective-permute-start(f32[8,2304]{1,0:T(8,128)S(1)} %get-tuple-element.103), channel_id=1, source_target_pairs={{0,4},{4,0},{8,12},{12,8},{16,20},{20,16},{24,28},{28,24},{1,5},{5... | collective-permute-start | bytes 221192 | tf_op jit(solution)/shard_map/ppermute | solution.py:853
  91.3 4.9 %collective-permute-start.18 = (bf16[8,2304]{1,0:T(8,128)(2,1)S(1)}, bf16[8,2304]{1,0:T(8,128)(2,1)S(1)}, u32[]{:S(2)}, u32[]{:S(2)}) collective-permute-start(bf16[8,2304]{1,0:T(8,128)(2,1)S(1)} %add_convert_fusion.3), channel_id=1, source_target_pairs={{0,24},{4,28},{8,16},{12,20},{16,8},{20,12},{24,0},{28,4},{1,25},{... | collective-permute-start | bytes 110600 | tf_op jit(solution)/shard_map/ppermute | solution.py:853
  92.8 4.0 %collective-permute-start.17 = (bf16[8,2304]{1,0:T(8,128)(2,1)S(1)}, bf16[8,2304]{1,0:T(8,128)(2,1)S(1)}, u32[]{:S(2)}, u32[]{:S(2)}) collective-permute-start(bf16[8,2304]{1,0:T(8,128)(2,1)S(1)} %add_convert_fusion.3), channel_id=1, source_target_pairs={{0,16},{4,20},{8,24},{12,28},{16,0},{20,4},{24,8},{28,12},{1,17},{... | collective-permute-start | bytes 110600 | tf_op jit(solution)/shard_map/ppermute | solution.py:853
  94.3 4.0 %collective-permute-start.16 = (bf16[8,2304]{1,0:T(8,128)(2,1)S(1)}, bf16[8,2304]{1,0:T(8,128)(2,1)S(1)}, u32[]{:S(2)}, u32[]{:S(2)}) collective-permute-start(bf16[8,2304]{1,0:T(8,128)(2,1)S(1)} %add_convert_fusion.3), channel_id=1, source_target_pairs={{0,8},{4,12},{8,0},{12,4},{16,24},{20,28},{24,16},{28,20},{1,9},{5... | collective-permute-start | bytes 110600 | tf_op jit(solution)/shard_map/ppermute | solution.py:853
  98.3 6.2 %collective-permute-start.21 = (bf16[8,2304]{1,0:T(8,128)(2,1)S(1)}, bf16[8,2304]{1,0:T(8,128)(2,1)S(1)}, u32[]{:S(2)}, u32[]{:S(2)}) collective-permute-start(bf16[8,2304]{1,0:T(8,128)(2,1)S(1)} %add_convert_fusion.2), channel_id=1, source_target_pairs={{0,3},{1,2},{2,1},{3,0},{4,7},{5,6},{6,5},{7,4},{8,11},{9,10},{10,... | collective-permute-start | bytes 110600 | tf_op jit(solution)/shard_map/ppermute | solution.py:853
  100.8 4.9 %collective-permute-start.20 = (bf16[8,2304]{1,0:T(8,128)(2,1)S(1)}, bf16[8,2304]{1,0:T(8,128)(2,1)S(1)}, u32[]{:S(2)}, u32[]{:S(2)}) collective-permute-start(bf16[8,2304]{1,0:T(8,128)(2,1)S(1)} %add_convert_fusion.2), channel_id=1, source_target_pairs={{0,2},{1,3},{2,0},{3,1},{4,6},{5,7},{6,4},{7,5},{8,10},{9,11},{10,... | collective-permute-start | bytes 110600 | tf_op jit(solution)/shard_map/ppermute | solution.py:853
  101.9 4.1 %collective-permute-start.19 = (bf16[8,2304]{1,0:T(8,128)(2,1)S(1)}, bf16[8,2304]{1,0:T(8,128)(2,1)S(1)}, u32[]{:S(2)}, u32[]{:S(2)}) collective-permute-start(bf16[8,2304]{1,0:T(8,128)(2,1)S(1)} %add_convert_fusion.2), channel_id=1, source_target_pairs={{0,1},{1,0},{2,3},{3,2},{4,5},{5,4},{6,7},{7,6},{8,9},{9,8},{10,11... | collective-permute-start | bytes 110600 | tf_op jit(solution)/shard_map/ppermute | solution.py:853
  106.0 1.3 %collective-permute-start.22 = (f32[8,2304]{1,0:T(8,128)S(1)}, f32[8,2304]{1,0:T(8,128)S(1)}, u32[]{:S(2)}, u32[]{:S(2)}) collective-permute-start(f32[8,2304]{1,0:T(8,128)S(1)} %convert_add_fusion.1.right_mine), channel_id=1, source_target_pairs={{0,4},{4,0},{8,12},{12,8},{16,20},{20,16},{24,28},{28,24},{1,5},{5... | collective-permute-start | bytes 221192 | tf_op jit(solution)/shard_map/ppermute | solution.py:853

commit v6 on v5

--- a/solution.py
+++ b/solution.py
@@ -550,8 +550,9 @@
         up_s[at, :] = up_low
     add_gain(1, grad_second * n2)
     add_gain(3, grad_second)
+    grad_first = grad_two + mm(win[t], up_s[...])
     acc_in[...] += mm_nt(first_in[i], up_s[...])
-    grad_first = grad_two + mm(win[t], up_s[...])
+    acc_out[...] += mm_nt(act_in[i], down_low)
     n1 = n1_in[i]
     grad_one = norm_columns_back(grad_first, n1, inv1_in[i, 0:1, :], wide(gain_bc[0:d, :]))
     branch_low = grad_one.astype(BF16)
@@ -563,7 +564,6 @@
     for u in range(GROUP):
         for h in range(heads):
             gp_s[u, h] = mm(v_in[i, u * TOK : (u + 1) * TOK, :], gz[u, :, h * TOK : (h + 1) * TOK])
-    acc_out[...] += mm_nt(act_in[i], down_low)
     add_gain(0, grad_first * n1)
     add_gain(2, grad_first)
     acc_o[...] += mm_nt(ctx_in[i], branch_low)
@@ -582,8 +582,8 @@
             gqkv[last_at, over] = mm_nt(grad_context[at, over], p_in[i, u, h]).astype(BF16)
             gqkv[at, over] = mm(qk_in[i, later, over], graw_s[u, h]).astype(BF16)
             gqkv[later, over] = mm_nt(qk_in[i, at, over], graw_s[u, h]).astype(BF16)
+    result = (grad_one + mm(wqkv[t], gqkv[...])).T.reshape(GROUP, TOK, d)
     acc_qkv[...] += mm_nt(x_in[i], gqkv[...])
-    result = (grad_one + mm(wqkv[t], gqkv[...])).T.reshape(GROUP, TOK, d)
 
     @pl.when(is_q)
     def _():
@@ -762,7 +762,7 @@
 ):
     i = pl.program_id(0)
     d, ff = w_in.shape[1:]
-    t, c = i // 4, i % 4
+    t, c = i // 2, i % 2
 
     @pl.when(i == 0)
     def _():
@@ -800,36 +800,49 @@
 
     clip = clip_s[0:1, 0:1]
 
-    def step(b_at, r_at, merged, weight, moment, weight_new, moment_new, error):
-        b1, b2, b3 = split_three(basis[:, pl.ds(pl.multiple_of(b_at, 128), d)])
-        r1, r2, r3 = split_three(right[:, pl.ds(pl.multiple_of(r_at, 128), d)])
+    def step(b_at, b_size, r_at, r_size, merged, weight, moment, weight_new, moment_new, error):
+        b1, b2, b3 = split_three(basis[:, pl.ds(pl.multiple_of(b_at, 128), b_size)])
+        r1, r2, r3 = split_three(right[:, pl.ds(pl.multiple_of(r_at, 128), r_size)])
         approx = mm_tn(jnp.concatenate([b1, b1, b2, b1, b2, b3], axis=0), jnp.concatenate([r1, r2, r1, r3, r2, r1], axis=0))
         moved = MOMENTUM_DECAY * moment + clip * approx
         moment_new[...] = moved.reshape(moment_new.shape)
         weight_new[...] = (weight - LEARNING_RATE * moved).reshape(weight_new.shape)
         error[...] = (merged - approx * (1.0 / replicas)).reshape(error.shape)
 
-    across = pl.ds(pl.multiple_of(c * d, 128), d)
-    step(i * d, i * d, attn_m[t, c], attn[t, c], attn_mom[t, c], attn_new, attn_mom_new, attn_err)
-    step((8 + t) * d, 8 * d + t * ff + c * d, in_m[t, :, across], w_in[t, :, across], in_mom[t, :, across], in_new, in_mom_new, in_err)
-    step(10 * d + t * ff + c * d, 8 * d + 2 * ff + t * d, out_m[t, across, :], w_out[t, across, :], out_mom[t, across, :], out_new, out_mom_new, out_err)
+    wider = ff // 2
+    across = pl.ds(pl.multiple_of(c * wider, 128), wider)
+    for j in range(2):
+        k = c * 2 + j
+        step(
+            (t * 4 + k) * d, d, (t * 4 + k) * d, d, attn_m[t, k], attn[t, k], attn_mom[t, k],
+            attn_new.at[0, j], attn_mom_new.at[0, j], attn_err.at[0, 0, j],
+        )
+    step(
+        (8 + t) * d, d, 8 * d + t * ff + c * wider, wider,
+        in_m[t, :, across], w_in[t, :, across], in_mom[t, :, across], in_new, in_mom_new, in_err,
+    )
+    step(
+        10 * d + t * ff + c * wider, wider, 8 * d + 2 * ff + t * d, d,
+        out_m[t, across, :], w_out[t, across, :], out_mom[t, across, :], out_new, out_mom_new, out_err,
+    )
 
 
 def update(replicas, basis, right_mine, right_other, vector, grams, gains, biases, gain_mom, bias_mom, merged, weights, moments):
     d, ff = weights[1].shape[1:]
-    a_spec = pl.BlockSpec((1, 1, d, d), lambda i: (i // 4, i % 4, 0, 0))
-    i_spec = pl.BlockSpec((1, d, d), lambda i: (i // 4, 0, i % 4))
-    o_spec = pl.BlockSpec((1, d, d), lambda i: (i // 4, i % 4, 0))
-    ae_spec = pl.BlockSpec((1, 1, 1, d, d), lambda i: (0, i // 4, i % 4, 0, 0))
-    ie_spec = pl.BlockSpec((1, 1, d, d), lambda i: (0, i // 4, 0, i % 4))
-    oe_spec = pl.BlockSpec((1, 1, d, d), lambda i: (0, i // 4, i % 4, 0))
+    half = ff // 2
+    a_spec = pl.BlockSpec((1, 2, d, d), lambda i: (i // 2, i % 2, 0, 0))
+    i_spec = pl.BlockSpec((1, d, half), lambda i: (i // 2, 0, i % 2))
+    o_spec = pl.BlockSpec((1, half, d), lambda i: (i // 2, i % 2, 0))
+    ae_spec = pl.BlockSpec((1, 1, 2, d, d), lambda i: (0, i // 2, i % 2, 0, 0))
+    ie_spec = pl.BlockSpec((1, 1, d, half), lambda i: (0, i // 2, 0, i % 2))
+    oe_spec = pl.BlockSpec((1, 1, half, d), lambda i: (0, i // 2, i % 2, 0))
     rows = functools.partial(jax.ShapeDtypeStruct, dtype=F32)
     small = (basis, right_mine, right_other, vector, grams, gains, biases, gain_mom, bias_mom)
     direct = pl.BlockSpec(memory_space=pltpu.VMEM)
     finals = [gains.shape, biases.shape] * 2 + [(2, 4, 8, d), (2, 8, ff), (2, 8, d)]
     return pl.pallas_call(
         functools.partial(update_kernel, replicas),
-        grid=(8,),
+        grid=(4,),
         in_specs=[direct] * (len(small) + 9),
         out_specs=[a_spec, i_spec, o_spec] * 2
         + [ae_spec, ie_spec, oe_spec]
@@ -840,7 +853,7 @@
         + [rows(shape) for shape in finals]
         + [rows((1,))],
         scratch_shapes=[pltpu.VMEM(basis.shape, F32), pltpu.VMEM((8, 128), F32)],
-        compiler_params=pltpu.CompilerParams(vmem_limit_bytes=14 << 20),
+        compiler_params=pltpu.CompilerParams(vmem_limit_bytes=22 << 20),
         name="update",
     )(*small, *merged, *weights, *moments)
 

time: 116 us -> 114 us (0.983)
  Pallas kernels: 60.4 us -> 58 us
    pallas_call x1, Pallas kernels: 25.3 us -> 23.3 us  [backward(): pl.pallas_call(functools.partial(backward_kernel, nqs), grid=(steps,), in...]
where the time goes in v6:
time: 114 us
  Pallas kernels  58 us (51%)
  waiting for transfers between devices  26.8 us (24%)
  starting transfers between devices  25.8 us (23%)
    ppermute x23, waiting for transfers between devices, swap_with(): lax.ppermute(x, axis, [(i, i ^ mask) for i in range(lax.axis_size(axis))])  26.8 us
    ppermute x23, starting transfers between devices, swap_with(): lax.ppermute(x, axis, [(i, i ^ mask) for i in range(lax.axis_size(axis))])  25.8 us
    pallas_call x1, Pallas kernels, backward(): pl.pallas_call(functools.partial(backward_kernel, nqs), grid=(steps,), in...  23.3 us
    pallas_call x1, Pallas kernels, forward(): pl.pallas_call(functools.partial(forward_kernel, nqs), grid_spec=pltpu.Pr...  21.7 us
    pallas_call x1, Pallas kernels, update(): pl.pallas_call(functools.partial(update_kernel, replicas), grid=(4,), in_...  7.94 us
    pallas_call x1, Pallas kernels, right_factors(): pl.pallas_call(right_kernel, in_specs=[vmem] * 5 + [pl.BlockSpec(memory_s...  3.04 us
  transfers between devices with their start and end apart: 23, of which 20 were waited for; matrix products, arithmetic and copies ran while one was open for 1% of the time, Pallas kernels for 0%

profile of v6, /device:TPU:0, one launch (start us, length us, event | category | flops | bytes accessed | tf_op | source)
XLA Modules:
  0.0 113.6 jit_solution(12198685264513796334)
XLA Ops:
  0.7 21.7 %forward.1 = (bf16[5,272,512]{2,1,0:T(8,128)(2,1)S(1)}, bf16[5,512,512]{2,1,0:T(8,128)(2,1)S(1)}, bf16[5,512,256]{2,1,0:T(8,128)(2,1)S(1)}, bf16[5,2,4,256,256]{...) custom-call(s32[8]{0:T(128)} %qlen.3, s32[8]{0:T(128)} %plen.3, ...), custom_call_target="tpu_custom_call" | custom-call | tf_op jit(solution)/shard_map/forward/pallas_call | solution.py:341
  22.4 3.1 %collective-permute-start = (bf16[1,40,128]{2,1,0:T(8,128)(2,1)}, bf16[1,40,128]{2,1,0:T(8,128)(2,1)S(1)}, u32[]{:S(2)}, u32[]{:S(2)}) collective-permute-start(bf16[1,40,128]{2,1,0:T(8,128)(2,1)} %get-tuple-element.73), channel_id=1, source_target_pairs={{0,1},{1,0},{2,3},{3,2},{4,5},{5,4},{6,7},{7,6},{8,9},{9,8},{10,11... | collective-permute-start | bytes 30728 | tf_op jit(solution)/shard_map/ppermute | solution.py:866
  25.5 2.6 %collective-permute-start.1 = (bf16[1,40,128]{2,1,0:T(8,128)(2,1)}, bf16[1,40,128]{2,1,0:T(8,128)(2,1)S(1)}, u32[]{:S(2)}, u32[]{:S(2)}) collective-permute-start(bf16[1,40,128]{2,1,0:T(8,128)(2,1)} %get-tuple-element.73), channel_id=1, source_target_pairs={{0,2},{1,3},{2,0},{3,1},{4,6},{5,7},{6,4},{7,5},{8,10},{9,11},{10,... | collective-permute-start | bytes 30728 | tf_op jit(solution)/shard_map/ppermute | solution.py:866
  28.1 0.8 constant_dynamic-update-slice_fusion.3
  28.9 1.4 %collective-permute-done.1 = bf16[1,40,128]{2,1,0:T(8,128)(2,1)S(1)} collective-permute-done((bf16[1,40,128]{2,1,0:T(8,128)(2,1)}, bf16[1,40,128]{2,1,0:T(8,128)(2,1)S(1)}, u32[]{:S(2)}, u32[]{:S(2)}) %collective-permute-start.1) | collective-permute-done | bytes 10272 | tf_op jit(solution)/shard_map/ppermute | solution.py:866
  30.3 3.5 %collective-permute-done.2 = bf16[1,40,128]{2,1,0:T(8,128)(2,1)S(1)} collective-permute-done((bf16[1,40,128]{2,1,0:T(8,128)(2,1)}, bf16[1,40,128]{2,1,0:T(8,128)(2,1)S(1)}, u32[]{:S(2)}, u32[]{:S(2)}) %collective-permute-start.2) | collective-permute-done | bytes 10272 | tf_op jit(solution)/shard_map/ppermute | solution.py:866
  33.8 1.5 %collective-permute-start.3 = (bf16[4,40,128]{2,1,0:T(8,128)(2,1)S(1)}, bf16[4,40,128]{2,1,0:T(8,128)(2,1)S(1)}, u32[]{:S(2)}, u32[]{:S(2)}) collective-permute-start(bf16[4,40,128]{2,1,0:T(8,128)(2,1)S(1)} %get-tuple-element.126), channel_id=1, source_target_pairs={{0,8},{4,12},{8,0},{12,4},{16,24},{20,28},{24,16},{28,20},{1,9},{5... | collective-permute-start | bytes 122888 | tf_op jit(solution)/shard_map/ppermute | solution.py:866
  35.3 1.5 %collective-permute-start.4 = (bf16[4,40,128]{2,1,0:T(8,128)(2,1)S(1)}, bf16[4,40,128]{2,1,0:T(8,128)(2,1)S(1)}, u32[]{:S(2)}, u32[]{:S(2)}) collective-permute-start(bf16[4,40,128]{2,1,0:T(8,128)(2,1)S(1)} %get-tuple-element.126), channel_id=1, source_target_pairs={{0,16},{4,20},{8,24},{12,28},{16,0},{20,4},{24,8},{28,12},{1,17},{... | collective-permute-start | bytes 122888 | tf_op jit(solution)/shard_map/ppermute | solution.py:866
  36.8 0.5 collective-permute-start.5
  37.3 0.5 collective-permute-done.3
  37.8 1.5 %collective-permute-done.4 = bf16[4,40,128]{2,1,0:T(8,128)(2,1)S(1)} collective-permute-done((bf16[4,40,128]{2,1,0:T(8,128)(2,1)S(1)}, bf16[4,40,128]{2,1,0:T(8,128)(2,1)S(1)}, u32[]{:S(2)}, u32[]{:S(2)}) %collective-permute-start.4) | collective-permute-done | bytes 40992 | tf_op jit(solution)/shard_map/ppermute | solution.py:866
  39.3 2.4 %collective-permute-done.5 = bf16[4,40,128]{2,1,0:T(8,128)(2,1)S(1)} collective-permute-done((bf16[4,40,128]{2,1,0:T(8,128)(2,1)S(1)}, bf16[4,40,128]{2,1,0:T(8,128)(2,1)S(1)}, u32[]{:S(2)}, u32[]{:S(2)}) %collective-permute-start.5) | collective-permute-done | bytes 40992 | tf_op jit(solution)/shard_map/ppermute | solution.py:866
  41.7 0.1 collective-permute-start.6
  41.8 1.4 %collective-permute-done.6.far = bf16[16,40,128]{2,1,0:T(8,128)(2,1)S(1)} collective-permute-done((bf16[16,40,128]{2,1,0:T(8,128)(2,1)S(1)}, bf16[16,40,128]{2,1,0:T(8,128)(2,1)S(1)}, u32[]{:S(2)}, u32[]{:S(2)}) %collective-permute-start.6) | collective-permute-done | bytes 163872 | tf_op jit(solution)/shard_map/ppermute | solution.py:866
  43.2 2.0 %contrast.1 = (f32[1,8]{1,0:T(1,128)}, bf16[10,48,256]{2,1,0:T(8,128)(2,1)S(1)}) custom-call(s32[8]{0:T(128)S(1)} %copy-done.7, s32[8]{0:T(128)S(1)} %copy-done.8, bf16[16,40,128]{2,1,0:T(8,128)(2,1)S(1)} %constant_dynamic-update-slice_fusion.4.near, bf16[16,40,128]{2,1,0:T(8,128)(2,1)S(1)} %collective-permute-done.6.far, f32[16,256]{1,0:T(8,128)S(1)} %get-tuple-element.74.pooled), custom_call_target="tpu_custom_call" | custom-call | tf_op jit(solution)/shard_map/contrast/pallas_call | solution.py:441
  45.2 23.3 %backward.1 = (f32[2,256,256]{2,1,0:T(8,128)}, f32[8,256,256]{2,1,0:T(8,128)}, f32[2,4,256,256]{3,2,1,0:T(8,128)S(1)}, f32[2,256,1024]{2,1,0:T(8,128)S(1)}, f32[...) custom-call(bf16[10,48,256]{2,1,0:T(8,128)(2,1)S(1)} %get-tuple-element.76.gp, ...), custom_call_target="tpu_custom_call" | custom-call | tf_op jit(solution)/shard_map/backward/pallas_call | solution.py:655
  68.5 0.2 collective-permute-start.7
  68.7 1.4 %collective-permute-done.7 = f32[8,2688]{1,0:T(8,128)S(1)} collective-permute-done((f32[8,2688]{1,0:T(8,128)}, f32[8,2688]{1,0:T(8,128)S(1)}, u32[]{:S(2)}, u32[]{:S(2)}) %collective-permute-start.7) | collective-permute-done | bytes 86048 | tf_op jit(solution)/shard_map/ppermute | solution.py:866
  70.1 0.9 add_convert_fusion.1
  71.0 0.5 collective-permute-start.10
  71.5 1.5 %collective-permute-start.9 = (bf16[8,2688]{1,0:T(8,128)(2,1)S(1)}, bf16[8,2688]{1,0:T(8,128)(2,1)S(1)}, u32[]{:S(2)}, u32[]{:S(2)}) collective-permute-start(bf16[8,2688]{1,0:T(8,128)(2,1)S(1)} %add_convert_fusion.1), channel_id=1, source_target_pairs={{0,16},{4,20},{8,24},{12,28},{16,0},{20,4},{24,8},{28,12},{1,17},{... | collective-permute-start | bytes 129032 | tf_op jit(solution)/shard_map/ppermute | solution.py:866
  73.0 1.5 %collective-permute-start.8 = (bf16[8,2688]{1,0:T(8,128)(2,1)S(1)}, bf16[8,2688]{1,0:T(8,128)(2,1)S(1)}, u32[]{:S(2)}, u32[]{:S(2)}) collective-permute-start(bf16[8,2688]{1,0:T(8,128)(2,1)S(1)} %add_convert_fusion.1), channel_id=1, source_target_pairs={{0,8},{4,12},{8,0},{12,4},{16,24},{20,28},{24,16},{28,20},{1,9},{5... | collective-permute-start | bytes 129032 | tf_op jit(solution)/shard_map/ppermute | solution.py:866
  74.5 1.6 %collective-permute-done.10 = bf16[8,2688]{1,0:T(8,128)(2,1)S(1)} collective-permute-done((bf16[8,2688]{1,0:T(8,128)(2,1)S(1)}, bf16[8,2688]{1,0:T(8,128)(2,1)S(1)}, u32[]{:S(2)}, u32[]{:S(2)}) %collective-permute-start.10) | collective-permute-done | bytes 43040 | tf_op jit(solution)/shard_map/ppermute | solution.py:866
  76.1 1.0 collective-permute-done.8
  77.1 0.3 collective-permute-start.13
  77.4 4.2 %collective-permute-start.11 = (bf16[8,2688]{1,0:T(8,128)(2,1)S(1)}, bf16[8,2688]{1,0:T(8,128)(2,1)S(1)}, u32[]{:S(2)}, u32[]{:S(2)}) collective-permute-start(bf16[8,2688]{1,0:T(8,128)(2,1)S(1)} %add_convert_fusion), channel_id=1, source_target_pairs={{0,1},{1,0},{2,3},{3,2},{4,5},{5,4},{6,7},{7,6},{8,9},{9,8},{10,11... | collective-permute-start | bytes 129032 | tf_op jit(solution)/shard_map/ppermute | solution.py:866
  81.5 1.4 %collective-permute-done.13 = bf16[8,2688]{1,0:T(8,128)(2,1)S(1)} collective-permute-done((bf16[8,2688]{1,0:T(8,128)(2,1)S(1)}, bf16[8,2688]{1,0:T(8,128)(2,1)S(1)}, u32[]{:S(2)}, u32[]{:S(2)}) %collective-permute-start.13) | collective-permute-done | bytes 43040 | tf_op jit(solution)/shard_map/ppermute | solution.py:866
  83.0 0.6 collective-permute-done.11
  83.6 0.1 collective-permute-start.14
  83.7 1.3 %collective-permute-done.14.left_other = f32[8,2688]{1,0:T(8,128)S(1)} collective-permute-done((f32[8,2688]{1,0:T(8,128)S(1)}, f32[8,2688]{1,0:T(8,128)S(1)}, u32[]{:S(2)}, u32[]{:S(2)}) %collective-permute-start.14) | collective-permute-done | bytes 86048 | tf_op jit(solution)/shard_map/ppermute | solution.py:866
  85.0 3.0 %right.1 = (f32[8,4608]{1,0:T(8,128)S(1)}, f32[8,2304]{1,0:T(8,128)S(1)}, f32[8,2304]{1,0:T(8,128)S(1)}, f32[8,768]{1,0:T(8,128)S(1)}, f32[12,8,8]{2,1,0:T(8,128...) custom-call(f32[8,2688]{1,0:T(8,128)S(1)} %convert_add_fusion.left_mine, ...), custom_call_target="tpu_custom_call" | custom-call | tf_op jit(solution)/shard_map/right/pallas_call | solution.py:744
  88.0 0.2 collective-permute-start.15
  88.2 1.1 collective-permute-done.15
  89.4 1.5 %collective-permute-start.18 = (bf16[8,2304]{1,0:T(8,128)(2,1)S(1)}, bf16[8,2304]{1,0:T(8,128)(2,1)S(1)}, u32[]{:S(2)}, u32[]{:S(2)}) collective-permute-start(bf16[8,2304]{1,0:T(8,128)(2,1)S(1)} %add_convert_fusion.3), channel_id=1, source_target_pairs={{0,24},{4,28},{8,16},{12,20},{16,8},{20,12},{24,0},{28,4},{1,25},{... | collective-permute-start | bytes 110600 | tf_op jit(solution)/shard_map/ppermute | solution.py:866
  90.9 1.5 %collective-permute-start.17 = (bf16[8,2304]{1,0:T(8,128)(2,1)S(1)}, bf16[8,2304]{1,0:T(8,128)(2,1)S(1)}, u32[]{:S(2)}, u32[]{:S(2)}) collective-permute-start(bf16[8,2304]{1,0:T(8,128)(2,1)S(1)} %add_convert_fusion.3), channel_id=1, source_target_pairs={{0,16},{4,20},{8,24},{12,28},{16,0},{20,4},{24,8},{28,12},{1,17},{... | collective-permute-start | bytes 110600 | tf_op jit(solution)/shard_map/ppermute | solution.py:866
  92.4 0.5 collective-permute-start.16
  92.9 1.4 %collective-permute-done.18 = bf16[8,2304]{1,0:T(8,128)(2,1)S(1)} collective-permute-done((bf16[8,2304]{1,0:T(8,128)(2,1)S(1)}, bf16[8,2304]{1,0:T(8,128)(2,1)S(1)}, u32[]{:S(2)}, u32[]{:S(2)}) %collective-permute-start.18) | collective-permute-done | bytes 36896 | tf_op jit(solution)/shard_map/ppermute | solution.py:866
  94.3 0.5 collective-permute-done.17
  94.8 1.5 %collective-permute-done.16 = bf16[8,2304]{1,0:T(8,128)(2,1)S(1)} collective-permute-done((bf16[8,2304]{1,0:T(8,128)(2,1)S(1)}, bf16[8,2304]{1,0:T(8,128)(2,1)S(1)}, u32[]{:S(2)}, u32[]{:S(2)}) %collective-permute-start.16) | collective-permute-done | bytes 36896 | tf_op jit(solution)/shard_map/ppermute | solution.py:866
  96.4 2.4 %collective-permute-start.21 = (bf16[8,2304]{1,0:T(8,128)(2,1)S(1)}, bf16[8,2304]{1,0:T(8,128)(2,1)S(1)}, u32[]{:S(2)}, u32[]{:S(2)}) collective-permute-start(bf16[8,2304]{1,0:T(8,128)(2,1)S(1)} %add_convert_fusion.2), channel_id=1, source_target_pairs={{0,3},{1,2},{2,1},{3,0},{4,7},{5,6},{6,5},{7,4},{8,11},{9,10},{10,... | collective-permute-start | bytes 110600 | tf_op jit(solution)/shard_map/ppermute | solution.py:866
  98.8 1.1 collective-permute-start.20
  99.9 0.9 collective-permute-start.19
  100.8 1.8 %collective-permute-done.21 = bf16[8,2304]{1,0:T(8,128)(2,1)S(1)} collective-permute-done((bf16[8,2304]{1,0:T(8,128)(2,1)S(1)}, bf16[8,2304]{1,0:T(8,128)(2,1)S(1)}, u32[]{:S(2)}, u32[]{:S(2)}) %collective-permute-start.21) | collective-permute-done | bytes 36896 | tf_op jit(solution)/shard_map/ppermute | solution.py:866
  102.6 1.1 collective-permute-done.20
  103.7 0.4 collective-permute-done.19
  104.1 0.1 collective-permute-start.22
  104.1 1.3 %collective-permute-done.22.right_other = f32[8,2304]{1,0:T(8,128)S(1)} collective-permute-done((f32[8,2304]{1,0:T(8,128)S(1)}, f32[8,2304]{1,0:T(8,128)S(1)}, u32[]{:S(2)}, u32[]{:S(2)}) %collective-permute-start.22) | collective-permute-done | bytes 73760 | tf_op jit(solution)/shard_map/ppermute | solution.py:866
  105.5 7.9 %update.1 = (f32[2,4,256,256]{3,2,1,0:T(8,128)}, f32[2,256,1024]{2,1,0:T(8,128)}, f32[2,1024,256]{2,1,0:T(8,128)}, f32[2,4,256,256]{3,2,1,0:T(8,128)}, f32[2,256...) custom-call(f32[8,4608]{1,0:T(8,128)S(1)} %get-tuple-element.101.bas, ...), custom_call_target="tpu_custom_call" | custom-call | tf_op jit(solution)/shard_map/update/pallas_call | solution.py:843
  (34 shorter events, 0.2 us)
Async XLA Ops:
  0.7 42.5 %copy-start.7 = (s32[8]{0:T(128)S(1)}, s32[8]{0:T(128)}, u32[]{:S(2)}) copy-start(s32[8]{0:T(128)} %qlen.3) | copy-start | bytes 100
  0.7 42.5 %copy-start.8 = (s32[8]{0:T(128)S(1)}, s32[8]{0:T(128)}, u32[]{:S(2)}) copy-start(s32[8]{0:T(128)} %plen.3) | copy-start | bytes 100
  22.4 6.5 %collective-permute-start = (bf16[1,40,128]{2,1,0:T(8,128)(2,1)}, bf16[1,40,128]{2,1,0:T(8,128)(2,1)S(1)}, u32[]{:S(2)}, u32[]{:S(2)}) collective-permute-start(bf16[1,40,128]{2,1,0:T(8,128)(2,1)} %get-tuple-element.73), channel_id=1, source_target_pairs={{0,1},{1,0},{2,3},{3,2},{4,5},{5,4},{6,7},{7,6},{8,9},{9,8},{10,11... | collective-permute-start | bytes 30728 | tf_op jit(solution)/shard_map/ppermute | solution.py:866
  25.5 4.8 %collective-permute-start.1 = (bf16[1,40,128]{2,1,0:T(8,128)(2,1)}, bf16[1,40,128]{2,1,0:T(8,128)(2,1)S(1)}, u32[]{:S(2)}, u32[]{:S(2)}) collective-permute-start(bf16[1,40,128]{2,1,0:T(8,128)(2,1)} %get-tuple-element.73), channel_id=1, source_target_pairs={{0,2},{1,3},{2,0},{3,1},{4,6},{5,7},{6,4},{7,5},{8,10},{9,11},{10,... | collective-permute-start | bytes 30728 | tf_op jit(solution)/shard_map/ppermute | solution.py:866
  28.1 5.7 %collective-permute-start.2 = (bf16[1,40,128]{2,1,0:T(8,128)(2,1)}, bf16[1,40,128]{2,1,0:T(8,128)(2,1)S(1)}, u32[]{:S(2)}, u32[]{:S(2)}) collective-permute-start(bf16[1,40,128]{2,1,0:T(8,128)(2,1)} %get-tuple-element.73), channel_id=1, source_target_pairs={{0,3},{1,2},{2,1},{3,0},{4,7},{5,6},{6,5},{7,4},{8,11},{9,10},{10,... | collective-permute-start | bytes 30728 | tf_op jit(solution)/shard_map/ppermute | solution.py:866
  33.8 4.0 %collective-permute-start.3 = (bf16[4,40,128]{2,1,0:T(8,128)(2,1)S(1)}, bf16[4,40,128]{2,1,0:T(8,128)(2,1)S(1)}, u32[]{:S(2)}, u32[]{:S(2)}) collective-permute-start(bf16[4,40,128]{2,1,0:T(8,128)(2,1)S(1)} %get-tuple-element.126), channel_id=1, source_target_pairs={{0,8},{4,12},{8,0},{12,4},{16,24},{20,28},{24,16},{28,20},{1,9},{5... | collective-permute-start | bytes 122888 | tf_op jit(solution)/shard_map/ppermute | solution.py:866
  35.3 4.0 %collective-permute-start.4 = (bf16[4,40,128]{2,1,0:T(8,128)(2,1)S(1)}, bf16[4,40,128]{2,1,0:T(8,128)(2,1)S(1)}, u32[]{:S(2)}, u32[]{:S(2)}) collective-permute-start(bf16[4,40,128]{2,1,0:T(8,128)(2,1)S(1)} %get-tuple-element.126), channel_id=1, source_target_pairs={{0,16},{4,20},{8,24},{12,28},{16,0},{20,4},{24,8},{28,12},{1,17},{... | collective-permute-start | bytes 122888 | tf_op jit(solution)/shard_map/ppermute | solution.py:866
  36.8 4.9 %collective-permute-start.5 = (bf16[4,40,128]{2,1,0:T(8,128)(2,1)S(1)}, bf16[4,40,128]{2,1,0:T(8,128)(2,1)S(1)}, u32[]{:S(2)}, u32[]{:S(2)}) collective-permute-start(bf16[4,40,128]{2,1,0:T(8,128)(2,1)S(1)} %get-tuple-element.126), channel_id=1, source_target_pairs={{0,24},{4,28},{8,16},{12,20},{16,8},{20,12},{24,0},{28,4},{1,25},{... | collective-permute-start | bytes 122888 | tf_op jit(solution)/shard_map/ppermute | solution.py:866
  41.7 1.5 %collective-permute-start.6 = (bf16[16,40,128]{2,1,0:T(8,128)(2,1)S(1)}, bf16[16,40,128]{2,1,0:T(8,128)(2,1)S(1)}, u32[]{:S(2)}, u32[]{:S(2)}) collective-permute-start(bf16[16,40,128]{2,1,0:T(8,128)(2,1)S(1)} %constant_dynamic-update-slice_fusion.4.near), channel_id=1, source_target_pairs={{0,4},{4,0},{8,12},{12,8},{16,20},{20,16},{24,28},{28,24},{1,5},{5... | collective-permute-start | bytes 491528 | tf_op jit(solution)/shard_map/ppermute | solution.py:866
  68.5 1.6 %collective-permute-start.7 = (f32[8,2688]{1,0:T(8,128)}, f32[8,2688]{1,0:T(8,128)S(1)}, u32[]{:S(2)}, u32[]{:S(2)}) collective-permute-start(f32[8,2688]{1,0:T(8,128)} %get-tuple-element.97), channel_id=1, source_target_pairs={{0,4},{4,0},{8,12},{12,8},{16,20},{20,16},{24,28},{28,24},{1,5},{5... | collective-permute-start | bytes 258056 | tf_op jit(solution)/shard_map/ppermute | solution.py:866
  71.0 5.1 %collective-permute-start.10 = (bf16[8,2688]{1,0:T(8,128)(2,1)S(1)}, bf16[8,2688]{1,0:T(8,128)(2,1)S(1)}, u32[]{:S(2)}, u32[]{:S(2)}) collective-permute-start(bf16[8,2688]{1,0:T(8,128)(2,1)S(1)} %add_convert_fusion.1), channel_id=1, source_target_pairs={{0,24},{4,28},{8,16},{12,20},{16,8},{20,12},{24,0},{28,4},{1,25},{... | collective-permute-start | bytes 129032 | tf_op jit(solution)/shard_map/ppermute | solution.py:866
  71.5 4.6 %collective-permute-start.9 = (bf16[8,2688]{1,0:T(8,128)(2,1)S(1)}, bf16[8,2688]{1,0:T(8,128)(2,1)S(1)}, u32[]{:S(2)}, u32[]{:S(2)}) collective-permute-start(bf16[8,2688]{1,0:T(8,128)(2,1)S(1)} %add_convert_fusion.1), channel_id=1, source_target_pairs={{0,16},{4,20},{8,24},{12,28},{16,0},{20,4},{24,8},{28,12},{1,17},{... | collective-permute-start | bytes 129032 | tf_op jit(solution)/shard_map/ppermute | solution.py:866
  73.0 4.0 %collective-permute-start.8 = (bf16[8,2688]{1,0:T(8,128)(2,1)S(1)}, bf16[8,2688]{1,0:T(8,128)(2,1)S(1)}, u32[]{:S(2)}, u32[]{:S(2)}) collective-permute-start(bf16[8,2688]{1,0:T(8,128)(2,1)S(1)} %add_convert_fusion.1), channel_id=1, source_target_pairs={{0,8},{4,12},{8,0},{12,4},{16,24},{20,28},{24,16},{28,20},{1,9},{5... | collective-permute-start | bytes 129032 | tf_op jit(solution)/shard_map/ppermute | solution.py:866
  77.1 5.9 %collective-permute-start.13 = (bf16[8,2688]{1,0:T(8,128)(2,1)S(1)}, bf16[8,2688]{1,0:T(8,128)(2,1)S(1)}, u32[]{:S(2)}, u32[]{:S(2)}) collective-permute-start(bf16[8,2688]{1,0:T(8,128)(2,1)S(1)} %add_convert_fusion), channel_id=1, source_target_pairs={{0,3},{1,2},{2,1},{3,0},{4,7},{5,6},{6,5},{7,4},{8,11},{9,10},{10,... | collective-permute-start | bytes 129032 | tf_op jit(solution)/shard_map/ppermute | solution.py:866
  77.4 5.6 %collective-permute-start.12 = (bf16[8,2688]{1,0:T(8,128)(2,1)S(1)}, bf16[8,2688]{1,0:T(8,128)(2,1)S(1)}, u32[]{:S(2)}, u32[]{:S(2)}) collective-permute-start(bf16[8,2688]{1,0:T(8,128)(2,1)S(1)} %add_convert_fusion), channel_id=1, source_target_pairs={{0,2},{1,3},{2,0},{3,1},{4,6},{5,7},{6,4},{7,5},{8,10},{9,11},{10,... | collective-permute-start | bytes 129032 | tf_op jit(solution)/shard_map/ppermute | solution.py:866
  77.4 6.2 %collective-permute-start.11 = (bf16[8,2688]{1,0:T(8,128)(2,1)S(1)}, bf16[8,2688]{1,0:T(8,128)(2,1)S(1)}, u32[]{:S(2)}, u32[]{:S(2)}) collective-permute-start(bf16[8,2688]{1,0:T(8,128)(2,1)S(1)} %add_convert_fusion), channel_id=1, source_target_pairs={{0,1},{1,0},{2,3},{3,2},{4,5},{5,4},{6,7},{7,6},{8,9},{9,8},{10,11... | collective-permute-start | bytes 129032 | tf_op jit(solution)/shard_map/ppermute | solution.py:866
  83.6 1.3 %collective-permute-start.14 = (f32[8,2688]{1,0:T(8,128)S(1)}, f32[8,2688]{1,0:T(8,128)S(1)}, u32[]{:S(2)}, u32[]{:S(2)}) collective-permute-start(f32[8,2688]{1,0:T(8,128)S(1)} %convert_add_fusion.left_mine), channel_id=1, source_target_pairs={{0,4},{4,0},{8,12},{12,8},{16,20},{20,16},{24,28},{28,24},{1,5},{5... | collective-permute-start | bytes 258056 | tf_op jit(solution)/shard_map/ppermute | solution.py:866
  84.9 20.5 %copy-start = (f32[2,4,256,256]{3,2,1,0:T(8,128)S(1)}, f32[2,4,256,256]{3,2,1,0:T(8,128)}, u32[]{:S(2)}) copy-start(f32[2,4,256,256]{3,2,1,0:T(8,128)} %attn.3) | copy-start | bytes 6291460
  84.9 20.5 %copy-start.1 = (f32[2,256,1024]{2,1,0:T(8,128)S(1)}, f32[2,256,1024]{2,1,0:T(8,128)}, u32[]{:S(2)}) copy-start(f32[2,256,1024]{2,1,0:T(8,128)} %w_in.3) | copy-start | bytes 6291460
  84.9 20.5 %copy-start.2 = (f32[2,1024,256]{2,1,0:T(8,128)S(1)}, f32[2,1024,256]{2,1,0:T(8,128)}, u32[]{:S(2)}) copy-start(f32[2,1024,256]{2,1,0:T(8,128)} %w_out.3) | copy-start | bytes 6291460
  84.9 20.5 %copy-start.3 = (f32[2,2560]{1,0:T(2,128)S(1)}, f32[2,2560]{1,0:T(2,128)}, u32[]{:S(2)}) copy-start(f32[2,2560]{1,0:T(2,128)} %biases.3) | copy-start | bytes 61444
  84.9 20.5 %copy-start.4 = (f32[2,2,256]{2,1,0:T(2,128)S(1)}, f32[2,2,256]{2,1,0:T(2,128)}, u32[]{:S(2)}) copy-start(f32[2,2,256]{2,1,0:T(2,128)} %gains.5) | copy-start | bytes 12292
  84.9 20.5 %copy-start.5 = (f32[2,2560]{1,0:T(2,128)S(1)}, f32[2,2560]{1,0:T(2,128)}, u32[]{:S(2)}) copy-start(f32[2,2560]{1,0:T(2,128)} %bias_mom.1) | copy-start | bytes 61444
  85.0 20.5 %copy-start.6 = (f32[2,2,256]{2,1,0:T(2,128)S(1)}, f32[2,2,256]{2,1,0:T(2,128)}, u32[]{:S(2)}) copy-start(f32[2,2,256]{2,1,0:T(2,128)} %gain_mom.1) | copy-start | bytes 12292
  88.0 1.3 %collective-permute-start.15 = (f32[8,2304]{1,0:T(8,128)S(1)}, f32[8,2304]{1,0:T(8,128)S(1)}, u32[]{:S(2)}, u32[]{:S(2)}) collective-permute-start(f32[8,2304]{1,0:T(8,128)S(1)} %get-tuple-element.103), channel_id=1, source_target_pairs={{0,4},{4,0},{8,12},{12,8},{16,20},{20,16},{24,28},{28,24},{1,5},{5... | collective-permute-start | bytes 221192 | tf_op jit(solution)/shard_map/ppermute | solution.py:866
  89.4 4.9 %collective-permute-start.18 = (bf16[8,2304]{1,0:T(8,128)(2,1)S(1)}, bf16[8,2304]{1,0:T(8,128)(2,1)S(1)}, u32[]{:S(2)}, u32[]{:S(2)}) collective-permute-start(bf16[8,2304]{1,0:T(8,128)(2,1)S(1)} %add_convert_fusion.3), channel_id=1, source_target_pairs={{0,24},{4,28},{8,16},{12,20},{16,8},{20,12},{24,0},{28,4},{1,25},{... | collective-permute-start | bytes 110600 | tf_op jit(solution)/shard_map/ppermute | solution.py:866
  90.9 4.0 %collective-permute-start.17 = (bf16[8,2304]{1,0:T(8,128)(2,1)S(1)}, bf16[8,2304]{1,0:T(8,128)(2,1)S(1)}, u32[]{:S(2)}, u32[]{:S(2)}) collective-permute-start(bf16[8,2304]{1,0:T(8,128)(2,1)S(1)} %add_convert_fusion.3), channel_id=1, source_target_pairs={{0,16},{4,20},{8,24},{12,28},{16,0},{20,4},{24,8},{28,12},{1,17},{... | collective-permute-start | bytes 110600 | tf_op jit(solution)/shard_map/ppermute | solution.py:866
  92.4 4.0 %collective-permute-start.16 = (bf16[8,2304]{1,0:T(8,128)(2,1)S(1)}, bf16[8,2304]{1,0:T(8,128)(2,1)S(1)}, u32[]{:S(2)}, u32[]{:S(2)}) collective-permute-start(bf16[8,2304]{1,0:T(8,128)(2,1)S(1)} %add_convert_fusion.3), channel_id=1, source_target_pairs={{0,8},{4,12},{8,0},{12,4},{16,24},{20,28},{24,16},{28,20},{1,9},{5... | collective-permute-start | bytes 110600 | tf_op jit(solution)/shard_map/ppermute | solution.py:866
  96.4 6.2 %collective-permute-start.21 = (bf16[8,2304]{1,0:T(8,128)(2,1)S(1)}, bf16[8,2304]{1,0:T(8,128)(2,1)S(1)}, u32[]{:S(2)}, u32[]{:S(2)}) collective-permute-start(bf16[8,2304]{1,0:T(8,128)(2,1)S(1)} %add_convert_fusion.2), channel_id=1, source_target_pairs={{0,3},{1,2},{2,1},{3,0},{4,7},{5,6},{6,5},{7,4},{8,11},{9,10},{10,... | collective-permute-start | bytes 110600 | tf_op jit(solution)/shard_map/ppermute | solution.py:866
  98.8 4.9 %collective-permute-start.20 = (bf16[8,2304]{1,0:T(8,128)(2,1)S(1)}, bf16[8,2304]{1,0:T(8,128)(2,1)S(1)}, u32[]{:S(2)}, u32[]{:S(2)}) collective-permute-start(bf16[8,2304]{1,0:T(8,128)(2,1)S(1)} %add_convert_fusion.2), channel_id=1, source_target_pairs={{0,2},{1,3},{2,0},{3,1},{4,6},{5,7},{6,4},{7,5},{8,10},{9,11},{10,... | collective-permute-start | bytes 110600 | tf_op jit(solution)/shard_map/ppermute | solution.py:866
  99.9 4.1 %collective-permute-start.19 = (bf16[8,2304]{1,0:T(8,128)(2,1)S(1)}, bf16[8,2304]{1,0:T(8,128)(2,1)S(1)}, u32[]{:S(2)}, u32[]{:S(2)}) collective-permute-start(bf16[8,2304]{1,0:T(8,128)(2,1)S(1)} %add_convert_fusion.2), channel_id=1, source_target_pairs={{0,1},{1,0},{2,3},{3,2},{4,5},{5,4},{6,7},{7,6},{8,9},{9,8},{10,11... | collective-permute-start | bytes 110600 | tf_op jit(solution)/shard_map/ppermute | solution.py:866
  104.1 1.3 %collective-permute-start.22 = (f32[8,2304]{1,0:T(8,128)S(1)}, f32[8,2304]{1,0:T(8,128)S(1)}, u32[]{:S(2)}, u32[]{:S(2)}) collective-permute-start(f32[8,2304]{1,0:T(8,128)S(1)} %convert_add_fusion.1.right_mine), channel_id=1, source_target_pairs={{0,4},{4,0},{8,12},{12,8},{16,20},{20,16},{24,28},{28,24},{1,5},{5... | collective-permute-start | bytes 221192 | tf_op jit(solution)/shard_map/ppermute | solution.py:866
